TPU v7x, 128 devices: a whole 4x4x4 slice. The times are simulated.
128 devices in a mesh: row: 8 (over x, z_lo), col: 16 (over z_hi, y, core).
Axes of the slice: x: 4, y: 4, z: 4 (z_hi: 2, z_lo: 2; z = z_hi * 2 + z_lo), core: 2. Of those that a mesh axis runs over, the one named last changes fastest.
Arguments:
- student: bfloat16 [12288, 4096], P('col', 'row'), may hold values from -25 to 25
- teacher: bfloat16 [12288, 4096], P('col', 'row'), may hold values from -6 to 6
Outputs:
- gradient: float32 [12288, 4096], P('col', 'row')
- total_loss: float32 [], replicated
All inputs are finite; a program needn't handle non-finite values.
Results may differ from a plain program's by a relative error of at most 0.0025.
Values may be sent and summed in bfloat16 or wider, within the bound.
No kernel may reach another device: no remote copies, remote signals or barrier semaphores. Data moves between devices by JAX's collectives and lax.ppermute only.
A program may use at most 128 MiB of HBM per device.

v0:
```python
import jax
import jax.numpy as jnp
from jax import lax
from jax.sharding import PartitionSpec as P


def per_device(student, teacher):
    n_row = lax.axis_size("row")
    n_col = lax.axis_size("col")
    row_index = lax.axis_index("row")
    col_index = lax.axis_index("col")
    gathered = lax.all_gather(student, "col", axis=0, tiled=True)
    batch = gathered.shape[0]
    own_feats = gathered.shape[1]
    feats = own_feats * n_row
    narrow = own_feats // n_col
    floats = gathered.astype(jnp.float32)
    average = jnp.mean(floats, axis=0)
    centered_all = floats - average
    spread = jnp.sqrt(jnp.sum(centered_all * centered_all, axis=0) / (batch - 1) + 0.0001)
    centered_b = centered_all.astype(jnp.bfloat16)
    own_piece = lax.dynamic_slice_in_dim(centered_b, col_index * narrow, narrow, 1)
    columns = lax.all_gather(own_piece, "row", axis=1, tiled=True)
    covar = lax.dot_general(
        centered_b, columns, (((0,), (0,)), ((), ())), preferred_element_type=jnp.float32
    ) / (batch - 1)
    row_ids = row_index * own_feats + jnp.arange(own_feats, dtype=jnp.int32)[:, None]
    col_pos = jnp.arange(narrow * n_row, dtype=jnp.int32)[None, :]
    col_ids = col_pos // narrow * own_feats + col_index * narrow + col_pos % narrow
    masked = jnp.where(row_ids == col_ids, jnp.float32(0.0), covar)
    cov_part = jnp.sum(masked * masked)
    masked_b = masked.astype(jnp.bfloat16)
    spread_slice = lax.dynamic_slice_in_dim(spread, col_index * narrow, narrow, 0)
    var_part = jnp.sum(jnp.maximum(0.0, 1.0 - spread_slice))
    local_floats = student.astype(jnp.float32)
    diff = local_floats - teacher.astype(jnp.float32)
    inv_part = jnp.sum(diff * diff)
    cov_grad = lax.psum_scatter(
        lax.dot_general(
            columns, masked_b, (((1,), (1,)), ((), ())), preferred_element_type=jnp.float32
        ).astype(jnp.bfloat16),
        "col",
        scatter_dimension=0,
        tiled=True,
    ).astype(jnp.float32)
    cov_sum, var_sum, inv_sum = lax.psum((cov_part, var_part, inv_part), ("row", "col"))
    total_loss = 25.0 * inv_sum / (batch * feats) + 25.0 * var_sum / feats + cov_sum / feats
    local_centered = local_floats - average
    hinge = jnp.where(spread < 1.0, local_centered / (spread * (batch - 1)), jnp.float32(0.0))
    gradient = (
        25.0 * diff / 32.0 - 25.0 * batch / 64.0 * hinge + batch / (16.0 * (batch - 1)) * cov_grad
    )
    return (gradient, total_loss)


def solution(mesh):
    in_specs = (P("col", "row"), P("col", "row"))
    out_specs = (P("col", "row"), P())
    return jax.shard_map(
        per_device, mesh=mesh, in_specs=in_specs, out_specs=out_specs, check_vma=False
    )
```

profile of v0, /device:TPU:1, one launch (start us, length us, event | category | flops | bytes accessed | tf_op | source)
XLA Modules:
  0.0 469.5 jit_solution(16289441222221574008)
XLA Ops:
  7.2 0.0 all-gather.3.cloned.1.call-start
  7.2 2.3 copy.4
  9.5 0.0 all-gather.3.cloned.1.call-update
  9.5 0.0 all-gather.5.cloned.1.call-start
  9.6 95.3 %all-gather.3.cloned.1.call-done = bf16[12288,512]{0,1:T(8,128)(2,1)} async-done(((bf16[768,512]{0,1:T(8,128)(2,1)}), bf16[12288,512]{0,1:T(8,128)(2,1)}) %all-gather.3.cloned.1.call-update) | async-done | bytes 12582928 | tf_op jit(solution)/shard_map/all_gather | solution.py:12
  104.9 6.3 %convert_reduce_fusion = f32[512]{0:T(512)S(1)} fusion(bf16[12288,512]{0,1:T(8,128)(2,1)} %all-gather.3.cloned.1.call-done), kind=kLoop, calls=%fused_computation.1 | loop fusion | flops 12582400 | bytes 12584960 | tf_op jit(solution)/shard_map/reduce_sum | solution.py:18
  111.2 8.2 %fusion.2 = (f32[512]{0:T(512)S(1)}, bf16[12288,512]{0,1:T(8,128)(2,1)S(1)}) fusion(bf16[12288,512]{0,1:T(8,128)(2,1)} %all-gather.3.cloned.1.call-done, f32[512]{0:T(512)S(1)} %broadcast_multiply_fusion.1), kind=kLoop, calls=%fused_computation.4 | loop fusion | flops 31456768 | bytes 25169920 | tf_op jit(solution)/shard_map/reduce_sum | solution.py:20
  119.4 0.0 copy-start
  119.4 4.6 copy-done
  124.0 0.9 constant_dynamic-slice_fusion
  124.9 0.0 all-gather.5.cloned.1.call-update
  125.0 0.0 reduce-scatter.2.cloned.1.call-start
  125.0 126.4 %all-gather.5.cloned.1.call-done = bf16[12288,256]{0,1:T(8,128)(2,1)} async-done(((bf16[12288,32]{0,1:T(8,128)(2,1)}), bf16[12288,256]{0,1:T(8,128)(2,1)}) %all-gather.5.cloned.1.call-update) | async-done | bytes 6291472 | tf_op jit(solution)/shard_map/all_gather | solution.py:23
  251.4 0.0 copy-start.1
  251.4 10.6 %multiply_reduce_fusion.1 = (f32[]{:T(128)}, bf16[512,256]{1,0:T(8,128)(2,1)S(1)}) fusion(bf16[12288,512]{0,1:T(8,128)(2,1)} %copy-done, bf16[12288,256]{0,1:T(8,128)(2,1)} %all-gather.5.cloned.1.call-done, s32[256]{0:T(256)S(1)} %fusion.12, s32[512]{0:T(512)S(1)} %iota_add_fusion), kind=kOutput, calls=%fused_computation.16 | convolution fusion | flops 3222011904 | bytes 19139588 | tf_op jit(solution)/shard_map/dot_general | solution.py:24
  262.0 0.0 copy-done.1
  262.0 6.4 %convolution_convert_fusion = bf16[12288,512]{1,0:T(8,128)(2,1)} fusion(bf16[12288,256]{0,1:T(8,128)(2,1)S(1)} %copy-done.1, bf16[512,256]{1,0:T(8,128)(2,1)S(1)} %get-tuple-element.12), kind=kOutput, calls=%fused_computation.5 | convolution fusion | flops 3227516928 | bytes 19136512 | tf_op jit(solution)/shard_map/dot_general | solution.py:39
  268.4 0.0 reduce-scatter.2.cloned.1.call-update
  268.5 0.7 maximum_reduce_fusion
  269.2 122.5 %reduce-scatter.2.cloned.1.call-done = bf16[768,512]{1,0:T(8,128)(2,1)} async-done(((bf16[12288,512]{1,0:T(8,128)(2,1)}), bf16[768,512]{1,0:T(8,128)(2,1)}) %reduce-scatter.2.cloned.1.call-update) | async-done | bytes 786448 | tf_op jit(solution)/shard_map/reduce_scatter | solution.py:38
  391.7 0.0 copy-done.2
  391.7 0.0 copy-done.3
  391.7 3.7 multiply_reduce_fusion
  395.4 64.6 %all-reduce = (f32[]{:T(128)}, f32[]{:T(128)}, f32[]{:T(128)}) all-reduce(f32[]{:T(128)} %get-tuple-element.7, f32[]{:T(128)} %maximum_reduce_fusion, f32[]{:T(128)} %get-tuple-element.11), channel_id=1, replica_groups=mesh['row'=8,'col'=16] {'row','col'}, use_global_device_ids=true, to_apply=%region_4.5 | all-reduce | flops 3 | bytes 24 | tf_op jit(solution)/shard_map/psum | solution.py:46
  (7 shorter events, 0.0 us)
Async XLA Ops:
  7.2 97.7 %all-gather.3.cloned.1.call-start = ((), (), s32[]{:S(2)}) async-start(), calls=%async_computation.1 | async-start | bytes 13369344 | tf_op jit(solution)/shard_map/all_gather | solution.py:12
  9.5 241.9 %all-gather.5.cloned.1.call-start = ((), (), s32[]{:S(2)}) async-start(), calls=%async_computation.2 | async-start | bytes 7077888 | tf_op jit(solution)/shard_map/all_gather | solution.py:23
  119.4 4.6 copy-start
  125.0 266.7 %reduce-scatter.2.cloned.1.call-start = ((), (), s32[]{:S(2)}) async-start(), calls=%async_computation.3 | async-start | bytes 13369344 | tf_op jit(solution)/shard_map/reduce_scatter | solution.py:38
  251.4 10.6 %copy-start.1 = (bf16[12288,256]{0,1:T(8,128)(2,1)S(1)}, bf16[12288,256]{0,1:T(8,128)(2,1)}, u32[]{:S(2)}) copy-start(bf16[12288,256]{0,1:T(8,128)(2,1)} %all-gather.5.cloned.1.call-done) | copy-start | bytes 18874372
  268.4 123.3 %copy-start.2 = (bf16[768,512]{1,0:T(8,128)(2,1)S(1)}, bf16[768,512]{1,0:T(8,128)(2,1)}, u32[]{:S(2)}) copy-start(bf16[768,512]{1,0:T(8,128)(2,1)} %param.2) | copy-start | bytes 2359300
  268.4 123.3 %copy-start.3 = (bf16[768,512]{1,0:T(8,128)(2,1)S(1)}, bf16[768,512]{1,0:T(8,128)(2,1)}, u32[]{:S(2)}) copy-start(bf16[768,512]{1,0:T(8,128)(2,1)} %param.3) | copy-start | bytes 2359300
Sparse Core Ops, SparseCore 0:
  11.0 93.8 all-gather.2
  125.1 126.2 all-gather.4
  268.6 123.0 reduce-scatter.1
where the time goes:
time: 470 us
  waiting for transfers between devices  344 us (73%)
  blocking collectives  64.6 us (14%)
  other arithmetic  19 us (4%)
  matrix products  17 us (4%)
  between operations  16.8 us (4%)
  local copies, waits for them, and re-layouts  7.79 us (2%)
    all_gather x1, waiting for transfers between devices, per_device(): columns = lax.all_gather(own_piece, 'row', axis=1, tiled=True)  126 us
    reduce_scatter x1, waiting for transfers between devices, per_device(): lax.psum_scatter(lax.dot_general(columns, masked_b, (((1,), (1,)), ((), (...  122 us
    all_gather x1, waiting for transfers between devices, per_device(): gathered = lax.all_gather(student, 'col', axis=0, tiled=True)  95.3 us
    psum x1, blocking collectives, per_device(): lax.psum((cov_part, var_part, inv_part), ('row', 'col'))  64.6 us
    dot_general x1, matrix products, per_device(): lax.dot_general(centered_b, columns, (((0,), (0,)), ((), ())), preferred_...  10.6 us
  transfers between devices with their start and end apart: 3, of which 3 were waited for; matrix products, arithmetic and copies ran while one was open for 0% of the time, Pallas kernels for 0%

commit v1 on v0

v1 whole, which is shorter than its diff:
```python
import jax
import jax.numpy as jnp
from jax import lax
from jax.sharding import PartitionSpec as P

F32 = jnp.float32
BF16 = jnp.bfloat16

CORE_GROUPS = [[2 * chip + core for chip in range(8)] for core in range(2)]


def shift_row(block, dx, dz):
    pairs = [(2 * x + z, 2 * ((x + dx) % 4) + (z + dz) % 2) for x in range(4) for z in range(2)]
    return lax.ppermute(block, "row", pairs)


def swap_cores(block):
    return lax.ppermute(block, "col", [(i, i ^ 1) for i in range(16)])


def exchange_chips(pieces):
    return lax.all_to_all(pieces, "col", 0, 0, axis_index_groups=CORE_GROUPS)


def share(block, axes, count):
    return lax.all_to_all(jnp.broadcast_to(block[None], (count,) + block.shape), axes, 0, 0)


def per_device(student, teacher):
    images, feats = student.shape
    batch = images * 16
    half = feats // 2
    slab = feats // 8
    row_index = lax.axis_index("row")
    col_index = lax.axis_index("col")
    core = col_index % 2
    chip = col_index // 2

    own = jnp.concatenate([student, swap_cores(student)], axis=0)
    mine = lax.dynamic_slice_in_dim(own, core * half, half, 1)
    x_lo = shift_row(mine, 1, 0)
    x_hi = shift_row(mine, -1, 0)
    z_own = shift_row(mine, 0, 1)

    floats = student.astype(F32)
    sums = jnp.sum(floats, axis=0)
    dev = floats - sums / images
    squares = jnp.sum(dev * dev, axis=0)
    message = jnp.concatenate([sums.reshape(4, 128), squares.reshape(4, 128)], axis=0)
    stats = share(message, ("row", "col"), 128).reshape(8, 16, 2, feats)
    means = jnp.sum(stats[:, :, 0], axis=1) / batch
    offsets = stats[:, :, 0] / images - means[:, None]
    variances = jnp.sum(stats[:, :, 1] + images * (offsets * offsets), axis=1) / (batch - 1)
    spreads = jnp.sqrt(variances + 0.0001)
    var_sum = jnp.sum(jnp.maximum(0.0, 1.0 - spreads))
    average = lax.dynamic_index_in_dim(means, row_index, 0, keepdims=False)
    spread = lax.dynamic_index_in_dim(spreads, row_index, 0, keepdims=False)
    half_means = lax.dynamic_slice_in_dim(means, core * half, half, 1)

    def centered(block, mean):
        return (block.astype(F32) - mean).astype(BF16)

    def centered_from(block, dx, dz):
        source = (row_index // 2 + dx) % 4 * 2 + (row_index + dz) % 2
        return centered(block, lax.dynamic_index_in_dim(half_means, source, 0))

    rows = centered(own, average)

    x_far = jnp.concatenate(
        [shift_row(x_lo[:images], 1, 0), shift_row(x_hi[images:], -1, 0)], axis=0
    )
    z_lo = shift_row(z_own, 1, 0)
    z_hi = shift_row(z_own, -1, 0)
    z_far = shift_row(x_far, 0, 1)

    def covariance(columns, diagonal):
        part = lax.dot_general(
            rows, columns, (((0,), (0,)), ((), ())), preferred_element_type=F32
        ).astype(BF16)
        pieces = exchange_chips(part.reshape(8, slab, columns.shape[1]))
        covar = jnp.sum(pieces.astype(F32), axis=0) / (batch - 1)
        if diagonal:
            row_ids = chip * slab + jnp.arange(slab, dtype=jnp.int32)[:, None]
            col_ids = jnp.arange(columns.shape[1], dtype=jnp.int32)[None, :]
            on_diagonal = (col_ids < half) & (row_ids == col_ids + core * half)
            covar = jnp.where(on_diagonal, F32(0.0), covar)
        cov_part = jnp.sum(covar * covar)
        masked_b = covar.astype(BF16)
        full = exchange_chips(jnp.broadcast_to(masked_b[None], (8,) + masked_b.shape))
        return full.reshape(feats, columns.shape[1]), cov_part

    def grad_part(columns, masked_b):
        return lax.dot_general(
            columns, masked_b, (((1,), (1,)), ((), ())), preferred_element_type=F32
        )

    near = jnp.concatenate(
        [
            lax.dynamic_slice_in_dim(rows, core * half, half, 1),
            centered_from(x_lo, -1, 0),
            centered_from(x_hi, 1, 0),
            centered_from(z_own, 0, 1),
            centered_from(x_far, 2, 0),
        ],
        axis=1,
    )
    near_masked, near_part = covariance(near, True)
    far = jnp.concatenate(
        [centered_from(z_lo, -1, 1), centered_from(z_hi, 1, 1), centered_from(z_far, 2, 1)], axis=1
    )
    far_masked, far_part = covariance(far, False)
    grads = grad_part(near, near_masked) + grad_part(far, far_masked)
    cov_grad = grads[:images] + swap_cores(grads[images:].astype(BF16)).astype(F32)

    diff = floats - teacher.astype(F32)
    inv_part = jnp.sum(diff * diff)
    lanes = jnp.arange(128, dtype=jnp.int32)[None, :]
    parts = jnp.where(lanes == 0, near_part + far_part, jnp.where(lanes == 1, inv_part, F32(0.0)))
    totals = jnp.sum(share(parts, ("row", "col"), 128), axis=(0, 1))
    cov_sum, inv_sum = totals[0], totals[1]
    total_feats = 8 * feats
    total_loss = (
        25.0 * inv_sum / (batch * total_feats)
        + 25.0 * var_sum / total_feats
        + cov_sum / total_feats
    )
    hinge = jnp.where(spread < 1.0, (floats - average) / (spread * (batch - 1)), F32(0.0))
    gradient = (
        25.0 * diff / 32.0 - 25.0 * batch / 64.0 * hinge + batch / (16.0 * (batch - 1)) * cov_grad
    )
    return (gradient, total_loss)


def solution(mesh):
    in_specs = (P("col", "row"), P("col", "row"))
    out_specs = (P("col", "row"), P())
    return jax.shard_map(
        per_device, mesh=mesh, in_specs=in_specs, out_specs=out_specs, check_vma=False
    )
```

time: 470 us -> 183 us (0.39)
  waiting for transfers between devices: 344 us -> 82.9 us
  blocking collectives: 64.6 us -> 0 us
  starting transfers between devices: 0.12 us -> 51.5 us
  between operations: 16.8 us -> 5.32 us
    all_gather x2 -> x0, waiting for transfers between devices: 222 us -> none  [the longest x1 126 us: per_device(): columns = lax.all_gather(own_piece, 'row', axis=1, tiled=True)]
    reduce_scatter x1 -> x0, waiting for transfers between devices: 122 us -> none  [per_device(): lax.psum_scatter(lax.dot_general(columns, masked_b, (((1,), (1,)), ((), (...]
    psum x1 -> x0, blocking collectives: 64.6 us -> none  [per_device(): lax.psum((cov_part, var_part, inv_part), ('row', 'col'))]
    all_to_all x0 -> x6, waiting for transfers between devices: none -> 54.1 us  [the longest x4 31.7 us: exchange_chips(): return lax.all_to_all(pieces, 'col', 0, 0, axis_index_groups=CORE_GROUPS)]
    all_to_all x0 -> x6, starting transfers between devices: none -> 31 us  [the longest x2 16.5 us: share(): lax.all_to_all(jnp.broadcast_to(block[None], (count,) + block.shape), axe...]
    ppermute x0 -> x10, waiting for transfers between devices: none -> 28.8 us  [the longest x8 28.8 us: shift_row(): return lax.ppermute(block, 'row', pairs)]
    ppermute x0 -> x10, starting transfers between devices: none -> 20.5 us  [the longest x2 12 us: swap_cores(): return lax.ppermute(block, 'col', [(i, i ^ 1) for i in range(16)])]
    reduce_sum x3 -> x8, other arithmetic: 15.3 us -> 2.84 us  [the longest x2 1.51 us: covariance(): cov_part = jnp.sum(covar * covar)]
  transfers between devices with their start and end apart: 3 -> 16, of which waited for: 3 -> 9; matrix products, arithmetic and copies ran while one was open for 0% -> 14% of each run, Pallas kernels for 0% -> 0%
where the time goes in v1:
time: 183 us; the launch traced here: 182 us
  waiting for transfers between devices  82.9 us (45%)
  starting transfers between devices  51.5 us (28%)
  other arithmetic  17.1 us (9%)
  matrix products  15.9 us (9%)
  local copies, waits for them, and re-layouts  9.67 us (5%)
  between operations  5.32 us (3%)
    all_to_all x4, waiting for transfers between devices, exchange_chips(): return lax.all_to_all(pieces, 'col', 0, 0, axis_index_groups=CORE_GROUPS)  31.7 us
    ppermute x8, waiting for transfers between devices, shift_row(): return lax.ppermute(block, 'row', pairs)  28.8 us
    all_to_all x2, waiting for transfers between devices, share(): lax.all_to_all(jnp.broadcast_to(block[None], (count,) + block.shape), axe...  22.3 us
    all_to_all x2, starting transfers between devices, share(): lax.all_to_all(jnp.broadcast_to(block[None], (count,) + block.shape), axe...  16.5 us
    all_to_all x4, starting transfers between devices, exchange_chips(): return lax.all_to_all(pieces, 'col', 0, 0, axis_index_groups=CORE_GROUPS)  14.5 us
    ppermute x2, starting transfers between devices, swap_cores(): return lax.ppermute(block, 'col', [(i, i ^ 1) for i in range(16)])  12 us
    dot_general x2, matrix products, grad_part(): lax.dot_general(columns, masked_b, (((1,), (1,)), ((), ())), preferred_el...  10.1 us
    ppermute x8, starting transfers between devices, shift_row(): return lax.ppermute(block, 'row', pairs)  8.44 us
  transfers between devices with their start and end apart: 16, of which 9 were waited for; matrix products, arithmetic and copies ran while one was open for 14% of the time, Pallas kernels for 0%

profile of v1, /device:TPU:1, one launch (start us, length us, event | category | flops | bytes accessed | tf_op | source)
XLA Modules:
  0.0 182.4 jit_solution(17938088114738811915)
XLA Ops:
  0.6 2.5 %multiply_reduce_fusion = (f32[]{:T(128)}, f32[512]{0:T(512)S(1)}) fusion(bf16[768,512]{1,0:T(8,128)(2,1)} %param.3, bf16[768,512]{1,0:T(8,128)(2,1)} %param.2), kind=kLoop, calls=%fused_computation.19 | loop fusion | flops 2358783 | bytes 1574916 | tf_op jit(solution)/shard_map/reduce_sum | solution.py:116
  4.2 11.5 %all-to-all-start = ((f32[128,8,128]{2,1,0:T(8,128)}), f32[128,8,128]{2,1,0:T(8,128)S(1)}, u32[]{:S(2)}, u32[]{:S(2)}) async-start(f32[128,8,128]{2,1,0:T(8,128)} %broadcast_in_dim.30), calls=%async_computation | async-start | bytes 1048576 | tf_op jit(solution)/shard_map/all_to_all | solution.py:26
  16.9 12.6 %all-to-all-done = f32[128,8,128]{2,1,0:T(8,128)S(1)} async-done(((f32[128,8,128]{2,1,0:T(8,128)}), f32[128,8,128]{2,1,0:T(8,128)S(1)}, u32[]{:S(2)}, u32[]{:S(2)}) %all-to-all-start) | async-done | bytes 524320 | tf_op jit(solution)/shard_map/all_to_all | solution.py:26
  32.9 2.3 %collective-permute-start.2 = (bf16[1536,256]{1,0:T(8,128)(2,1)S(1)}, bf16[1536,256]{1,0:T(8,128)(2,1)S(1)}, u32[]{:S(2)}, u32[]{:S(2)}) collective-permute-start(bf16[1536,256]{1,0:T(8,128)(2,1)S(1)} %constant_dynamic-slice_fusion), channel_id=1, source_target_pairs={{0,96},{16,112},{32,0},{48,16},{64,32},{80,48},{96,64},{112,80},{1... | collective-permute-start | bytes 2359304 | tf_op jit(solution)/shard_map/ppermute | solution.py:14
  36.1 16.3 %collective-permute-done.1 = bf16[1536,256]{1,0:T(8,128)(2,1)S(1)} collective-permute-done((bf16[1536,256]{1,0:T(8,128)(2,1)S(1)}, bf16[1536,256]{1,0:T(8,128)(2,1)S(1)}, u32[]{:S(2)}, u32[]{:S(2)}) %collective-permute-start.1) | collective-permute-done | bytes 786464 | tf_op jit(solution)/shard_map/ppermute | solution.py:14
  52.6 2.7 %collective-permute-start.5 = (bf16[768,256]{1,0:T(8,128)(2,1)S(1)}, bf16[768,256]{1,0:T(8,128)(2,1)S(1)}, u32[]{:S(2)}, u32[]{:S(2)}) collective-permute-start(bf16[768,256]{1,0:T(8,128)(2,1)S(1)} %slice.37), channel_id=1, source_target_pairs={{0,96},{16,112},{32,0},{48,16},{64,32},{80,48},{96,64},{112,80},{1... | collective-permute-start | bytes 1179656 | tf_op jit(solution)/shard_map/ppermute | solution.py:14
  58.5 4.6 %collective-permute-done.4 = bf16[768,256]{1,0:T(8,128)(2,1)S(1)} collective-permute-done((bf16[768,256]{1,0:T(8,128)(2,1)S(1)}, bf16[768,256]{1,0:T(8,128)(2,1)S(1)}, u32[]{:S(2)}, u32[]{:S(2)}) %collective-permute-start.4) | collective-permute-done | bytes 393248 | tf_op jit(solution)/shard_map/ppermute | solution.py:14
  64.3 3.4 %convolution_convert_fusion = bf16[512,1280]{1,0:T(8,128)(2,1)} fusion(bf16[1536,512]{1,0:T(8,128)(2,1)S(1)} %subtract_convert_fusion, bf16[1536,1280]{1,0:T(8,128)(2,1)S(1)} %fusion.11), kind=kOutput, calls=%fused_computation.2 | convolution fusion | flops 2013921280 | bytes 6815744 | tf_op jit(solution)/shard_map/dot_general | solution.py:77
  67.7 3.6 %all-to-all-start.1 = ((bf16[8,64,1280]{2,1,0:T(8,128)(2,1)}), bf16[8,64,1280]{2,1,0:T(8,128)(2,1)S(1)}, u32[]{:S(2)}, u32[]{:S(2)}) async-start(bf16[8,64,1280]{2,1,0:T(8,128)(2,1)} %bitcast.38), calls=%async_computation.1 | async-start | bytes 2621440 | tf_op jit(solution)/shard_map/all_to_all | solution.py:22
  71.3 7.9 %collective-permute-done.7 = bf16[1536,256]{1,0:T(8,128)(2,1)} collective-permute-done((bf16[1536,256]{1,0:T(8,128)(2,1)}, bf16[1536,256]{1,0:T(8,128)(2,1)}, u32[]{:S(2)}, u32[]{:S(2)}) %collective-permute-start.7) | collective-permute-done | bytes 786464 | tf_op jit(solution)/shard_map/ppermute | solution.py:14
  84.6 2.3 %convolution_convert_fusion.1 = bf16[512,768]{1,0:T(8,128)(2,1)} fusion(bf16[1536,512]{1,0:T(8,128)(2,1)S(1)} %copy-done.2, bf16[1536,256]{1,0:T(8,128)(2,1)S(1)} %subtract_convert_fusion.1, bf16[1536,256]{1,0:T(8,128)(2,1)S(1)} %subtract_convert_fusion.2, bf16[1536,256]{1,0:T(8,128)(2,1)S(1)} %subtract_convert_fusion.3), kind=kOutput, calls=%fused_computation.28 | convolution fusion | flops 1215430656 | bytes 4718592 | tf_op jit(solution)/shard_map/dot_general | solution.py:77
  87.0 5.7 %all-to-all-done.1 = bf16[8,64,1280]{2,1,0:T(8,128)(2,1)S(1)} async-done(((bf16[8,64,1280]{2,1,0:T(8,128)(2,1)}), bf16[8,64,1280]{2,1,0:T(8,128)(2,1)S(1)}, u32[]{:S(2)}, u32[]{:S(2)}) %all-to-all-start.1) | async-done | bytes 1310752 | tf_op jit(solution)/shard_map/all_to_all | solution.py:22
  92.7 3.6 %all-to-all-start.3 = ((bf16[8,64,768]{2,1,0:T(8,128)(2,1)}), bf16[8,64,768]{2,1,0:T(8,128)(2,1)S(1)}, u32[]{:S(2)}, u32[]{:S(2)}) async-start(bf16[8,64,768]{2,1,0:T(8,128)(2,1)} %bitcast.40), calls=%async_computation.3 | async-start | bytes 1572864 | tf_op jit(solution)/shard_map/all_to_all | solution.py:22
  97.4 9.4 %all-to-all-done.3 = bf16[8,64,768]{2,1,0:T(8,128)(2,1)S(1)} async-done(((bf16[8,64,768]{2,1,0:T(8,128)(2,1)}), bf16[8,64,768]{2,1,0:T(8,128)(2,1)S(1)}, u32[]{:S(2)}, u32[]{:S(2)}) %all-to-all-start.3) | async-done | bytes 786464 | tf_op jit(solution)/shard_map/all_to_all | solution.py:22
  107.9 3.8 %all-to-all-start.2 = ((bf16[8,64,1280]{2,1,0:T(8,128)(2,1)}), bf16[8,64,1280]{2,1,0:T(8,128)(2,1)S(1)}, u32[]{:S(2)}, u32[]{:S(2)}) async-start(bf16[8,64,1280]{2,1,0:T(8,128)(2,1)} %broadcast_in_dim.60), calls=%async_computation.2 | async-start | bytes 2621440 | tf_op jit(solution)/shard_map/all_to_all | solution.py:22
  112.4 12.3 %all-to-all-done.2 = bf16[8,64,1280]{2,1,0:T(8,128)(2,1)S(1)} async-done(((bf16[8,64,1280]{2,1,0:T(8,128)(2,1)}), bf16[8,64,1280]{2,1,0:T(8,128)(2,1)S(1)}, u32[]{:S(2)}, u32[]{:S(2)}) %all-to-all-start.2) | async-done | bytes 1310752 | tf_op jit(solution)/shard_map/all_to_all | solution.py:22
  125.6 3.5 %all-to-all-start.4 = ((bf16[8,64,768]{2,1,0:T(8,128)(2,1)}), bf16[8,64,768]{2,1,0:T(8,128)(2,1)S(1)}, u32[]{:S(2)}, u32[]{:S(2)}) async-start(bf16[8,64,768]{2,1,0:T(8,128)(2,1)} %broadcast_in_dim.61), calls=%async_computation.4 | async-start | bytes 1572864 | tf_op jit(solution)/shard_map/all_to_all | solution.py:22
  129.2 6.0 %fusion.21 = f32[1536,512]{1,0:T(8,128)} fusion(bf16[1536,1280]{1,0:T(8,128)(2,1)} %copy-done.10, bf16[512,1280]{1,0:T(8,128)(2,1)S(1)} %bitcast.39), kind=kOutput, calls=%fused_computation.70 | convolution fusion | flops 2013265920 | bytes 8388608 | tf_op jit(solution)/shard_map/dot_general | solution.py:93
  135.2 4.4 %all-to-all-done.4 = bf16[8,64,768]{2,1,0:T(8,128)(2,1)S(1)} async-done(((bf16[8,64,768]{2,1,0:T(8,128)(2,1)}), bf16[8,64,768]{2,1,0:T(8,128)(2,1)S(1)}, u32[]{:S(2)}, u32[]{:S(2)}) %all-to-all-start.4) | async-done | bytes 786464 | tf_op jit(solution)/shard_map/all_to_all | solution.py:22
  139.6 4.1 %convolution_add_fusion = f32[1536,512]{1,0:T(8,128)S(1)} fusion(f32[1536,512]{1,0:T(8,128)} %fusion.21, bf16[512,768]{1,0:T(8,128)(2,1)S(1)} %bitcast.41, bf16[1536,256]{1,0:T(8,128)(2,1)} %copy-done.9, bf16[1536,256]{1,0:T(8,128)(2,1)} %copy-done.7, bf16[1536,256]{1,0:T(8,128)(2,1)} %copy-done.8), kind=kOutput, calls=%fused_computation | convolution fusion | flops 1215823872 | bytes 9437184 | tf_op jit(solution)/shard_map/dot_general | solution.py:93
  146.3 10.9 %collective-permute-start.9 = (bf16[768,512]{1,0:T(8,128)(2,1)}, bf16[768,512]{1,0:T(8,128)(2,1)S(1)}, u32[]{:S(2)}, u32[]{:S(2)}) collective-permute-start(bf16[768,512]{1,0:T(8,128)(2,1)} %slice.48), channel_id=1, source_target_pairs={{0,1},{1,0},{2,3},{3,2},{4,5},{5,4},{6,7},{7,6},{8,9},{9,8},{10,11... | collective-permute-start | bytes 2359304 | tf_op jit(solution)/shard_map/ppermute | solution.py:18
  161.2 5.0 %all-to-all-start.5 = ((f32[128,1,128]{2,1,0:T(1,128)}), f32[128,1,128]{2,1,0:T(1,128)S(1)}, u32[]{:S(2)}, u32[]{:S(2)}) async-start(f32[128,1,128]{2,1,0:T(1,128)} %broadcast_in_dim.65), calls=%async_computation.5 | async-start | bytes 131072 | tf_op jit(solution)/shard_map/all_to_all | solution.py:26
  166.2 9.8 %all-to-all-done.5 = f32[128,1,128]{2,1,0:T(1,128)S(1)} async-done(((f32[128,1,128]{2,1,0:T(1,128)}), f32[128,1,128]{2,1,0:T(1,128)S(1)}, u32[]{:S(2)}, u32[]{:S(2)}) %all-to-all-start.5) | async-done | bytes 65568 | tf_op jit(solution)/shard_map/all_to_all | solution.py:26
  178.0 3.2 %fusion.6 = f32[768,512]{1,0:T(8,128)} fusion(bf16[768,512]{1,0:T(8,128)(2,1)S(1)} %copy-done, f32[1536,512]{1,0:T(8,128)} %copy-done.4, bf16[768,512]{1,0:T(8,128)(2,1)S(1)} %collective-permute-done.9, bf16[768,512]{1,0:T(8,128)(2,1)S(1)} %copy-done.3, f32[512]{0:T(512)S(1)} %bitcast.46, f32[512]{0:T(512)S(1)} %bitcast.44, ...), kind=kLoop, calls=%fused_computation.15 | loop fusion | flops 5111808 | bytes 5509632 | tf_op jit(solution)/shard_map/add | solution.py:129
  (79 shorter events, 25.7 us)
Async XLA Ops:
  0.6 2.5 %copy-start = (bf16[768,512]{1,0:T(8,128)(2,1)S(1)}, bf16[768,512]{1,0:T(8,128)(2,1)}, u32[]{:S(2)}) copy-start(bf16[768,512]{1,0:T(8,128)(2,1)} %param.2) | copy-start | bytes 2359300
  4.2 25.3 %all-to-all-start = ((f32[128,8,128]{2,1,0:T(8,128)}), f32[128,8,128]{2,1,0:T(8,128)S(1)}, u32[]{:S(2)}, u32[]{:S(2)}) async-start(f32[128,8,128]{2,1,0:T(8,128)} %broadcast_in_dim.30), calls=%async_computation | async-start | bytes 1048576 | tf_op jit(solution)/shard_map/all_to_all | solution.py:26
  15.7 15.5 %collective-permute-start = (bf16[768,512]{1,0:T(8,128)(2,1)S(1)}, bf16[768,512]{1,0:T(8,128)(2,1)}, u32[]{:S(2)}, u32[]{:S(2)}) collective-permute-start(bf16[768,512]{1,0:T(8,128)(2,1)S(1)} %copy-done), channel_id=1, source_target_pairs={{0,1},{1,0},{2,3},{3,2},{4,5},{5,4},{6,7},{7,6},{8,9},{9,8},{10,11... | collective-permute-start | bytes 2359304 | tf_op jit(solution)/shard_map/ppermute | solution.py:18
  32.5 20.0 %collective-permute-start.1 = (bf16[1536,256]{1,0:T(8,128)(2,1)S(1)}, bf16[1536,256]{1,0:T(8,128)(2,1)S(1)}, u32[]{:S(2)}, u32[]{:S(2)}) collective-permute-start(bf16[1536,256]{1,0:T(8,128)(2,1)S(1)} %constant_dynamic-slice_fusion), channel_id=1, source_target_pairs={{0,32},{16,48},{32,64},{48,80},{64,96},{80,112},{96,0},{112,16},{1... | collective-permute-start | bytes 2359304 | tf_op jit(solution)/shard_map/ppermute | solution.py:14
  32.9 19.7 %collective-permute-start.2 = (bf16[1536,256]{1,0:T(8,128)(2,1)S(1)}, bf16[1536,256]{1,0:T(8,128)(2,1)S(1)}, u32[]{:S(2)}, u32[]{:S(2)}) collective-permute-start(bf16[1536,256]{1,0:T(8,128)(2,1)S(1)} %constant_dynamic-slice_fusion), channel_id=1, source_target_pairs={{0,96},{16,112},{32,0},{48,16},{64,32},{80,48},{96,64},{112,80},{1... | collective-permute-start | bytes 2359304 | tf_op jit(solution)/shard_map/ppermute | solution.py:14
  35.2 20.1 %collective-permute-start.3 = (bf16[1536,256]{1,0:T(8,128)(2,1)S(1)}, bf16[1536,256]{1,0:T(8,128)(2,1)}, u32[]{:S(2)}, u32[]{:S(2)}) collective-permute-start(bf16[1536,256]{1,0:T(8,128)(2,1)S(1)} %constant_dynamic-slice_fusion), channel_id=1, source_target_pairs={{0,16},{16,0},{32,48},{48,32},{64,80},{80,64},{96,112},{112,96},{1... | collective-permute-start | bytes 2359304 | tf_op jit(solution)/shard_map/ppermute | solution.py:14
  36.1 28.2 %copy-start.1 = (bf16[1536,512]{1,0:T(8,128)(2,1)}, bf16[1536,512]{1,0:T(8,128)(2,1)S(1)}, u32[]{:S(2)}) copy-start(bf16[1536,512]{1,0:T(8,128)(2,1)S(1)} %subtract_convert_fusion) | copy-start | bytes 4718596
  52.5 10.6 %collective-permute-start.4 = (bf16[768,256]{1,0:T(8,128)(2,1)S(1)}, bf16[768,256]{1,0:T(8,128)(2,1)S(1)}, u32[]{:S(2)}, u32[]{:S(2)}) collective-permute-start(bf16[768,256]{1,0:T(8,128)(2,1)S(1)} %slice.36), channel_id=1, source_target_pairs={{0,32},{16,48},{32,64},{48,80},{64,96},{80,112},{96,0},{112,16},{1... | collective-permute-start | bytes 1179656 | tf_op jit(solution)/shard_map/ppermute | solution.py:14
  52.6 10.5 %collective-permute-start.5 = (bf16[768,256]{1,0:T(8,128)(2,1)S(1)}, bf16[768,256]{1,0:T(8,128)(2,1)S(1)}, u32[]{:S(2)}, u32[]{:S(2)}) collective-permute-start(bf16[768,256]{1,0:T(8,128)(2,1)S(1)} %slice.37), channel_id=1, source_target_pairs={{0,96},{16,112},{32,0},{48,16},{64,32},{80,48},{96,64},{112,80},{1... | collective-permute-start | bytes 1179656 | tf_op jit(solution)/shard_map/ppermute | solution.py:14
  55.3 23.8 %collective-permute-start.7 = (bf16[1536,256]{1,0:T(8,128)(2,1)}, bf16[1536,256]{1,0:T(8,128)(2,1)}, u32[]{:S(2)}, u32[]{:S(2)}) collective-permute-start(bf16[1536,256]{1,0:T(8,128)(2,1)} %collective-permute-done.3), channel_id=1, source_target_pairs={{0,96},{16,112},{32,0},{48,16},{64,32},{80,48},{96,64},{112,80},{1... | collective-permute-start | bytes 2359304 | tf_op jit(solution)/shard_map/ppermute | solution.py:14
  55.4 25.0 %collective-permute-start.6 = (bf16[1536,256]{1,0:T(8,128)(2,1)}, bf16[1536,256]{1,0:T(8,128)(2,1)}, u32[]{:S(2)}, u32[]{:S(2)}) collective-permute-start(bf16[1536,256]{1,0:T(8,128)(2,1)} %collective-permute-done.3), channel_id=1, source_target_pairs={{0,32},{16,48},{32,64},{48,80},{64,96},{80,112},{96,0},{112,16},{1... | collective-permute-start | bytes 2359304 | tf_op jit(solution)/shard_map/ppermute | solution.py:14
  63.2 18.9 %collective-permute-start.8 = (bf16[1536,256]{1,0:T(8,128)(2,1)S(1)}, bf16[1536,256]{1,0:T(8,128)(2,1)}, u32[]{:S(2)}, u32[]{:S(2)}) collective-permute-start(bf16[1536,256]{1,0:T(8,128)(2,1)S(1)} %constant_dynamic-update-slice_fusion.2), channel_id=1, source_target_pairs={{0,16},{16,0},{32,48},{48,32},{64,80},{80,64},{96,112},{112,96},{1... | collective-permute-start | bytes 2359304 | tf_op jit(solution)/shard_map/ppermute | solution.py:14
  64.3 3.4 %copy-start.10 = (bf16[1536,1280]{1,0:T(8,128)(2,1)}, bf16[1536,1280]{1,0:T(8,128)(2,1)S(1)}, u32[]{:S(2)}) copy-start(bf16[1536,1280]{1,0:T(8,128)(2,1)S(1)} %fusion.11) | copy-start | bytes 11796484
  67.7 25.0 %all-to-all-start.1 = ((bf16[8,64,1280]{2,1,0:T(8,128)(2,1)}), bf16[8,64,1280]{2,1,0:T(8,128)(2,1)S(1)}, u32[]{:S(2)}, u32[]{:S(2)}) async-start(bf16[8,64,1280]{2,1,0:T(8,128)(2,1)} %bitcast.38), calls=%async_computation.1 | async-start | bytes 2621440 | tf_op jit(solution)/shard_map/all_to_all | solution.py:22
  80.4 3.2 %copy-start.7 = (bf16[1536,256]{1,0:T(8,128)(2,1)}, bf16[1536,256]{1,0:T(8,128)(2,1)S(1)}, u32[]{:S(2)}) copy-start(bf16[1536,256]{1,0:T(8,128)(2,1)S(1)} %subtract_convert_fusion.2) | copy-start | bytes 2359300
  80.4 4.2 %copy-start.2 = (bf16[1536,512]{1,0:T(8,128)(2,1)S(1)}, bf16[1536,512]{1,0:T(8,128)(2,1)}, u32[]{:S(2)}) copy-start(bf16[1536,512]{1,0:T(8,128)(2,1)} %copy-done.1) | copy-start | bytes 4718596
  92.7 14.1 %all-to-all-start.3 = ((bf16[8,64,768]{2,1,0:T(8,128)(2,1)}), bf16[8,64,768]{2,1,0:T(8,128)(2,1)S(1)}, u32[]{:S(2)}, u32[]{:S(2)}) async-start(bf16[8,64,768]{2,1,0:T(8,128)(2,1)} %bitcast.40), calls=%async_computation.3 | async-start | bytes 1572864 | tf_op jit(solution)/shard_map/all_to_all | solution.py:22
  107.9 16.8 %all-to-all-start.2 = ((bf16[8,64,1280]{2,1,0:T(8,128)(2,1)}), bf16[8,64,1280]{2,1,0:T(8,128)(2,1)S(1)}, u32[]{:S(2)}, u32[]{:S(2)}) async-start(bf16[8,64,1280]{2,1,0:T(8,128)(2,1)} %broadcast_in_dim.60), calls=%async_computation.2 | async-start | bytes 2621440 | tf_op jit(solution)/shard_map/all_to_all | solution.py:22
  125.6 13.9 %all-to-all-start.4 = ((bf16[8,64,768]{2,1,0:T(8,128)(2,1)}), bf16[8,64,768]{2,1,0:T(8,128)(2,1)S(1)}, u32[]{:S(2)}, u32[]{:S(2)}) async-start(bf16[8,64,768]{2,1,0:T(8,128)(2,1)} %broadcast_in_dim.61), calls=%async_computation.4 | async-start | bytes 1572864 | tf_op jit(solution)/shard_map/all_to_all | solution.py:22
  145.3 11.9 %copy-start.5 = (f32[8,16,1,512]{3,2,1,0:T(1,128)S(1)}, f32[8,16,1,512]{3,2,1,0:T(1,128)}, u32[]{:S(2)}) copy-start(f32[8,16,1,512]{3,2,1,0:T(1,128)} %get-tuple-element.4) | copy-start | bytes 786436
  145.3 11.9 %copy-start.6 = (f32[8,16,1,512]{3,2,1,0:T(1,128)S(1)}, f32[8,16,1,512]{3,2,1,0:T(1,128)}, u32[]{:S(2)}) copy-start(f32[8,16,1,512]{3,2,1,0:T(1,128)} %get-tuple-element.6) | copy-start | bytes 786436
  145.3 32.7 %copy-start.3 = (bf16[768,512]{1,0:T(8,128)(2,1)S(1)}, bf16[768,512]{1,0:T(8,128)(2,1)}, u32[]{:S(2)}) copy-start(bf16[768,512]{1,0:T(8,128)(2,1)} %param.3) | copy-start | bytes 2359300
  146.3 31.7 %collective-permute-start.9 = (bf16[768,512]{1,0:T(8,128)(2,1)}, bf16[768,512]{1,0:T(8,128)(2,1)S(1)}, u32[]{:S(2)}, u32[]{:S(2)}) collective-permute-start(bf16[768,512]{1,0:T(8,128)(2,1)} %slice.48), channel_id=1, source_target_pairs={{0,1},{1,0},{2,3},{3,2},{4,5},{5,4},{6,7},{7,6},{8,9},{9,8},{10,11... | collective-permute-start | bytes 2359304 | tf_op jit(solution)/shard_map/ppermute | solution.py:18
  161.2 14.8 %all-to-all-start.5 = ((f32[128,1,128]{2,1,0:T(1,128)}), f32[128,1,128]{2,1,0:T(1,128)S(1)}, u32[]{:S(2)}, u32[]{:S(2)}) async-start(f32[128,1,128]{2,1,0:T(1,128)} %broadcast_in_dim.65), calls=%async_computation.5 | async-start | bytes 131072 | tf_op jit(solution)/shard_map/all_to_all | solution.py:26
  (3 other events, 4.2 us)

commit v2 on v0

v2 whole, which is shorter than its diff:
```python
import functools

import jax
import jax.numpy as jnp
from jax import lax
from jax.experimental import pallas as pl
from jax.experimental.pallas import tpu as pltpu
from jax.sharding import PartitionSpec as P

F32 = jnp.float32
BF16 = jnp.bfloat16
IMAGES, FEATS, CHIPS = 768, 512, 8
BATCH = IMAGES * 16
CHIP_IMAGES = 2 * IMAGES
HALF = FEATS // 2
SLAB = FEATS // CHIPS
STAT_ROWS = 16

CORE_GROUPS = [[2 * chip + core for chip in range(CHIPS)] for core in range(2)]
VMEM = pl.BlockSpec(memory_space=pltpu.VMEM)
SMEM = pl.BlockSpec(memory_space=pltpu.SMEM)


def shift_row(block, dx, dz):
    pairs = [(2 * x + z, 2 * ((x + dx) % 4) + (z + dz) % 2) for x in range(4) for z in range(2)]
    return lax.ppermute(block, "row", pairs)


def swap_cores(block):
    return lax.ppermute(block, "col", [(i, i ^ 1) for i in range(16)])


def exchange_chips(pieces):
    return lax.all_to_all(pieces, "col", 0, 0, axis_index_groups=CORE_GROUPS)


def share(block, axes, count):
    return lax.all_to_all(jnp.broadcast_to(block[None], (count,) + block.shape), axes, 0, 0)


def call(body, outs, ins, scratch, flops, name):
    specs = [SMEM if a.dtype == jnp.int32 else VMEM for a in ins]
    moved = sum(a.size * a.dtype.itemsize for a in list(ins) + list(outs))
    return pl.pallas_call(
        body,
        out_shape=tuple(jax.ShapeDtypeStruct(a.shape, a.dtype) for a in outs),
        in_specs=specs,
        out_specs=tuple(VMEM for _ in outs),
        scratch_shapes=scratch,
        compiler_params=pltpu.CompilerParams(vmem_limit_bytes=48 * 2**20),
        cost_estimate=pl.CostEstimate(flops=flops, bytes_accessed=moved, transcendentals=0),
        name=name,
    )(*ins)


def shape(dims, dtype):
    return jax.ShapeDtypeStruct(dims, dtype)


def layout(chunks):
    places, column, at = [], 0, 0
    while at < len(chunks):
        rows, width = chunks[at].shape
        count = CHIP_IMAGES // rows
        for part in range(count):
            places.append((at + part, part * rows, column))
        column += width
        at += count
    return places, column


def split3(value):
    high = value.astype(BF16).astype(F32)
    middle = (value - high).astype(BF16).astype(F32)
    return [high, middle, value - high - middle]


def column_sum(ref):
    ones = jnp.ones((8, ref.shape[0]), BF16)
    return jnp.dot(ones, ref[...], preferred_element_type=F32)[0:1]


def center_into(target, first, column, ref, mean):
    width = ref.shape[1]
    step = 128

    def body(i, carry):
        at = pl.multiple_of(i * step, step)
        block = ref[pl.ds(at, step), :].astype(F32) - mean
        target[pl.ds(first + at, step), column:column + width] = block.astype(BF16)
        return carry

    lax.fori_loop(0, ref.shape[0] // step, body, 0)


def fill_columns(places, refs, columns, stats):
    means = {}
    for at, _, column in places:
        means[column] = means.get(column, 0.0) + column_sum(refs[at])
    for column, total in means.items():
        mean = total / CHIP_IMAGES
        stats[0:1, column:column + mean.shape[1]] = mean
        means[column] = mean
    for at, first, column in places:
        center_into(columns, first, column, refs[at], means[column])


def write_message(message, rows_t, columns, stats, row_mean, width):
    for piece in range(CHIPS):
        part = jnp.dot(
            rows_t[piece * SLAB:(piece + 1) * SLAB, :], columns[...], preferred_element_type=F32
        )
        message[piece, 0:SLAB, :] = part.astype(BF16)
    lines = split3(stats[0:1, :])
    if row_mean is not None:
        pad = jnp.zeros((1, width - FEATS), F32)
        lines += [jnp.concatenate([line, pad], axis=1) for line in split3(row_mean)]
    lines.append(jnp.zeros((STAT_ROWS - len(lines), width), F32))
    block = jnp.concatenate(lines, axis=0).astype(BF16)
    for piece in range(CHIPS):
        message[piece, SLAB:SLAB + STAT_ROWS, :] = block


def near_kernel(places, width, count, *refs):
    own, sibling = refs[0], refs[1]
    chunks = refs[2:2 + count]
    message, rows_t, rows, columns, stats = refs[2 + count:]
    row_mean = (column_sum(own) + column_sum(sibling)) / CHIP_IMAGES
    center_into(rows, 0, 0, own, row_mean)
    center_into(rows, IMAGES, 0, sibling, row_mean)
    for at in range(0, FEATS, 128):
        rows_t[at:at + 128, :] = rows[:, at:at + 128].T
    fill_columns(places, chunks, columns, stats)
    write_message(message, rows_t, columns, stats, row_mean, width)


def later_kernel(places, width, count, *refs):
    rows_t = refs[0]
    chunks = refs[1:1 + count]
    message, columns, stats = refs[1 + count:]
    fill_columns(places, chunks, columns, stats)
    write_message(message, rows_t, columns, stats, None, width)


def partial_near(own, sibling, chunks):
    places, width = layout(chunks)
    return call(
        functools.partial(near_kernel, places, width, len(chunks)),
        [shape((CHIPS, SLAB + STAT_ROWS, width), BF16), shape((FEATS, CHIP_IMAGES), BF16)],
        [own, sibling] + chunks,
        [
            pltpu.VMEM((CHIP_IMAGES, FEATS), BF16),
            pltpu.VMEM((CHIP_IMAGES, width), BF16),
            pltpu.VMEM((8, width), F32),
        ],
        2 * CHIP_IMAGES * FEATS * width,
        "partial_near",
    )


def partial_later(rows_t, chunks, name):
    places, width = layout(chunks)
    return call(
        functools.partial(later_kernel, places, width, len(chunks)),
        [shape((CHIPS, SLAB + STAT_ROWS, width), BF16)],
        [rows_t] + chunks,
        [pltpu.VMEM((CHIP_IMAGES, width), BF16), pltpu.VMEM((8, width), F32)],
        2 * CHIP_IMAGES * FEATS * width,
        name,
    )[0]


def combine(place, received, masked, part, means, offsets, row_offsets):
    total = jnp.zeros((SLAB, received.shape[2]), F32)
    lines = []
    for chip in range(CHIPS):
        total = total + received[chip, 0:SLAB, :].astype(F32)
        stats = received[chip, SLAB:SLAB + STAT_ROWS, :].astype(F32)
        lines.append(stats[0:1] + stats[1:2] + stats[2:3])
    local = jnp.concatenate(lines, axis=0)
    mean = jnp.sum(local, axis=0, keepdims=True) / CHIPS
    means[...] = jnp.broadcast_to(mean, means.shape)
    offsets[...] = lax.dot_general(
        row_offsets[...],
        local - mean,
        (((0,), (0,)), ((), ())),
        precision=lax.Precision.HIGHEST,
        preferred_element_type=F32,
    )
    first = pl.multiple_of(place[0] % 2 * SLAB, SLAB)
    covar = (total + CHIP_IMAGES * offsets[pl.ds(first, SLAB), :]) / (BATCH - 1)
    return covar


def finish(covar, masked, part):
    part[...] = jnp.broadcast_to(jnp.sum(covar * covar, keepdims=True), part.shape)
    masked_b = covar.astype(BF16)
    for piece in range(CHIPS):
        masked[piece] = masked_b


def combine_near_kernel(place, received, masked, part, means, row_offsets, offsets, all_rows):
    lines = []
    for chip in range(CHIPS):
        stats = received[chip, SLAB:SLAB + STAT_ROWS, 0:FEATS].astype(F32)
        lines.append(stats[3:4] + stats[4:5] + stats[5:6])
    local = jnp.concatenate(lines, axis=0)
    all_rows[...] = local - jnp.sum(local, axis=0, keepdims=True) / CHIPS
    block = pl.multiple_of(place[0] // 2 * 128, 128)
    row_offsets[...] = all_rows[:, pl.ds(block, 128)]
    covar = combine(place, received, masked, part, means, offsets, row_offsets)
    row_ids = place[0] * SLAB + lax.broadcasted_iota(jnp.int32, covar.shape, 0)
    col_ids = lax.broadcasted_iota(jnp.int32, covar.shape, 1)
    on_diagonal = (col_ids < HALF) & (row_ids == col_ids + place[1] * HALF)
    finish(jnp.where(on_diagonal, F32(0.0), covar), masked, part)


def combine_later_kernel(place, received, row_offsets, masked, part, means, offsets):
    covar = combine(place, received, masked, part, means, offsets, row_offsets)
    finish(covar, masked, part)


def combined(place, received, row_offsets, name):
    width = received.shape[2]
    outs = [
        shape((CHIPS, SLAB, width), BF16),
        shape((8, 128), F32),
        shape((8, width), F32),
    ]
    scratch = [pltpu.VMEM((128, width), F32)]
    flops = 24 * SLAB * width
    if row_offsets is None:
        outs.append(shape((8, 128), F32))
        scratch.append(pltpu.VMEM((8, FEATS), F32))
        return call(combine_near_kernel, outs, [place, received], scratch, flops, name)
    return call(
        combine_later_kernel, outs, [place, received, row_offsets], scratch, flops, name
    )


def grad_kernel(places, count, first, rows, with_sum, kind, *refs):
    chunks = refs[:count]
    means, masked = refs[count], refs[count + 1]
    rest = refs[count + 2:]
    previous = rest[0] if with_sum else None
    out, columns = rest[-2], rest[-1]
    width = masked.shape[1]
    step = 256
    for at in range(first, first + rows, step):
        for index, start, column in places:
            chunk = chunks[index]
            if start <= at < start + chunk.shape[0]:
                span = chunk.shape[1]
                block = chunk[at - start:at - start + step, :].astype(F32)
                block = block - means[0:1, column:column + span]
                columns[:, column:column + span] = block.astype(BF16)
        product = lax.dot_general(
            columns[...], masked[...], (((1,), (1,)), ((), ())), preferred_element_type=F32
        )
        if with_sum:
            product = product + previous[at:at + step, :]
        out[at - first:at - first + step, :] = product.astype(out.dtype)


def grad_part(chunks, means, masked, previous, first, rows, dtype, name):
    places, width = layout(chunks)
    ins = list(chunks) + [means, masked] + ([previous] if previous is not None else [])
    return call(
        functools.partial(
            grad_kernel, places, len(chunks), first, rows, previous is not None, None
        ),
        [shape((rows, FEATS), dtype)],
        ins,
        [pltpu.VMEM((256, width), BF16)],
        2 * rows * FEATS * width,
        name,
    )[0]


def per_device(student, teacher):
    row_index = lax.axis_index("row")
    col_index = lax.axis_index("col")
    core = col_index % 2
    place = jnp.stack([col_index // 2, core]).astype(jnp.int32)

    sibling = swap_cores(student)
    own_a = lax.dynamic_slice_in_dim(student, core * HALF, HALF, 1)
    x_lo_a = shift_row(own_a, 1, 0)
    x_hi_a = shift_row(own_a, -1, 0)
    z_own_a = shift_row(own_a, 0, 1)
    own_b = lax.dynamic_slice_in_dim(sibling, core * HALF, HALF, 1)
    x_lo_b = shift_row(own_b, 1, 0)
    x_hi_b = shift_row(own_b, -1, 0)
    z_own_b = shift_row(own_b, 0, 1)
    x_far_a = shift_row(x_lo_a, 1, 0)
    x_far_b = shift_row(x_hi_b, -1, 0)
    z_own_0 = jnp.concatenate([z_own_a[:, :128], z_own_b[:, :128]], axis=0)
    z_own_1 = jnp.concatenate([z_own_a[:, 128:], z_own_b[:, 128:]], axis=0)
    z_lo_0 = shift_row(z_own_0, 1, 0)
    z_hi_0 = shift_row(z_own_0, -1, 0)
    z_lo_1 = shift_row(z_own_1, 1, 0)
    z_hi_1 = shift_row(z_own_1, -1, 0)
    x_far_0 = jnp.concatenate([x_far_a[:, :128], x_far_b[:, :128]], axis=0)
    x_far_1 = jnp.concatenate([x_far_a[:, 128:], x_far_b[:, 128:]], axis=0)
    z_far_0 = shift_row(x_far_0, 0, 1)
    z_far_1 = shift_row(x_far_1, 0, 1)

    near = [own_a, own_b, x_lo_a, x_lo_b, x_hi_a, x_hi_b, z_own_a, z_own_b]
    middle = [x_far_a, x_far_b, z_lo_0, z_hi_0, z_far_0]
    far = [z_lo_1, z_hi_1, z_far_1]

    near_sums, rows_t = partial_near(student, sibling, near)
    near_received = exchange_chips(near_sums)
    middle_received = exchange_chips(partial_later(rows_t, middle, "partial_middle"))
    far_received = exchange_chips(partial_later(rows_t, far, "partial_far"))

    near_masked, near_part, near_means, row_offsets = combined(
        place, near_received, None, "combine_near"
    )
    middle_masked, middle_part, middle_means = combined(
        place, middle_received, row_offsets, "combine_middle"
    )
    far_masked, far_part, far_means = combined(place, far_received, row_offsets, "combine_far")
    near_all = exchange_chips(near_masked).reshape(FEATS, -1)
    middle_all = exchange_chips(middle_masked).reshape(FEATS, -1)
    far_all = exchange_chips(far_masked).reshape(FEATS, -1)

    floats = student.astype(F32)
    sums = jnp.sum(floats, axis=0)
    dev = floats - sums / IMAGES
    squares = jnp.sum(dev * dev, axis=0)
    message = jnp.concatenate([sums.reshape(4, 128), squares.reshape(4, 128)], axis=0)
    stats = lax.all_gather(message, "col").reshape(16, 2, FEATS)
    average = jnp.sum(stats[:, 0], axis=0) / BATCH
    shift = stats[:, 0] / IMAGES - average
    variance = jnp.sum(stats[:, 1] + IMAGES * (shift * shift), axis=0) / (BATCH - 1)
    spread = jnp.sqrt(variance + 0.0001)
    var_part = jnp.sum(jnp.maximum(0.0, 1.0 - spread)) / 16
    diff = floats - teacher.astype(F32)
    inv_part = jnp.sum(diff * diff)
    hinge = jnp.where(spread < 1.0, (floats - average) / (spread * (BATCH - 1)), F32(0.0))
    base = lax.optimization_barrier(25.0 * diff / 32.0 - 25.0 * BATCH / 64.0 * hinge)

    cov_part = near_part[0, 0] + middle_part[0, 0] + far_part[0, 0]
    lanes = jnp.arange(128, dtype=jnp.int32)[None, :]
    parts = jnp.where(
        lanes == 0, cov_part, jnp.where(lanes == 1, inv_part, jnp.where(lanes == 2, var_part, 0.0))
    )
    totals = jnp.sum(share(parts, ("row", "col"), 128), axis=(0, 1))

    grads = grad_part(near, near_means, near_all, None, 0, CHIP_IMAGES, F32, "grad_near")
    grads = grad_part(middle, middle_means, middle_all, grads, 0, CHIP_IMAGES, F32, "grad_middle")
    outgoing = grad_part(far, far_means, far_all, grads, IMAGES, IMAGES, BF16, "grad_far_sent")
    outgoing, totals = lax.optimization_barrier((outgoing, totals))
    incoming = swap_cores(outgoing)
    kept = grad_part(far, far_means, far_all, grads, 0, IMAGES, F32, "grad_far_kept")

    cov_sum, inv_sum, var_sum = totals[0], totals[1], totals[2]
    total_feats = 8 * FEATS
    total_loss = (
        25.0 * inv_sum / (BATCH * total_feats)
        + 25.0 * var_sum / total_feats
        + cov_sum / total_feats
    )
    gradient = base + BATCH / (16.0 * (BATCH - 1)) * (kept + incoming.astype(F32))
    return (gradient, total_loss)


def solution(mesh):
    in_specs = (P("col", "row"), P("col", "row"))
    out_specs = (P("col", "row"), P())
    return jax.shard_map(
        per_device, mesh=mesh, in_specs=in_specs, out_specs=out_specs, check_vma=False
    )
```

time: 470 us -> 223 us (0.47)
  waiting for transfers between devices: 344 us -> 40.9 us
  starting transfers between devices: 0.12 us -> 42.2 us
  Pallas kernels: 0 us -> 33.6 us
  matrix products: 17 us -> 0 us
  blocking collectives: 64.6 us -> 74.9 us
  between operations: 16.8 us -> 6.67 us
  other arithmetic: 19 us -> 9.05 us
  local copies, waits for them, and re-layouts: 7.79 us -> 14.4 us
    all_gather x2 -> x0, waiting for transfers between devices: 222 us -> none  [the longest x1 126 us: per_device(): columns = lax.all_gather(own_piece, 'row', axis=1, tiled=True)]
    reduce_scatter x1 -> x0, waiting for transfers between devices: 122 us -> none  [per_device(): lax.psum_scatter(lax.dot_general(columns, masked_b, (((1,), (1,)), ((), (...]
    psum x1 -> x0, blocking collectives: 64.6 us -> none  [per_device(): lax.psum((cov_part, var_part, inv_part), ('row', 'col'))]
    all_to_all x0 -> x3, blocking collectives: none -> 47.5 us  [the longest x2 33.7 us: exchange_chips(): return lax.all_to_all(pieces, 'col', 0, 0, axis_index_groups=CORE_GROUPS)]
    ppermute x0 -> x16, waiting for transfers between devices: none -> 33.8 us  [the longest x14 33.8 us: shift_row(): return lax.ppermute(block, 'row', pairs)]
    pallas_call x0 -> x10, Pallas kernels: none -> 33.6 us  [call(): pl.pallas_call(body, out_shape=tuple((jax.ShapeDtypeStruct(a.shape, a.dty...]
    all_gather x0 -> x1, blocking collectives: none -> 27.3 us  [per_device(): stats = lax.all_gather(message, 'col').reshape(16, 2, FEATS)]
    all_to_all x0 -> x4, starting transfers between devices: none -> 22 us  [exchange_chips(): return lax.all_to_all(pieces, 'col', 0, 0, axis_index_groups=CORE_GROUPS)]
  transfers between devices with their start and end apart: 3 -> 20, of which waited for: 3 -> 7; matrix products, arithmetic and copies ran while one was open for 0% -> 5% of each run, Pallas kernels for 0% -> 10%
where the time goes in v2:
time: 223 us; the launch traced here: 222 us
  blocking collectives  74.9 us (34%)
  starting transfers between devices  42.2 us (19%)
  waiting for transfers between devices  40.9 us (18%)
  Pallas kernels  33.6 us (15%)
  local copies, waits for them, and re-layouts  14.4 us (6%)
  other arithmetic  9.05 us (4%)
  between operations  6.67 us (3%)
    ppermute x14, waiting for transfers between devices, shift_row(): return lax.ppermute(block, 'row', pairs)  33.8 us
    all_to_all x2, blocking collectives, exchange_chips(): return lax.all_to_all(pieces, 'col', 0, 0, axis_index_groups=CORE_GROUPS)  33.7 us
    pallas_call x10, Pallas kernels, call(): pl.pallas_call(body, out_shape=tuple((jax.ShapeDtypeStruct(a.shape, a.dty...  33.6 us
    all_gather x1, blocking collectives, per_device(): stats = lax.all_gather(message, 'col').reshape(16, 2, FEATS)  27.3 us
    all_to_all x4, starting transfers between devices, exchange_chips(): return lax.all_to_all(pieces, 'col', 0, 0, axis_index_groups=CORE_GROUPS)  22 us
    ppermute x14, starting transfers between devices, shift_row(): return lax.ppermute(block, 'row', pairs)  16.1 us
    all_to_all x1, blocking collectives, share(): lax.all_to_all(jnp.broadcast_to(block[None], (count,) + block.shape), axe...  13.8 us
    unnamed x80, local copies, waits for them, and re-layouts  9.53 us
  transfers between devices with their start and end apart: 20, of which 7 were waited for; matrix products, arithmetic and copies ran while one was open for 5% of the time, Pallas kernels for 10%

profile of v2, /device:TPU:1, one launch (start us, length us, event | category | flops | bytes accessed | tf_op | source)
XLA Modules:
  0.0 221.8 jit_solution(3438778115190595163)
XLA Ops:
  7.6 7.5 %collective-permute-done.5.refs_4_.refs_2_ = bf16[768,256]{1,0:T(8,128)(2,1)S(1)} collective-permute-done((bf16[768,256]{1,0:T(8,128)(2,1)S(1)}, bf16[768,256]{1,0:T(8,128)(2,1)S(1)}, u32[]{:S(2)}, u32[]{:S(2)}) %collective-permute-start.5) | collective-permute-done | bytes 393248 | tf_op jit(solution)/shard_map/ppermute | solution.py:26
  15.2 2.5 %multiply_reduce_fusion = (f32[]{:T(128)}, f32[512]{0:T(512)S(1)}) fusion(bf16[768,512]{1,0:T(8,128)(2,1)} %param.3, bf16[768,512]{1,0:T(8,128)(2,1)} %refs_0_.1), kind=kLoop, calls=%fused_computation.11 | loop fusion | flops 2358783 | bytes 1574916 | tf_op jit(solution)/shard_map/reduce_sum | solution.py:340
  22.9 3.3 %collective-permute-done.6.refs_1_.refs_0_ = bf16[768,256]{1,0:T(8,128)(2,1)S(1)} collective-permute-done((bf16[768,256]{1,0:T(8,128)(2,1)S(1)}, bf16[768,256]{1,0:T(8,128)(2,1)S(1)}, u32[]{:S(2)}, u32[]{:S(2)}) %collective-permute-start.6) | collective-permute-done | bytes 393248 | tf_op jit(solution)/shard_map/ppermute | solution.py:26
  26.9 7.6 %collective-permute-done.10.refs_5_.refs_3_ = bf16[768,256]{1,0:T(8,128)(2,1)S(1)} collective-permute-done((bf16[768,256]{1,0:T(8,128)(2,1)S(1)}, bf16[768,256]{1,0:T(8,128)(2,1)S(1)}, u32[]{:S(2)}, u32[]{:S(2)}) %collective-permute-start.10) | collective-permute-done | bytes 393248 | tf_op jit(solution)/shard_map/ppermute | solution.py:26
  34.6 8.6 %partial_near.1 = (bf16[8,80,1024]{2,1,0:T(8,128)(2,1)}, bf16[512,1536]{1,0:T(8,128)(2,1)}) custom-call(bf16[768,512]{1,0:T(8,128)(2,1)S(1)} %copy-done.1, bf16[768,512]{1,0:T(8,128)(2,1)S(1)} %collective-permute-done.1.refs_1_, bf16[768,256]{1,0:T(8,128)(2,1)S(1)} %constant_dynamic-slice_fusion.1.refs_2_.refs_0_, ...), custom_call_target="tpu_custom_call" | custom-call | flops 1610612736 | bytes 7602176 | tf_op jit(solution)/shard_map/partial_near/pallas_call | solution.py:44
  43.3 7.6 %all-to-all-start.1 = ((bf16[8,80,1024]{2,1,0:T(8,128)(2,1)}), bf16[8,80,1024]{2,1,0:T(8,128)(2,1)}, u32[]{:S(2)}, u32[]{:S(2)}) async-start(bf16[8,80,1024]{2,1,0:T(8,128)(2,1)} %get-tuple-element.17), calls=%async_computation.1 | async-start | bytes 2621440 | tf_op jit(solution)/shard_map/all_to_all | solution.py:34
  53.9 6.0 %collective-permute-done.8.refs_2_.refs_1_ = bf16[768,256]{1,0:T(8,128)(2,1)S(1)} collective-permute-done((bf16[768,256]{1,0:T(8,128)(2,1)}, bf16[768,256]{1,0:T(8,128)(2,1)S(1)}, u32[]{:S(2)}, u32[]{:S(2)}) %collective-permute-start.8) | collective-permute-done | bytes 393248 | tf_op jit(solution)/shard_map/ppermute | solution.py:26
  61.6 2.7 %collective-permute-start.13 = (bf16[1536,128]{1,0:T(8,128)(2,1)}, bf16[1536,128]{1,0:T(8,128)(2,1)}, u32[]{:S(2)}, u32[]{:S(2)}) collective-permute-start(bf16[1536,128]{1,0:T(8,128)(2,1)} %pad_maximum_fusion.2), channel_id=1, source_target_pairs={{0,96},{16,112},{32,0},{48,16},{64,32},{80,48},{96,64},{112,80},{1... | collective-permute-start | bytes 1179656 | tf_op jit(solution)/shard_map/ppermute | solution.py:26
  65.8 2.4 %collective-permute-done.4.refs_2_.refs_1_ = bf16[1536,128]{1,0:T(8,128)(2,1)S(1)} collective-permute-done((bf16[1536,128]{1,0:T(8,128)(2,1)S(1)}, bf16[1536,128]{1,0:T(8,128)(2,1)S(1)}, u32[]{:S(2)}, u32[]{:S(2)}) %collective-permute-start.4) | collective-permute-done | bytes 393248 | tf_op jit(solution)/shard_map/ppermute | solution.py:26
  68.2 6.8 %collective-permute-done.9.refs_3_.refs_2_ = bf16[1536,128]{1,0:T(8,128)(2,1)S(1)} collective-permute-done((bf16[1536,128]{1,0:T(8,128)(2,1)S(1)}, bf16[1536,128]{1,0:T(8,128)(2,1)S(1)}, u32[]{:S(2)}, u32[]{:S(2)}) %collective-permute-start.9) | collective-permute-done | bytes 393248 | tf_op jit(solution)/shard_map/ppermute | solution.py:26
  75.0 2.3 %partial_far.1 = bf16[8,80,384]{2,1,0:T(8,128)(2,1)S(1)} custom-call(bf16[512,1536]{1,0:T(8,128)(2,1)S(1)} %copy-done.3, bf16[1536,128]{1,0:T(8,128)(2,1)S(1)} %collective-permute-done.3.refs_1_.refs_0_, bf16[1536,128]{1,0:T(8,128)(2,1)S(1)} %collective-permute-done.4.refs_2_.refs_1_, bf16[1536,128]{1,0:T(8,128)(2,1)S(1)} %collective-permute-done.9.refs_3_.refs_2_), custom_call_target="tpu_custom_call" | custom-call | flops 603979776 | bytes 3244032 | tf_op jit(solution)/shard_map/partial_far/pallas_call | solution.py:44
  79.7 6.8 %all-to-all-start = ((bf16[8,80,384]{2,1,0:T(8,128)(2,1)}), bf16[8,80,384]{2,1,0:T(8,128)(2,1)}, u32[]{:S(2)}, u32[]{:S(2)}) async-start(bf16[8,80,384]{2,1,0:T(8,128)(2,1)} %copy-done.14), calls=%async_computation | async-start | bytes 983040 | tf_op jit(solution)/shard_map/all_to_all | solution.py:34
  86.7 27.3 %all-gather = f32[128,128]{1,0:T(8,128)S(1)} all-gather(f32[8,128]{1,0:T(8,128)S(1)} %pad_maximum_fusion.4), channel_id=2, replica_groups=mesh['row'=8,'col'=16] {'col'}, dimensions={0}, use_global_device_ids=true | all-gather | bytes 69632 | tf_op jit(solution)/shard_map/all_gather | solution.py:333
  114.1 5.0 %partial_middle.1 = bf16[8,80,640]{2,1,0:T(8,128)(2,1)S(1)} custom-call(bf16[512,1536]{1,0:T(8,128)(2,1)S(1)} %copy-done.3, bf16[768,256]{1,0:T(8,128)(2,1)S(1)} %collective-permute-done.6.refs_1_.refs_0_, bf16[768,256]{1,0:T(8,128)(2,1)S(1)} %collective-permute-done.8.refs_2_.refs_1_, bf16[1536,128]{1,0:T(8,128)(2,1)} %collective-permute-done.12.refs_3_.refs_2_, ...), custom_call_target="tpu_custom_call" | custom-call | flops 1006632960 | bytes 4358144 | tf_op jit(solution)/shard_map/partial_middle/pallas_call | solution.py:44
  120.0 3.5 %all-to-all-start.3 = ((bf16[8,80,640]{2,1,0:T(8,128)(2,1)}), bf16[8,80,640]{2,1,0:T(8,128)(2,1)S(1)}, u32[]{:S(2)}, u32[]{:S(2)}) async-start(bf16[8,80,640]{2,1,0:T(8,128)(2,1)} %copy-done.12), calls=%async_computation.3 | async-start | bytes 1638400 | tf_op jit(solution)/shard_map/all_to_all | solution.py:34
  131.3 7.2 %all-to-all-done.3.received = bf16[8,80,640]{2,1,0:T(8,128)(2,1)S(1)} async-done(((bf16[8,80,640]{2,1,0:T(8,128)(2,1)}), bf16[8,80,640]{2,1,0:T(8,128)(2,1)S(1)}, u32[]{:S(2)}, u32[]{:S(2)}) %all-to-all-start.3) | async-done | bytes 819232 | tf_op jit(solution)/shard_map/all_to_all | solution.py:34
  142.8 13.8 %all_to_all.35 = f32[128,1,128]{2,1,0:T(1,128)S(1)} all-to-all(f32[128,1,128]{2,1,0:T(1,128)S(1)} %broadcast_in_dim.40), channel_id=1, replica_groups=mesh['row'=8,'col'=16] {'row','col'}, dimensions={0} | all-to-all | bytes 131072 | tf_op jit(solution)/shard_map/all_to_all | solution.py:38
  156.6 19.1 %all_to_all.36 = bf16[8,64,1024]{2,1,0:T(8,128)(2,1)S(1)} all-to-all(bf16[8,64,1024]{2,1,0:T(8,128)(2,1)S(1)} %get-tuple-element.24), channel_id=1, replica_groups={{0,2,4,6,8,10,12,14},{1,3,5,7,9,11,13,15},{16,18,20,22,24,26,28,30},{17..., dimensions={0} | all-to-all | bytes 2097152 | tf_op jit(solution)/shard_map/all_to_all | solution.py:34
  175.7 14.6 %all_to_all.37 = bf16[8,64,640]{2,1,0:T(8,128)(2,1)} all-to-all(bf16[8,64,640]{2,1,0:T(8,128)(2,1)S(1)} %get-tuple-element.22), channel_id=1, replica_groups={{0,2,4,6,8,10,12,14},{1,3,5,7,9,11,13,15},{16,18,20,22,24,26,28,30},{17..., dimensions={0} | all-to-all | bytes 1310720 | tf_op jit(solution)/shard_map/all_to_all | solution.py:34
  190.4 4.1 %all-to-all-start.2 = ((bf16[8,64,384]{2,1,0:T(8,128)(2,1)}), bf16[8,64,384]{2,1,0:T(8,128)(2,1)}, u32[]{:S(2)}, u32[]{:S(2)}) async-start(bf16[8,64,384]{2,1,0:T(8,128)(2,1)} %copy-done.29), calls=%async_computation.2 | async-start | bytes 786432 | tf_op jit(solution)/shard_map/all_to_all | solution.py:34
  197.0 4.5 %grad_near.1.refs_7_ = f32[1536,512]{1,0:T(8,128)} custom-call(bf16[768,256]{1,0:T(8,128)(2,1)S(1)} %copy-done.20, bf16[768,256]{1,0:T(8,128)(2,1)S(1)} %copy-done.22, bf16[768,256]{1,0:T(8,128)(2,1)S(1)} %copy-done.24, bf16[768,256]{1,0:T(8,128)(2,1)S(1)} %copy-done.28, bf16[768,256]{1,0:T(8,128)(2,1)S(1)} %copy-done.26, ...), custom_call_target="tpu_custom_call" | custom-call | flops 1610612736 | bytes 7372800 | tf_op jit(solution)/shard_map/grad_near/pallas_call | solution.py:44
  201.6 3.7 %grad_middle.1.refs_5_ = f32[1536,512]{1,0:T(8,128)S(1)} custom-call(bf16[768,256]{1,0:T(8,128)(2,1)S(1)} %collective-permute-done.6.refs_1_.refs_0_, bf16[768,256]{1,0:T(8,128)(2,1)S(1)} %copy-done.5, bf16[1536,128]{1,0:T(8,128)(2,1)} %collective-permute-done.12.refs_3_.refs_2_, bf16[1536,128]{1,0:T(8,128)(2,1)} %collective-permute-done.13.refs_4_.refs_3_, ...), custom_call_target="tpu_custom_call" | custom-call | flops 1006632960 | bytes 8933376 | tf_op jit(solution)/shard_map/grad_middle/pallas_call | solution.py:44
  210.4 2.6 %collective-permute-start.15 = (bf16[768,512]{1,0:T(8,128)(2,1)S(1)}, bf16[768,512]{1,0:T(8,128)(2,1)S(1)}, u32[]{:S(2)}, u32[]{:S(2)}) collective-permute-start(bf16[768,512]{1,0:T(8,128)(2,1)S(1)} %grad_far_sent.1), channel_id=1, source_target_pairs={{0,1},{1,0},{2,3},{3,2},{4,5},{5,4},{6,7},{7,6},{8,9},{9,8},{10,11... | collective-permute-start | bytes 2359304 | tf_op jit(solution)/shard_map/ppermute | solution.py:30
  216.4 2.7 %grad_far_kept.1 = f32[768,512]{1,0:T(8,128)S(1)} custom-call(bf16[1536,128]{1,0:T(8,128)(2,1)S(1)} %copy-done.7, bf16[1536,128]{1,0:T(8,128)(2,1)S(1)} %copy-done.9, bf16[1536,128]{1,0:T(8,128)(2,1)S(1)} %copy-done.11, f32[8,384]{1,0:T(8,128)S(1)} %get-tuple-element.19.refs_3_, bf16[512,384]{1,0:T(8,128)(2,1)} %bitcast.5.refs_4_, f32[1536,512]{1,0:T(8,128)} %copy-done), custom_call_target="tpu_custom_call" | custom-call | flops 301989888 | bytes 6303744 | tf_op jit(solution)/shard_map/grad_far_kept/pallas_call | solution.py:44
  (140 shorter events, 42.7 us)
Async XLA Ops:
  0.6 17.1 %collective-permute-start.1 = (bf16[768,512]{1,0:T(8,128)(2,1)}, bf16[768,512]{1,0:T(8,128)(2,1)S(1)}, u32[]{:S(2)}, u32[]{:S(2)}) collective-permute-start(bf16[768,512]{1,0:T(8,128)(2,1)} %refs_0_.1), channel_id=1, source_target_pairs={{0,1},{1,0},{2,3},{3,2},{4,5},{5,4},{6,7},{7,6},{8,9},{9,8},{10,11... | collective-permute-start | bytes 2359304 | tf_op jit(solution)/shard_map/ppermute | solution.py:30
  3.2 31.5 %copy-start.19 = (bf16[768,256]{1,0:T(8,128)(2,1)}, bf16[768,256]{1,0:T(8,128)(2,1)S(1)}, u32[]{:S(2)}) copy-start(bf16[768,256]{1,0:T(8,128)(2,1)S(1)} %constant_dynamic-slice_fusion.1.refs_2_.refs_0_) | copy-start | bytes 1179652
  3.2 12.0 %collective-permute-start.5 = (bf16[768,256]{1,0:T(8,128)(2,1)S(1)}, bf16[768,256]{1,0:T(8,128)(2,1)S(1)}, u32[]{:S(2)}, u32[]{:S(2)}) collective-permute-start(bf16[768,256]{1,0:T(8,128)(2,1)S(1)} %constant_dynamic-slice_fusion.1.refs_2_.refs_0_), channel_id=1, source_target_pairs={{0,32},{16,48},{32,64},{48,80},{64,96},{80,112},{96,0},{112,16},{1... | collective-permute-start | bytes 1179656 | tf_op jit(solution)/shard_map/ppermute | solution.py:26
  4.5 16.1 %collective-permute-start = (bf16[768,256]{1,0:T(8,128)(2,1)S(1)}, bf16[768,256]{1,0:T(8,128)(2,1)S(1)}, u32[]{:S(2)}, u32[]{:S(2)}) collective-permute-start(bf16[768,256]{1,0:T(8,128)(2,1)S(1)} %constant_dynamic-slice_fusion.1.refs_2_.refs_0_), channel_id=1, source_target_pairs={{0,16},{16,0},{32,48},{48,32},{64,80},{80,64},{96,112},{112,96},{1... | collective-permute-start | bytes 1179656 | tf_op jit(solution)/shard_map/ppermute | solution.py:26
  6.2 20.8 %collective-permute-start.11 = (bf16[768,256]{1,0:T(8,128)(2,1)S(1)}, bf16[768,256]{1,0:T(8,128)(2,1)S(1)}, u32[]{:S(2)}, u32[]{:S(2)}) collective-permute-start(bf16[768,256]{1,0:T(8,128)(2,1)S(1)} %constant_dynamic-slice_fusion.1.refs_2_.refs_0_), channel_id=1, source_target_pairs={{0,96},{16,112},{32,0},{48,16},{64,32},{80,48},{96,64},{112,80},{1... | collective-permute-start | bytes 1179656 | tf_op jit(solution)/shard_map/ppermute | solution.py:26
  15.1 11.0 %collective-permute-start.6 = (bf16[768,256]{1,0:T(8,128)(2,1)S(1)}, bf16[768,256]{1,0:T(8,128)(2,1)S(1)}, u32[]{:S(2)}, u32[]{:S(2)}) collective-permute-start(bf16[768,256]{1,0:T(8,128)(2,1)S(1)} %collective-permute-done.5.refs_4_.refs_2_), channel_id=1, source_target_pairs={{0,32},{16,48},{32,64},{48,80},{64,96},{80,112},{96,0},{112,16},{1... | collective-permute-start | bytes 1179656 | tf_op jit(solution)/shard_map/ppermute | solution.py:26
  17.7 16.9 %collective-permute-start.10 = (bf16[768,256]{1,0:T(8,128)(2,1)S(1)}, bf16[768,256]{1,0:T(8,128)(2,1)S(1)}, u32[]{:S(2)}, u32[]{:S(2)}) collective-permute-start(bf16[768,256]{1,0:T(8,128)(2,1)S(1)} %constant_dynamic-slice_fusion.refs_3_.refs_1_), channel_id=1, source_target_pairs={{0,32},{16,48},{32,64},{48,80},{64,96},{80,112},{96,0},{112,16},{1... | collective-permute-start | bytes 1179656 | tf_op jit(solution)/shard_map/ppermute | solution.py:26
  18.9 15.7 %collective-permute-start.2 = (bf16[768,256]{1,0:T(8,128)(2,1)S(1)}, bf16[768,256]{1,0:T(8,128)(2,1)S(1)}, u32[]{:S(2)}, u32[]{:S(2)}) collective-permute-start(bf16[768,256]{1,0:T(8,128)(2,1)S(1)} %constant_dynamic-slice_fusion.refs_3_.refs_1_), channel_id=1, source_target_pairs={{0,16},{16,0},{32,48},{48,32},{64,80},{80,64},{96,112},{112,96},{1... | collective-permute-start | bytes 1179656 | tf_op jit(solution)/shard_map/ppermute | solution.py:26
  20.6 14.0 %collective-permute-start.7 = (bf16[768,256]{1,0:T(8,128)(2,1)S(1)}, bf16[768,256]{1,0:T(8,128)(2,1)}, u32[]{:S(2)}, u32[]{:S(2)}) collective-permute-start(bf16[768,256]{1,0:T(8,128)(2,1)S(1)} %constant_dynamic-slice_fusion.refs_3_.refs_1_), channel_id=1, source_target_pairs={{0,96},{16,112},{32,0},{48,16},{64,32},{80,48},{96,64},{112,80},{1... | collective-permute-start | bytes 1179656 | tf_op jit(solution)/shard_map/ppermute | solution.py:26
  43.3 36.4 %all-to-all-start.1 = ((bf16[8,80,1024]{2,1,0:T(8,128)(2,1)}), bf16[8,80,1024]{2,1,0:T(8,128)(2,1)}, u32[]{:S(2)}, u32[]{:S(2)}) async-start(bf16[8,80,1024]{2,1,0:T(8,128)(2,1)} %get-tuple-element.17), calls=%async_computation.1 | async-start | bytes 2621440 | tf_op jit(solution)/shard_map/all_to_all | solution.py:34
  50.9 9.0 %collective-permute-start.8 = (bf16[768,256]{1,0:T(8,128)(2,1)}, bf16[768,256]{1,0:T(8,128)(2,1)S(1)}, u32[]{:S(2)}, u32[]{:S(2)}) collective-permute-start(bf16[768,256]{1,0:T(8,128)(2,1)} %collective-permute-done.7.refs_7_.refs_5_), channel_id=1, source_target_pairs={{0,96},{16,112},{32,0},{48,16},{64,32},{80,48},{96,64},{112,80},{1... | collective-permute-start | bytes 1179656 | tf_op jit(solution)/shard_map/ppermute | solution.py:26
  51.1 13.9 %collective-permute-start.3 = (bf16[1536,128]{1,0:T(8,128)(2,1)S(1)}, bf16[1536,128]{1,0:T(8,128)(2,1)S(1)}, u32[]{:S(2)}, u32[]{:S(2)}) collective-permute-start(bf16[1536,128]{1,0:T(8,128)(2,1)S(1)} %pad_maximum_fusion), channel_id=1, source_target_pairs={{0,32},{16,48},{32,64},{48,80},{64,96},{80,112},{96,0},{112,16},{1... | collective-permute-start | bytes 1179656 | tf_op jit(solution)/shard_map/ppermute | solution.py:26
  52.6 15.6 %collective-permute-start.4 = (bf16[1536,128]{1,0:T(8,128)(2,1)S(1)}, bf16[1536,128]{1,0:T(8,128)(2,1)S(1)}, u32[]{:S(2)}, u32[]{:S(2)}) collective-permute-start(bf16[1536,128]{1,0:T(8,128)(2,1)S(1)} %pad_maximum_fusion), channel_id=1, source_target_pairs={{0,96},{16,112},{32,0},{48,16},{64,32},{80,48},{96,64},{112,80},{1... | collective-permute-start | bytes 1179656 | tf_op jit(solution)/shard_map/ppermute | solution.py:26
  59.9 54.2 %copy-start.4 = (bf16[768,256]{1,0:T(8,128)(2,1)}, bf16[768,256]{1,0:T(8,128)(2,1)S(1)}, u32[]{:S(2)}) copy-start(bf16[768,256]{1,0:T(8,128)(2,1)S(1)} %collective-permute-done.8.refs_2_.refs_1_) | copy-start | bytes 1179652
  60.0 15.1 %collective-permute-start.9 = (bf16[1536,128]{1,0:T(8,128)(2,1)S(1)}, bf16[1536,128]{1,0:T(8,128)(2,1)S(1)}, u32[]{:S(2)}, u32[]{:S(2)}) collective-permute-start(bf16[1536,128]{1,0:T(8,128)(2,1)S(1)} %pad_maximum_fusion.1), channel_id=1, source_target_pairs={{0,16},{16,0},{32,48},{48,32},{64,80},{80,64},{96,112},{112,96},{1... | collective-permute-start | bytes 1179656 | tf_op jit(solution)/shard_map/ppermute | solution.py:26
  61.5 52.5 %collective-permute-start.12 = (bf16[1536,128]{1,0:T(8,128)(2,1)}, bf16[1536,128]{1,0:T(8,128)(2,1)}, u32[]{:S(2)}, u32[]{:S(2)}) collective-permute-start(bf16[1536,128]{1,0:T(8,128)(2,1)} %pad_maximum_fusion.2), channel_id=1, source_target_pairs={{0,32},{16,48},{32,64},{48,80},{64,96},{80,112},{96,0},{112,16},{1... | collective-permute-start | bytes 1179656 | tf_op jit(solution)/shard_map/ppermute | solution.py:26
  61.6 52.5 %collective-permute-start.13 = (bf16[1536,128]{1,0:T(8,128)(2,1)}, bf16[1536,128]{1,0:T(8,128)(2,1)}, u32[]{:S(2)}, u32[]{:S(2)}) collective-permute-start(bf16[1536,128]{1,0:T(8,128)(2,1)} %pad_maximum_fusion.2), channel_id=1, source_target_pairs={{0,96},{16,112},{32,0},{48,16},{64,32},{80,48},{96,64},{112,80},{1... | collective-permute-start | bytes 1179656 | tf_op jit(solution)/shard_map/ppermute | solution.py:26
  65.0 49.1 %collective-permute-start.14 = (bf16[1536,128]{1,0:T(8,128)(2,1)}, bf16[1536,128]{1,0:T(8,128)(2,1)}, u32[]{:S(2)}, u32[]{:S(2)}) collective-permute-start(bf16[1536,128]{1,0:T(8,128)(2,1)} %pad_maximum_fusion.3), channel_id=1, source_target_pairs={{0,16},{16,0},{32,48},{48,32},{64,80},{80,64},{96,112},{112,96},{1... | collective-permute-start | bytes 1179656 | tf_op jit(solution)/shard_map/ppermute | solution.py:26
  79.7 40.3 %all-to-all-start = ((bf16[8,80,384]{2,1,0:T(8,128)(2,1)}), bf16[8,80,384]{2,1,0:T(8,128)(2,1)}, u32[]{:S(2)}, u32[]{:S(2)}) async-start(bf16[8,80,384]{2,1,0:T(8,128)(2,1)} %copy-done.14), calls=%async_computation | async-start | bytes 983040 | tf_op jit(solution)/shard_map/all_to_all | solution.py:34
  120.0 18.5 %all-to-all-start.3 = ((bf16[8,80,640]{2,1,0:T(8,128)(2,1)}), bf16[8,80,640]{2,1,0:T(8,128)(2,1)S(1)}, u32[]{:S(2)}, u32[]{:S(2)}) async-start(bf16[8,80,640]{2,1,0:T(8,128)(2,1)} %copy-done.12), calls=%async_computation.3 | async-start | bytes 1638400 | tf_op jit(solution)/shard_map/all_to_all | solution.py:34
  123.7 32.9 %copy-start.36 = (f32[512]{0:T(512)}, f32[512]{0:T(512)S(1)}, u32[]{:S(2)}) copy-start(f32[512]{0:T(512)S(1)} %broadcast_multiply_fusion.1) | copy-start | bytes 6148
  139.7 50.7 %copy-start.30 = (f32[8,640]{1,0:T(8,128)}, f32[8,640]{1,0:T(8,128)S(1)}, u32[]{:S(2)}) copy-start(f32[8,640]{1,0:T(8,128)S(1)} %get-tuple-element.21.refs_5_) | copy-start | bytes 61444
  190.4 15.0 %all-to-all-start.2 = ((bf16[8,64,384]{2,1,0:T(8,128)(2,1)}), bf16[8,64,384]{2,1,0:T(8,128)(2,1)}, u32[]{:S(2)}, u32[]{:S(2)}) async-start(bf16[8,64,384]{2,1,0:T(8,128)(2,1)} %copy-done.29), calls=%async_computation.2 | async-start | bytes 786432 | tf_op jit(solution)/shard_map/all_to_all | solution.py:34
  210.4 8.6 %collective-permute-start.15 = (bf16[768,512]{1,0:T(8,128)(2,1)S(1)}, bf16[768,512]{1,0:T(8,128)(2,1)S(1)}, u32[]{:S(2)}, u32[]{:S(2)}) collective-permute-start(bf16[768,512]{1,0:T(8,128)(2,1)S(1)} %grad_far_sent.1), channel_id=1, source_target_pairs={{0,1},{1,0},{2,3},{3,2},{4,5},{5,4},{6,7},{7,6},{8,9},{9,8},{10,11... | collective-permute-start | bytes 2359304 | tf_op jit(solution)/shard_map/ppermute | solution.py:30
  (36 other events, 337.4 us)

commit v3 on v0

v3 whole, which is shorter than its diff:
```python
import functools

import jax
import jax.numpy as jnp
from jax import lax
from jax.experimental import pallas as pl
from jax.experimental.pallas import tpu as pltpu
from jax.sharding import PartitionSpec as P

F32 = jnp.float32
BF16 = jnp.bfloat16
IMAGES, FEATS, CHIPS = 768, 512, 8
BATCH = IMAGES * 16
CHIP_IMAGES = 2 * IMAGES
HALF = FEATS // 2
STAT_ROWS = 16

QUARTER = FEATS // 4
VMEM = pl.BlockSpec(memory_space=pltpu.VMEM)
SMEM = pl.BlockSpec(memory_space=pltpu.SMEM)
ANY = pl.BlockSpec(memory_space=pl.ANY)


def shift_row(block, dx, dz):
    pairs = [(2 * x + z, 2 * ((x + dx) % 4) + (z + dz) % 2) for x in range(4) for z in range(2)]
    return lax.ppermute(block, "row", pairs)


def swap_cores(block):
    return lax.ppermute(block, "col", [(i, i ^ 1) for i in range(16)])


def shift_y(block, dy):
    pairs = [
        (8 * z + 2 * y + core, 8 * z + 2 * ((y + dy) % 4) + core)
        for z in range(2) for y in range(4) for core in range(2)
    ]
    return lax.ppermute(block, "col", pairs)


def swap_z_hi(block):
    return lax.ppermute(block, "col", [(i, i ^ 8) for i in range(16)])


def call(body, outs, ins, scratch, name, after=(), flops=0):
    count, waits = len(ins), len(after)

    def kernel(*refs):
        body(*refs[:count], *refs[count + waits:])

    return pl.pallas_call(
        kernel,
        out_shape=tuple(outs),
        in_specs=[SMEM if a.dtype == jnp.int32 else VMEM for a in ins] + [ANY] * waits,
        out_specs=tuple(VMEM for _ in outs),
        scratch_shapes=scratch,
        compiler_params=pltpu.CompilerParams(vmem_limit_bytes=26 * 2**20),
        cost_estimate=pl.CostEstimate(flops=flops, bytes_accessed=0, transcendentals=0),
        name=name,
    )(*ins, *after)


def shape(dims, dtype):
    return jax.ShapeDtypeStruct(dims, dtype)


def layout(chunks):
    places, column, at = [], 0, 0
    while at < len(chunks):
        rows, width = chunks[at].shape
        count = CHIP_IMAGES // rows
        for part in range(count):
            places.append((at + part, part * rows, column))
        column += width
        at += count
    return places, column


def split3(value):
    high = value.astype(BF16).astype(F32)
    middle = (value - high).astype(BF16).astype(F32)
    return [high, middle, value - high - middle]


def column_sum(ref):
    ones = jnp.ones((8, ref.shape[0]), BF16)
    return jnp.dot(ones, ref[...], preferred_element_type=F32)[0:1]


def center_into(target, first, column, ref, mean):
    width = ref.shape[1]
    step = 128

    def body(i, carry):
        at = pl.multiple_of(i * step, step)
        block = ref[pl.ds(at, step), :].astype(F32) - mean
        target[pl.ds(first + at, step), column:column + width] = block.astype(BF16)
        return carry

    lax.fori_loop(0, ref.shape[0] // step, body, 0)


def fill_columns(places, refs, columns, stats):
    means = {}
    for at, _, column in places:
        means[column] = means.get(column, 0.0) + column_sum(refs[at])
    for column, total in means.items():
        mean = total / CHIP_IMAGES
        stats[0:1, column:column + mean.shape[1]] = mean
        means[column] = mean
    for at, first, column in places:
        center_into(columns, first, column, refs[at], means[column])


def center_rows(target, first, ref, mean):
    step = 128

    def body(i, total):
        at = pl.multiple_of(i * step, step)
        block = ref[pl.ds(at, step), :].astype(F32) - mean
        target[pl.ds(first + at, step), :] = block.astype(BF16)
        return total + jnp.sum((block * block).reshape(step // 8, 8, FEATS), axis=0)

    total = lax.fori_loop(0, ref.shape[0] // step, body, jnp.zeros((8, FEATS), F32))
    return jnp.sum(total, axis=0, keepdims=True)


def padded(lines, width):
    pad = width - lines[0].shape[1]
    return [jnp.concatenate([line, jnp.zeros((line.shape[0], pad), F32)], axis=1) for line in lines]


def filled(lines, width):
    count = sum(line.shape[0] for line in lines)
    lines = lines + [jnp.zeros((-count % STAT_ROWS, width), F32)]
    return jnp.concatenate([line for line in lines if line.shape[0]], axis=0)


def rows_kernel(own, sibling, rows_t, row_stats, rows):
    row_mean = (column_sum(own) + column_sum(sibling)) / CHIP_IMAGES
    squares = center_rows(rows, 0, own, row_mean) + center_rows(rows, IMAGES, sibling, row_mean)
    for at in range(0, FEATS, 128):
        rows_t[at:at + 128, :] = rows[:, at:at + 128].T
    row_stats[...] = jnp.concatenate([row_mean, squares, jnp.zeros((6, FEATS), F32)], axis=0)


def center_own(own, sibling):
    return call(
        rows_kernel,
        [shape((FEATS, CHIP_IMAGES), BF16), shape((8, FEATS), F32)],
        [own, sibling],
        [pltpu.VMEM((CHIP_IMAGES, FEATS), BF16)],
        "center_own",
    )


def products(rows_t, columns, at, step):
    return jnp.dot(rows_t[...], columns[:, at:at + step], preferred_element_type=F32)


def partial_kernel(places, width, count, with_rows, *refs):
    place, rows_t, row_stats = refs[:3]
    chunks = refs[3:3 + count]
    pieces = refs[3 + count:7 + count]
    columns, stats, sums = refs[7 + count:]
    fill_columns(places, chunks, columns, stats)
    for at in range(0, width, 256):
        sums[:, at:at + 256] = jnp.dot(
            rows_t[...], columns[:, at:at + 256], preferred_element_type=F32
        )
    lines = split3(stats[0:1, :])
    if with_rows:
        lines += padded(split3(row_stats[0:1, :]) + split3(row_stats[1:2, :]), width)
    block = filled(lines, width)
    for d in range(4):
        first = pl.multiple_of((place[2] + d) % 4 * QUARTER, QUARTER)
        pieces[d][0:QUARTER, :] = sums[pl.ds(first, QUARTER), :].astype(pieces[d].dtype)
        pieces[d][QUARTER:QUARTER + STAT_ROWS, :] = block.astype(pieces[d].dtype)


def partial_sums(place, rows_t, row_stats, chunks, with_rows, name, after=()):
    places, width = layout(chunks)
    rows = QUARTER + STAT_ROWS
    *pieces, columns, stats = call(
        functools.partial(partial_kernel, places, width, len(chunks), with_rows),
        [shape((rows, width), F32)]
        + [shape((rows, width), BF16)] * 3
        + [shape((CHIP_IMAGES, width), BF16), shape((8, width), F32)],
        [place, rows_t, row_stats] + chunks,
        [pltpu.VMEM((FEATS, width), F32)],
        name,
        after,
        flops=2 * CHIP_IMAGES * FEATS * width,
    )
    return pieces, columns, stats


def spread_out(local):
    mean = jnp.sum(local, axis=0, keepdims=True) / CHIPS
    return local - mean, mean


def mean_term(row_offsets, col_offsets):
    return CHIP_IMAGES * lax.dot_general(
        row_offsets,
        col_offsets,
        (((0,), (0,)), ((), ())),
        precision=lax.Precision.HIGHEST,
        preferred_element_type=F32,
    )


def three(stats, first):
    return stats[first:first + 1] + stats[first + 1:first + 2] + stats[first + 2:first + 3]


def combine_y_kernel(with_rows, place, own, one, two, three_on, plane, message, local, *row_local):
    width = own.shape[1]
    columns = jnp.zeros((4, width), F32)
    rows = jnp.zeros((4, FEATS), F32)
    squares = jnp.zeros((1, FEATS), F32)
    total = own[0:QUARTER, :]
    for d, piece in enumerate((own, one, two, three_on)):
        if d:
            total = total + piece[0:QUARTER, :].astype(F32)
        at = (place[2] + 4 - d) % 4
        stats = piece[QUARTER:QUARTER + STAT_ROWS, :].astype(F32)
        here = lax.broadcasted_iota(jnp.int32, columns.shape, 0) == at
        columns = jnp.where(here, three(stats, 0), columns)
        if with_rows:
            here = lax.broadcasted_iota(jnp.int32, rows.shape, 0) == at
            rows = jnp.where(here, three(stats[:, 0:FEATS], 3), rows)
            squares = squares + three(stats[:, 0:FEATS], 6)

    def rounded(value):
        high, middle, low = split3(value)
        low = low.astype(BF16).astype(F32)
        return [high, middle, low], high + middle + low

    plane[...] = total.astype(BF16)
    message[0:QUARTER, :] = total.astype(BF16)
    lines, local[0:4, :] = rounded(columns)
    if with_rows:
        row_lines, row_local[0][0:4, :] = rounded(rows)
        square_lines, row_local[0][4:5, :] = rounded(squares)
        lines = lines + padded(row_lines + square_lines, width)
    block = filled(lines, width)
    message[QUARTER:QUARTER + block.shape[0], :] = block.astype(BF16)


def combine_y(place, pieces, with_rows, name, after):
    width = pieces[0].shape[1]
    rows = QUARTER + (2 if with_rows else 1) * STAT_ROWS
    outs = [shape((QUARTER, width), BF16), shape((rows, width), BF16), shape((8, width), F32)]
    outs += [shape((8, FEATS), F32)] if with_rows else []
    return call(
        functools.partial(combine_y_kernel, with_rows), outs, [place] + pieces, [], name, after
    )


def all_chips(place, mine, theirs):
    low = place[3] == 0
    return jnp.concatenate([jnp.where(low, mine, theirs), jnp.where(low, theirs, mine)], axis=0)


def combine_z_kernel(
    with_rows, place, plane, local, rows, received, parts, masked, part, means, *more
):
    stats = received[QUARTER:, :].astype(F32)
    theirs = stats[0:4] + stats[4:8] + stats[8:12]
    col_off, col_mean = spread_out(all_chips(place, local[0:4, :], theirs))
    means[...] = jnp.broadcast_to(col_mean, means.shape)
    row_offsets = rows
    if with_rows:
        row_offsets, row_stats = more
        stats = stats[:, 0:FEATS]
        theirs = stats[12:16] + stats[16:20] + stats[20:24]
        row_off, row_mean = spread_out(all_chips(place, rows[0:4, :], theirs))
        squares = rows[4:5, :] + three(stats, 24)
        squares = squares + CHIP_IMAGES * jnp.sum(row_off * row_off, axis=0, keepdims=True)
        variance = squares / (BATCH - 1)
        row_offsets[...] = row_off
        row_stats[...] = jnp.concatenate([row_mean, variance, jnp.zeros((6, FEATS), F32)], axis=0)
    block = pl.multiple_of(place[2] * QUARTER, QUARTER)
    term = mean_term(row_offsets[:, pl.ds(block, QUARTER)], col_off)
    covar = plane[...].astype(F32) + received[0:QUARTER, :].astype(F32)
    covar = (covar + term) / (BATCH - 1)
    if with_rows:
        row_ids = place[2] * QUARTER + lax.broadcasted_iota(jnp.int32, covar.shape, 0)
        col_ids = lax.broadcasted_iota(jnp.int32, covar.shape, 1)
        on_diagonal = (col_ids < HALF) & (row_ids == col_ids + place[1] * HALF)
        covar = jnp.where(on_diagonal, F32(0.0), covar)
    lanes = lax.broadcasted_iota(jnp.int32, part.shape, 1)
    part[...] = parts[...] + jnp.where(lanes == 0, jnp.sum(covar * covar, keepdims=True), 0.0)
    masked[0:QUARTER, :] = covar.astype(BF16)
    if not with_rows:
        block = filled(padded(split3(part[0:1, :]), covar.shape[1]), covar.shape[1])
        masked[QUARTER:QUARTER + STAT_ROWS, :] = block.astype(BF16)


def combine_z(place, plane, local, rows, received, parts, with_rows, name, after=()):
    width = plane.shape[1]
    count = QUARTER + (0 if with_rows else STAT_ROWS)
    outs = [shape((count, width), BF16), shape((8, 128), F32), shape((8, width), F32)]
    outs += [shape((8, FEATS), F32)] * 2 if with_rows else []
    ins = [place, plane, local, rows, received, parts]
    return call(functools.partial(combine_z_kernel, with_rows), outs, ins, [], name, after)


def parts_kernel(place, own, one, two, three_on, out):
    lines = jnp.zeros((4, 128), F32)
    for d, piece in enumerate((own, one, two, three_on)):
        here = lax.broadcasted_iota(jnp.int32, lines.shape, 0) == (place[2] + 4 - d) % 4
        lines = jnp.where(here, three(piece[QUARTER:, 0:128].astype(F32), 0), lines)
    out[...] = jnp.broadcast_to(jnp.sum(lines, axis=0, keepdims=True), out.shape)


def sum_parts(place, pieces, after):
    return call(
        parts_kernel, [shape((8, 128), F32)], [place] + pieces, [], "sum_parts", after
    )[0]


def shift_term(stats, means, masked):
    lines = filled(split3(stats[0:1, :] - means[0:1, :]), stats.shape[1]).astype(BF16)
    rows = lax.dot_general(
        lines, masked[...], (((1,), (1,)), ((), ())), preferred_element_type=F32
    )
    return rows[0:1] + rows[1:2] + rows[2:3]


def times_masked(columns, at, masked):
    return lax.dot_general(
        columns[at:at + 256, :], masked[...], (((1,), (1,)), ((), ())), preferred_element_type=F32
    )


def grad_kernel(
    first, rows, add, place, columns, stats, means, own, one, two, three_on, *rest
):
    out, masked = rest[-2:]
    for d, piece in enumerate((own, one, two, three_on)):
        row = pl.multiple_of((place[2] + 4 - d) % 4 * QUARTER, QUARTER)
        masked[pl.ds(row, QUARTER), :] = piece[0:QUARTER, :]
    shift = shift_term(stats, means, masked)
    for at in range(first, first + rows, 256):
        product = times_masked(columns, at, masked) + shift
        if add:
            product = product + rest[0][at:at + 256, :]
        out[at - first:at - first + 256, :] = product.astype(out.dtype)


def grad_part(place, inputs, pieces, previous, first, rows, dtype, name, after=()):
    columns, stats, means = inputs
    ins = [place, columns, stats, means] + pieces + ([] if previous is None else [previous])
    return call(
        functools.partial(grad_kernel, first, rows, previous is not None),
        [shape((rows, FEATS), dtype)],
        ins,
        [pltpu.VMEM((FEATS, columns.shape[1]), BF16)],
        name,
        after,
    )[0]


def per_device(student, teacher):
    row_index = lax.axis_index("row")
    col_index = lax.axis_index("col")
    core = col_index % 2
    chip = col_index // 2
    place = jnp.stack([chip, core, chip % 4, chip // 4]).astype(jnp.int32)

    sibling = swap_cores(student)
    own_a = lax.dynamic_slice_in_dim(student, core * HALF, HALF, 1)
    x_lo_a = shift_row(own_a, 1, 0)
    x_hi_a = shift_row(own_a, -1, 0)
    z_own_a = shift_row(own_a, 0, 1)
    own_b = lax.dynamic_slice_in_dim(sibling, core * HALF, HALF, 1)
    x_lo_b = shift_row(own_b, 1, 0)
    x_hi_b = shift_row(own_b, -1, 0)
    z_own_b = shift_row(own_b, 0, 1)
    x_far_a = shift_row(x_lo_a, 1, 0)
    x_far_b = shift_row(x_hi_b, -1, 0)
    z_lo_a = shift_row(z_own_a, 1, 0)
    z_hi_a = shift_row(z_own_a, -1, 0)
    z_lo_b = shift_row(z_own_b, 1, 0)
    z_hi_b = shift_row(z_own_b, -1, 0)
    z_far_a = shift_row(x_far_a, 0, 1)
    z_far_b = shift_row(x_far_b, 0, 1)
    near = [own_a, own_b, x_lo_a, x_lo_b, x_hi_a, x_hi_b, z_own_a, z_own_b]

    rows_t, own_stats = center_own(student, sibling)
    near_sums, near_columns, near_stats = partial_sums(
        place, rows_t, own_stats, near, True, "partial_near", [x_far_a]
    )
    near_sums, z_lo_a, z_hi_a = lax.optimization_barrier((near_sums, z_lo_a, z_hi_a))
    far = [x_far_a, x_far_b, z_lo_a, z_lo_b, z_hi_a, z_hi_b, z_far_a, z_far_b]
    near_sums[1:] = [shift_y(near_sums[d], d) for d in (1, 2, 3)]
    far_sums, far_columns, far_stats = partial_sums(
        place, rows_t, own_stats, far, False, "partial_far"
    )
    far_sums[1:] = [shift_y(far_sums[d], d) for d in (1, 2, 3)]

    floats = student.astype(F32)
    diff = floats - teacher.astype(F32)
    lanes = lax.broadcasted_iota(jnp.int32, (8, 128), 1)
    parts = jnp.where(lanes == 1, jnp.sum(diff * diff), F32(0.0))
    parts = parts + swap_z_hi(parts)

    plane, message, local, row_local = combine_y(
        place, near_sums, True, "combine_y_near", [far_sums[0]]
    )
    near_masked, parts, near_means, row_offsets, row_stats = combine_z(
        place, plane, local, row_local, swap_z_hi(message), parts, True, "combine_z_near"
    )
    near_pieces = [near_masked] + [shift_y(near_masked, d) for d in (1, 2, 3)]
    average = row_stats[0]
    spread = jnp.sqrt(row_stats[1] + 0.0001)
    hinge = jnp.where(spread < 1.0, (floats - average) / (spread * (BATCH - 1)), F32(0.0))
    base = lax.optimization_barrier(25.0 * diff / 32.0 - 25.0 * BATCH / 64.0 * hinge)
    var_part = jnp.sum(jnp.maximum(0.0, 1.0 - spread)) / 8
    parts = jnp.where(lanes == 2, var_part, parts)

    plane, message, local = combine_y(place, far_sums, False, "combine_y_far", [near_masked])
    far_masked, _, far_means = combine_z(
        place, plane, local, row_offsets, swap_z_hi(message), parts, False, "combine_z_far"
    )
    far_pieces = [far_masked] + [shift_y(far_masked, d) for d in (1, 2, 3)]

    near_inputs = (near_columns, near_stats, near_means)
    far_inputs = (far_columns, far_stats, far_means)
    grads = grad_part(
        place, near_inputs, near_pieces, None, 0, CHIP_IMAGES, F32, "grad_near", [base]
    )
    parts = sum_parts(place, far_pieces, [grads])
    steps = [parts]
    for axis, bit in (("row", 2), ("row", 4), ("row", 1), ("col", 1)):
        size = 8 if axis == "row" else 16
        parts = parts + lax.ppermute(parts, axis, [(i, i ^ bit) for i in range(size)])
        steps.append(parts)
    totals = parts[0]
    outgoing = grad_part(
        place, far_inputs, far_pieces, grads, IMAGES, IMAGES, BF16, "grad_far_sent", [steps[0]]
    )
    incoming = swap_cores(outgoing)
    kept = grad_part(
        place, far_inputs, far_pieces, grads, 0, IMAGES, F32, "grad_far_kept", [steps[1], outgoing]
    )

    cov_sum, inv_sum, var_sum = totals[0], totals[1], totals[2]
    total_feats = 8 * FEATS
    total_loss = (
        25.0 * inv_sum / (BATCH * total_feats)
        + 25.0 * var_sum / total_feats
        + cov_sum / total_feats
    )
    gradient = base + BATCH / (16.0 * (BATCH - 1)) * (kept + incoming.astype(F32))
    return (gradient, total_loss)


def solution(mesh):
    in_specs = (P("col", "row"), P("col", "row"))
    out_specs = (P("col", "row"), P())
    return jax.shard_map(
        per_device, mesh=mesh, in_specs=in_specs, out_specs=out_specs, check_vma=False
    )
```

time: 470 us -> 142 us (0.30)
  waiting for transfers between devices: 344 us -> 36.5 us
  blocking collectives: 64.6 us -> 0 us
  starting transfers between devices: 0.12 us -> 60.5 us
  Pallas kernels: 0 us -> 24 us
  matrix products: 17 us -> 0 us
  between operations: 16.8 us -> 4.55 us
  other arithmetic: 19 us -> 7.75 us
    all_gather x2 -> x0, waiting for transfers between devices: 222 us -> none  [the longest x1 126 us: per_device(): columns = lax.all_gather(own_piece, 'row', axis=1, tiled=True)]
    reduce_scatter x1 -> x0, waiting for transfers between devices: 122 us -> none  [per_device(): lax.psum_scatter(lax.dot_general(columns, masked_b, (((1,), (1,)), ((), (...]
    psum x1 -> x0, blocking collectives: 64.6 us -> none  [per_device(): lax.psum((cov_part, var_part, inv_part), ('row', 'col'))]
    ppermute x0 -> x35, starting transfers between devices: none -> 60.5 us  [the longest x12 27.1 us: shift_y(): return lax.ppermute(block, 'col', pairs)]
    ppermute x0 -> x35, waiting for transfers between devices: none -> 36.5 us  [the longest x14 22 us: shift_row(): return lax.ppermute(block, 'row', pairs)]
    pallas_call x0 -> x11, Pallas kernels: none -> 24 us  [call(): pl.pallas_call(kernel, out_shape=tuple(outs), in_specs=[SMEM if a.dtype =...]
    reduce_sum x4 -> x2, other arithmetic: 18.9 us -> 1.63 us  [the longest x1 1.01 us: per_device(): parts = jnp.where(lanes == 1, jnp.sum(diff * diff), F32(0.0))]
    dot_general x2 -> x0, matrix products: 17 us -> none  [the longest x1 10.6 us: per_device(): lax.dot_general(centered_b, columns, (((0,), (0,)), ((), ())), preferred_...]
  transfers between devices with their start and end apart: 3 -> 35, of which waited for: 3 -> 10; matrix products, arithmetic and copies ran while one was open for 0% -> 6% of each run, Pallas kernels for 0% -> 15%
where the time goes in v3:
time: 142 us
  starting transfers between devices  60.5 us (43%)
  waiting for transfers between devices  36.5 us (26%)
  Pallas kernels  24 us (17%)
  local copies, waits for them, and re-layouts  8.25 us (6%)
  other arithmetic  7.75 us (5%)
  between operations  4.55 us (3%)
    ppermute x12, starting transfers between devices, shift_y(): return lax.ppermute(block, 'col', pairs)  27.1 us
    pallas_call x11, Pallas kernels, call(): pl.pallas_call(kernel, out_shape=tuple(outs), in_specs=[SMEM if a.dtype =...  24 us
    ppermute x14, waiting for transfers between devices, shift_row(): return lax.ppermute(block, 'row', pairs)  22 us
    ppermute x14, starting transfers between devices, shift_row(): return lax.ppermute(block, 'row', pairs)  16.3 us
    ppermute x4, waiting for transfers between devices, per_device(): lax.ppermute(parts, axis, [(i, i ^ bit) for i in range(size)])  8.05 us
    unnamed x36, local copies, waits for them, and re-layouts  6.62 us
    ppermute x3, starting transfers between devices, swap_z_hi(): return lax.ppermute(block, 'col', [(i, i ^ 8) for i in range(16)])  6.57 us
    ppermute x12, waiting for transfers between devices, shift_y(): return lax.ppermute(block, 'col', pairs)  6.45 us
  transfers between devices with their start and end apart: 35, of which 10 were waited for; matrix products, arithmetic and copies ran while one was open for 6% of the time, Pallas kernels for 15%

profile of v3, /device:TPU:1, one launch (start us, length us, event | category | flops | bytes accessed | tf_op | source)
XLA Modules:
  0.0 141.6 jit_solution(1985158809133697098)
XLA Ops:
  9.0 6.1 %collective-permute-done.1.refs_5_ = bf16[768,256]{1,0:T(8,128)(2,1)S(1)} collective-permute-done((bf16[768,256]{1,0:T(8,128)(2,1)S(1)}, bf16[768,256]{1,0:T(8,128)(2,1)S(1)}, u32[]{:S(2)}, u32[]{:S(2)}) %collective-permute-start.1) | collective-permute-done | bytes 393248 | tf_op jit(solution)/shard_map/ppermute | solution.py:26
  20.6 4.2 %collective-permute-done.4.refs_8_ = bf16[768,256]{1,0:T(8,128)(2,1)} collective-permute-done((bf16[768,256]{1,0:T(8,128)(2,1)S(1)}, bf16[768,256]{1,0:T(8,128)(2,1)}, u32[]{:S(2)}, u32[]{:S(2)}) %collective-permute-start.4) | collective-permute-done | bytes 393248 | tf_op jit(solution)/shard_map/ppermute | solution.py:26
  24.8 2.7 %collective-permute-start.13 = (bf16[768,256]{1,0:T(8,128)(2,1)}, bf16[768,256]{1,0:T(8,128)(2,1)S(1)}, u32[]{:S(2)}, u32[]{:S(2)}) collective-permute-start(bf16[768,256]{1,0:T(8,128)(2,1)} %collective-permute-done.4.refs_8_), channel_id=1, source_target_pairs={{0,96},{16,112},{32,0},{48,16},{64,32},{80,48},{96,64},{112,80},{1... | collective-permute-start | bytes 1179656 | tf_op jit(solution)/shard_map/ppermute | solution.py:26
  27.5 7.0 %collective-permute-done.8.refs_5_ = bf16[768,256]{1,0:T(8,128)(2,1)S(1)} collective-permute-done((bf16[768,256]{1,0:T(8,128)(2,1)}, bf16[768,256]{1,0:T(8,128)(2,1)S(1)}, u32[]{:S(2)}, u32[]{:S(2)}) %collective-permute-start.8) | collective-permute-done | bytes 393248 | tf_op jit(solution)/shard_map/ppermute | solution.py:26
  38.4 4.7 %collective-permute-done.2.refs_6_ = bf16[768,256]{1,0:T(8,128)(2,1)} collective-permute-done((bf16[768,256]{1,0:T(8,128)(2,1)S(1)}, bf16[768,256]{1,0:T(8,128)(2,1)}, u32[]{:S(2)}, u32[]{:S(2)}) %collective-permute-start.2) | collective-permute-done | bytes 393248 | tf_op jit(solution)/shard_map/ppermute | solution.py:26
  45.1 4.6 %partial_near.1 = (f32[144,1024]{1,0:T(8,128)S(1)}, bf16[144,1024]{1,0:T(8,128)(2,1)S(1)}, bf16[144,1024]{1,0:T(8,128)(2,1)S(1)}, bf16[144,1024]{1,0:T(8,128)(2,...) custom-call(s32[4]{0:T(128)S(1)} %pad_add_fusion.refs_0_, ...), custom_call_target="tpu_custom_call" | custom-call | flops 1610612736 | tf_op jit(solution)/shard_map/partial_near/pallas_call | solution.py:51
  52.7 2.6 %collective-permute-start.11 = (bf16[144,1024]{1,0:T(8,128)(2,1)S(1)}, bf16[144,1024]{1,0:T(8,128)(2,1)S(1)}, u32[]{:S(2)}, u32[]{:S(2)}) collective-permute-start(bf16[144,1024]{1,0:T(8,128)(2,1)S(1)} %get-tuple-element.44), channel_id=1, source_target_pairs={{0,4},{1,5},{2,6},{3,7},{4,0},{5,1},{6,2},{7,3},{8,12},{9,13},{10,... | collective-permute-start | bytes 884744 | tf_op jit(solution)/shard_map/ppermute | solution.py:38
  58.1 3.4 %collective-permute-start.19 = (f32[8,128]{1,0:T(8,128)S(1)}, f32[8,128]{1,0:T(8,128)S(1)}, u32[]{:S(2)}, u32[]{:S(2)}) collective-permute-start(f32[8,128]{1,0:T(8,128)S(1)} %iota.11), channel_id=1, source_target_pairs={{0,8},{1,9},{2,10},{3,11},{4,12},{5,13},{6,14},{7,15},{8,0},{9,1},... | collective-permute-start | bytes 12296 | tf_op jit(solution)/shard_map/ppermute | solution.py:42
  61.5 4.4 %partial_far.1 = (f32[144,1024]{1,0:T(8,128)S(1)}, bf16[144,1024]{1,0:T(8,128)(2,1)S(1)}, bf16[144,1024]{1,0:T(8,128)(2,1)S(1)}, bf16[144,1024]{1,0:T(8,128)(2,1...) custom-call(s32[4]{0:T(128)S(1)} %pad_add_fusion.refs_0_, bf16[512,1536]{1,0:T(8,128)(2,1)S(1)} %get-tuple-element.36.refs_1_, ...), custom_call_target="tpu_custom_call" | custom-call | flops 1610612736 | tf_op jit(solution)/shard_map/partial_far/pallas_call | solution.py:51
  66.7 2.9 %collective-permute-start.18 = (bf16[160,1024]{1,0:T(8,128)(2,1)S(1)}, bf16[160,1024]{1,0:T(8,128)(2,1)S(1)}, u32[]{:S(2)}, u32[]{:S(2)}) collective-permute-start(bf16[160,1024]{1,0:T(8,128)(2,1)S(1)} %get-tuple-element.52), channel_id=1, source_target_pairs={{0,8},{1,9},{2,10},{3,11},{4,12},{5,13},{6,14},{7,15},{8,0},{9,1},... | collective-permute-start | bytes 983048 | tf_op jit(solution)/shard_map/ppermute | solution.py:42
  70.1 3.5 %collective-permute-start.20 = (bf16[144,1024]{1,0:T(8,128)(2,1)S(1)}, bf16[144,1024]{1,0:T(8,128)(2,1)S(1)}, u32[]{:S(2)}, u32[]{:S(2)}) collective-permute-start(bf16[144,1024]{1,0:T(8,128)(2,1)S(1)} %get-tuple-element.56), channel_id=1, source_target_pairs={{0,2},{1,3},{2,4},{3,5},{4,6},{5,7},{6,0},{7,1},{8,10},{9,11},{10,... | collective-permute-start | bytes 884744 | tf_op jit(solution)/shard_map/ppermute | solution.py:38
  78.4 2.8 %collective-permute-start.27 = (bf16[128,1024]{1,0:T(8,128)(2,1)S(1)}, bf16[128,1024]{1,0:T(8,128)(2,1)}, u32[]{:S(2)}, u32[]{:S(2)}) collective-permute-start(bf16[128,1024]{1,0:T(8,128)(2,1)S(1)} %get-tuple-element.59.refs_5_.refs_4_), channel_id=1, source_target_pairs={{0,2},{1,3},{2,4},{3,5},{4,6},{5,7},{6,0},{7,1},{8,10},{9,11},{10,... | collective-permute-start | bytes 786440 | tf_op jit(solution)/shard_map/ppermute | solution.py:38
  81.2 3.9 %collective-permute-done.21.refs_3_ = bf16[144,1024]{1,0:T(8,128)(2,1)S(1)} collective-permute-done((bf16[144,1024]{1,0:T(8,128)(2,1)S(1)}, bf16[144,1024]{1,0:T(8,128)(2,1)S(1)}, u32[]{:S(2)}, u32[]{:S(2)}) %collective-permute-start.21) | collective-permute-done | bytes 294944 | tf_op jit(solution)/shard_map/ppermute | solution.py:38
  88.4 3.1 %collective-permute-start.28 = (bf16[128,1024]{1,0:T(8,128)(2,1)S(1)}, bf16[128,1024]{1,0:T(8,128)(2,1)}, u32[]{:S(2)}, u32[]{:S(2)}) collective-permute-start(bf16[128,1024]{1,0:T(8,128)(2,1)S(1)} %get-tuple-element.59.refs_5_.refs_4_), channel_id=1, source_target_pairs={{0,4},{1,5},{2,6},{3,7},{4,0},{5,1},{6,2},{7,3},{8,12},{9,13},{10,... | collective-permute-start | bytes 786440 | tf_op jit(solution)/shard_map/ppermute | solution.py:38
  91.5 2.8 %collective-permute-start.29 = (bf16[128,1024]{1,0:T(8,128)(2,1)S(1)}, bf16[128,1024]{1,0:T(8,128)(2,1)}, u32[]{:S(2)}, u32[]{:S(2)}) collective-permute-start(bf16[128,1024]{1,0:T(8,128)(2,1)S(1)} %get-tuple-element.59.refs_5_.refs_4_), channel_id=1, source_target_pairs={{0,6},{1,7},{2,0},{3,1},{4,2},{5,3},{6,4},{7,5},{8,14},{9,15},{10,... | collective-permute-start | bytes 786440 | tf_op jit(solution)/shard_map/ppermute | solution.py:38
  97.3 2.4 %combine_z_far.1 = (bf16[144,1024]{1,0:T(8,128)(2,1)S(1)}, f32[8,128]{1,0:T(8,128)}, f32[8,1024]{1,0:T(8,128)S(1)}) custom-call(s32[4]{0:T(128)S(1)} %pad_add_fusion.refs_0_, bf16[128,1024]{1,0:T(8,128)(2,1)S(1)} %copy-done.4, f32[8,1024]{1,0:T(8,128)S(1)} %get-tuple-element.61.refs_2_, f32[8,512]{1,0:T(8,128)S(1)} %copy-done.6, ...), custom_call_target="tpu_custom_call" | custom-call | tf_op jit(solution)/shard_map/combine_z_far/pallas_call | solution.py:51
  99.7 4.7 %collective-permute-start.24 = (bf16[144,1024]{1,0:T(8,128)(2,1)S(1)}, bf16[144,1024]{1,0:T(8,128)(2,1)S(1)}, u32[]{:S(2)}, u32[]{:S(2)}) collective-permute-start(bf16[144,1024]{1,0:T(8,128)(2,1)S(1)} %get-tuple-element.66.refs_1_.refs_4_), channel_id=1, source_target_pairs={{0,2},{1,3},{2,4},{3,5},{4,6},{5,7},{6,0},{7,1},{8,10},{9,11},{10,... | collective-permute-start | bytes 884744 | tf_op jit(solution)/shard_map/ppermute | solution.py:38
  104.4 2.4 %collective-permute-start.26 = (bf16[144,1024]{1,0:T(8,128)(2,1)S(1)}, bf16[144,1024]{1,0:T(8,128)(2,1)S(1)}, u32[]{:S(2)}, u32[]{:S(2)}) collective-permute-start(bf16[144,1024]{1,0:T(8,128)(2,1)S(1)} %get-tuple-element.66.refs_1_.refs_4_), channel_id=1, source_target_pairs={{0,6},{1,7},{2,0},{3,1},{4,2},{5,3},{6,4},{7,5},{8,14},{9,15},{10,... | collective-permute-start | bytes 884744 | tf_op jit(solution)/shard_map/ppermute | solution.py:38
  109.2 3.3 %grad_near.1.refs_5_.refs_8_ = f32[1536,512]{1,0:T(8,128)S(1)} custom-call(s32[4]{0:T(128)S(1)} %pad_add_fusion.refs_0_, bf16[1536,1024]{1,0:T(8,128)(2,1)S(1)} %copy-done.2, f32[8,1024]{1,0:T(8,128)S(1)} %get-tuple-element.68.refs_2_, f32[8,1024]{1,0:T(8,128)S(1)} %get-tuple-element.69.refs_3_, bf16[128,1024]{1,0:T(8,128)(2,1)S(1)} %get-tuple-element.59.refs_5_.refs_4_, ...), custom_call_target="tpu_custom_call" | custom-call | tf_op jit(solution)/shard_map/grad_near/pallas_call | solution.py:51
  112.5 2.3 %collective-permute-done.25.refs_3_.refs_6_ = bf16[144,1024]{1,0:T(8,128)(2,1)S(1)} collective-permute-done((bf16[144,1024]{1,0:T(8,128)(2,1)S(1)}, bf16[144,1024]{1,0:T(8,128)(2,1)S(1)}, u32[]{:S(2)}, u32[]{:S(2)}) %collective-permute-start.25) | collective-permute-done | bytes 294944 | tf_op jit(solution)/shard_map/ppermute | solution.py:38
  117.3 4.7 %collective-permute-start.31 = (bf16[768,512]{1,0:T(8,128)(2,1)S(1)}, bf16[768,512]{1,0:T(8,128)(2,1)S(1)}, u32[]{:S(2)}, u32[]{:S(2)}) collective-permute-start(bf16[768,512]{1,0:T(8,128)(2,1)S(1)} %grad_far_sent.1.refs_10_), channel_id=1, source_target_pairs={{0,1},{1,0},{2,3},{3,2},{4,5},{5,4},{6,7},{7,6},{8,9},{9,8},{10,11... | collective-permute-start | bytes 2359304 | tf_op jit(solution)/shard_map/ppermute | solution.py:30
  125.0 3.4 %collective-permute-done.32 = f32[8,128]{1,0:T(8,128)S(1)} collective-permute-done((f32[8,128]{1,0:T(8,128)S(1)}, f32[8,128]{1,0:T(8,128)S(1)}, u32[]{:S(2)}, u32[]{:S(2)}) %collective-permute-start.32) | collective-permute-done | bytes 4128 | tf_op jit(solution)/shard_map/ppermute | solution.py:439
  128.5 2.5 %collective-permute-done.33 = f32[8,128]{1,0:T(8,128)S(1)} collective-permute-done((f32[8,128]{1,0:T(8,128)S(1)}, f32[8,128]{1,0:T(8,128)S(1)}, u32[]{:S(2)}, u32[]{:S(2)}) %collective-permute-start.33) | collective-permute-done | bytes 4128 | tf_op jit(solution)/shard_map/ppermute | solution.py:439
  130.9 3.5 %collective-permute-start.34 = (f32[8,128]{1,0:T(8,128)S(1)}, f32[8,128]{1,0:T(8,128)S(1)}, u32[]{:S(2)}, u32[]{:S(2)}) collective-permute-start(f32[8,128]{1,0:T(8,128)S(1)} %add.62), channel_id=1, source_target_pairs={{0,1},{1,0},{2,3},{3,2},{4,5},{5,4},{6,7},{7,6},{8,9},{9,8},{10,11... | collective-permute-start | bytes 12296 | tf_op jit(solution)/shard_map/ppermute | solution.py:439
  (112 shorter events, 49.1 us)
Async XLA Ops:
  3.2 12.0 %collective-permute-start.1 = (bf16[768,256]{1,0:T(8,128)(2,1)S(1)}, bf16[768,256]{1,0:T(8,128)(2,1)S(1)}, u32[]{:S(2)}, u32[]{:S(2)}) collective-permute-start(bf16[768,256]{1,0:T(8,128)(2,1)S(1)} %constant_dynamic-slice_fusion.1.refs_3_), channel_id=1, source_target_pairs={{0,32},{16,48},{32,64},{48,80},{64,96},{80,112},{96,0},{112,16},{1... | collective-permute-start | bytes 1179656 | tf_op jit(solution)/shard_map/ppermute | solution.py:26
  4.6 11.5 %collective-permute-start.5 = (bf16[768,256]{1,0:T(8,128)(2,1)S(1)}, bf16[768,256]{1,0:T(8,128)(2,1)}, u32[]{:S(2)}, u32[]{:S(2)}) collective-permute-start(bf16[768,256]{1,0:T(8,128)(2,1)S(1)} %constant_dynamic-slice_fusion.1.refs_3_), channel_id=1, source_target_pairs={{0,16},{16,0},{32,48},{48,32},{64,80},{80,64},{96,112},{112,96},{1... | collective-permute-start | bytes 1179656 | tf_op jit(solution)/shard_map/ppermute | solution.py:26
  6.2 12.7 %collective-permute-start.3 = (bf16[768,256]{1,0:T(8,128)(2,1)S(1)}, bf16[768,256]{1,0:T(8,128)(2,1)S(1)}, u32[]{:S(2)}, u32[]{:S(2)}) collective-permute-start(bf16[768,256]{1,0:T(8,128)(2,1)S(1)} %constant_dynamic-slice_fusion.1.refs_3_), channel_id=1, source_target_pairs={{0,96},{16,112},{32,0},{48,16},{64,32},{80,48},{96,64},{112,80},{1... | collective-permute-start | bytes 1179656 | tf_op jit(solution)/shard_map/ppermute | solution.py:26
  7.7 17.1 %collective-permute-start.4 = (bf16[768,256]{1,0:T(8,128)(2,1)S(1)}, bf16[768,256]{1,0:T(8,128)(2,1)}, u32[]{:S(2)}, u32[]{:S(2)}) collective-permute-start(bf16[768,256]{1,0:T(8,128)(2,1)S(1)} %constant_dynamic-slice_fusion.refs_4_), channel_id=1, source_target_pairs={{0,96},{16,112},{32,0},{48,16},{64,32},{80,48},{96,64},{112,80},{1... | collective-permute-start | bytes 1179656 | tf_op jit(solution)/shard_map/ppermute | solution.py:26
  15.1 12.3 %collective-permute-start.7 = (bf16[768,256]{1,0:T(8,128)(2,1)S(1)}, bf16[768,256]{1,0:T(8,128)(2,1)S(1)}, u32[]{:S(2)}, u32[]{:S(2)}) collective-permute-start(bf16[768,256]{1,0:T(8,128)(2,1)S(1)} %collective-permute-done.1.refs_5_), channel_id=1, source_target_pairs={{0,32},{16,48},{32,64},{48,80},{64,96},{80,112},{96,0},{112,16},{1... | collective-permute-start | bytes 1179656 | tf_op jit(solution)/shard_map/ppermute | solution.py:26
  16.1 18.5 %collective-permute-start.8 = (bf16[768,256]{1,0:T(8,128)(2,1)}, bf16[768,256]{1,0:T(8,128)(2,1)S(1)}, u32[]{:S(2)}, u32[]{:S(2)}) collective-permute-start(bf16[768,256]{1,0:T(8,128)(2,1)} %collective-permute-done.5.refs_9_), channel_id=1, source_target_pairs={{0,32},{16,48},{32,64},{48,80},{64,96},{80,112},{96,0},{112,16},{1... | collective-permute-start | bytes 1179656 | tf_op jit(solution)/shard_map/ppermute | solution.py:26
  17.3 19.7 %collective-permute-start.6 = (bf16[768,256]{1,0:T(8,128)(2,1)S(1)}, bf16[768,256]{1,0:T(8,128)(2,1)}, u32[]{:S(2)}, u32[]{:S(2)}) collective-permute-start(bf16[768,256]{1,0:T(8,128)(2,1)S(1)} %constant_dynamic-slice_fusion.refs_4_), channel_id=1, source_target_pairs={{0,16},{16,0},{32,48},{48,32},{64,80},{80,64},{96,112},{112,96},{1... | collective-permute-start | bytes 1179656 | tf_op jit(solution)/shard_map/ppermute | solution.py:26
  19.7 23.4 %collective-permute-start.2 = (bf16[768,256]{1,0:T(8,128)(2,1)S(1)}, bf16[768,256]{1,0:T(8,128)(2,1)}, u32[]{:S(2)}, u32[]{:S(2)}) collective-permute-start(bf16[768,256]{1,0:T(8,128)(2,1)S(1)} %constant_dynamic-slice_fusion.refs_4_), channel_id=1, source_target_pairs={{0,32},{16,48},{32,64},{48,80},{64,96},{80,112},{96,0},{112,16},{1... | collective-permute-start | bytes 1179656 | tf_op jit(solution)/shard_map/ppermute | solution.py:26
  24.8 18.7 %collective-permute-start.13 = (bf16[768,256]{1,0:T(8,128)(2,1)}, bf16[768,256]{1,0:T(8,128)(2,1)S(1)}, u32[]{:S(2)}, u32[]{:S(2)}) collective-permute-start(bf16[768,256]{1,0:T(8,128)(2,1)} %collective-permute-done.4.refs_8_), channel_id=1, source_target_pairs={{0,96},{16,112},{32,0},{48,16},{64,32},{80,48},{96,64},{112,80},{1... | collective-permute-start | bytes 1179656 | tf_op jit(solution)/shard_map/ppermute | solution.py:26
  27.4 23.9 %collective-permute-start.9 = (bf16[768,256]{1,0:T(8,128)(2,1)}, bf16[768,256]{1,0:T(8,128)(2,1)}, u32[]{:S(2)}, u32[]{:S(2)}) collective-permute-start(bf16[768,256]{1,0:T(8,128)(2,1)} %collective-permute-done.5.refs_9_), channel_id=1, source_target_pairs={{0,96},{16,112},{32,0},{48,16},{64,32},{80,48},{96,64},{112,80},{1... | collective-permute-start | bytes 1179656 | tf_op jit(solution)/shard_map/ppermute | solution.py:26
  35.3 17.4 %collective-permute-start.16 = (bf16[768,256]{1,0:T(8,128)(2,1)S(1)}, bf16[768,256]{1,0:T(8,128)(2,1)}, u32[]{:S(2)}, u32[]{:S(2)}) collective-permute-start(bf16[768,256]{1,0:T(8,128)(2,1)S(1)} %collective-permute-done.7.refs_11_.refs_3_), channel_id=1, source_target_pairs={{0,16},{16,0},{32,48},{48,32},{64,80},{80,64},{96,112},{112,96},{1... | collective-permute-start | bytes 1179656 | tf_op jit(solution)/shard_map/ppermute | solution.py:26
  37.0 18.3 %collective-permute-start.14 = (bf16[768,256]{1,0:T(8,128)(2,1)}, bf16[768,256]{1,0:T(8,128)(2,1)}, u32[]{:S(2)}, u32[]{:S(2)}) collective-permute-start(bf16[768,256]{1,0:T(8,128)(2,1)} %collective-permute-done.6.refs_10_), channel_id=1, source_target_pairs={{0,32},{16,48},{32,64},{48,80},{64,96},{80,112},{96,0},{112,16},{1... | collective-permute-start | bytes 1179656 | tf_op jit(solution)/shard_map/ppermute | solution.py:26
  43.1 15.0 %collective-permute-start.15 = (bf16[768,256]{1,0:T(8,128)(2,1)}, bf16[768,256]{1,0:T(8,128)(2,1)S(1)}, u32[]{:S(2)}, u32[]{:S(2)}) collective-permute-start(bf16[768,256]{1,0:T(8,128)(2,1)} %collective-permute-done.6.refs_10_), channel_id=1, source_target_pairs={{0,96},{16,112},{32,0},{48,16},{64,32},{80,48},{96,64},{112,80},{1... | collective-permute-start | bytes 1179656 | tf_op jit(solution)/shard_map/ppermute | solution.py:26
  43.4 18.0 %collective-permute-start.17 = (bf16[768,256]{1,0:T(8,128)(2,1)S(1)}, bf16[768,256]{1,0:T(8,128)(2,1)S(1)}, u32[]{:S(2)}, u32[]{:S(2)}) collective-permute-start(bf16[768,256]{1,0:T(8,128)(2,1)S(1)} %collective-permute-done.13.refs_4_), channel_id=1, source_target_pairs={{0,16},{16,0},{32,48},{48,32},{64,80},{80,64},{96,112},{112,96},{1... | collective-permute-start | bytes 1179656 | tf_op jit(solution)/shard_map/ppermute | solution.py:26
  51.3 14.6 %collective-permute-start.10 = (bf16[144,1024]{1,0:T(8,128)(2,1)S(1)}, bf16[144,1024]{1,0:T(8,128)(2,1)S(1)}, u32[]{:S(2)}, u32[]{:S(2)}) collective-permute-start(bf16[144,1024]{1,0:T(8,128)(2,1)S(1)} %get-tuple-element.43), channel_id=1, source_target_pairs={{0,2},{1,3},{2,4},{3,5},{4,6},{5,7},{6,0},{7,1},{8,10},{9,11},{10,... | collective-permute-start | bytes 884744 | tf_op jit(solution)/shard_map/ppermute | solution.py:38
  52.7 13.2 %collective-permute-start.11 = (bf16[144,1024]{1,0:T(8,128)(2,1)S(1)}, bf16[144,1024]{1,0:T(8,128)(2,1)S(1)}, u32[]{:S(2)}, u32[]{:S(2)}) collective-permute-start(bf16[144,1024]{1,0:T(8,128)(2,1)S(1)} %get-tuple-element.44), channel_id=1, source_target_pairs={{0,4},{1,5},{2,6},{3,7},{4,0},{5,1},{6,2},{7,3},{8,12},{9,13},{10,... | collective-permute-start | bytes 884744 | tf_op jit(solution)/shard_map/ppermute | solution.py:38
  58.1 12.1 %collective-permute-start.19 = (f32[8,128]{1,0:T(8,128)S(1)}, f32[8,128]{1,0:T(8,128)S(1)}, u32[]{:S(2)}, u32[]{:S(2)}) collective-permute-start(f32[8,128]{1,0:T(8,128)S(1)} %iota.11), channel_id=1, source_target_pairs={{0,8},{1,9},{2,10},{3,11},{4,12},{5,13},{6,14},{7,15},{8,0},{9,1},... | collective-permute-start | bytes 12296 | tf_op jit(solution)/shard_map/ppermute | solution.py:42
  70.1 11.1 %collective-permute-start.20 = (bf16[144,1024]{1,0:T(8,128)(2,1)S(1)}, bf16[144,1024]{1,0:T(8,128)(2,1)S(1)}, u32[]{:S(2)}, u32[]{:S(2)}) collective-permute-start(bf16[144,1024]{1,0:T(8,128)(2,1)S(1)} %get-tuple-element.56), channel_id=1, source_target_pairs={{0,2},{1,3},{2,4},{3,5},{4,6},{5,7},{6,0},{7,1},{8,10},{9,11},{10,... | collective-permute-start | bytes 884744 | tf_op jit(solution)/shard_map/ppermute | solution.py:38
  73.7 11.5 %collective-permute-start.21 = (bf16[144,1024]{1,0:T(8,128)(2,1)S(1)}, bf16[144,1024]{1,0:T(8,128)(2,1)S(1)}, u32[]{:S(2)}, u32[]{:S(2)}) collective-permute-start(bf16[144,1024]{1,0:T(8,128)(2,1)S(1)} %get-tuple-element.57), channel_id=1, source_target_pairs={{0,4},{1,5},{2,6},{3,7},{4,0},{5,1},{6,2},{7,3},{8,12},{9,13},{10,... | collective-permute-start | bytes 884744 | tf_op jit(solution)/shard_map/ppermute | solution.py:38
  78.4 26.1 %collective-permute-start.27 = (bf16[128,1024]{1,0:T(8,128)(2,1)S(1)}, bf16[128,1024]{1,0:T(8,128)(2,1)}, u32[]{:S(2)}, u32[]{:S(2)}) collective-permute-start(bf16[128,1024]{1,0:T(8,128)(2,1)S(1)} %get-tuple-element.59.refs_5_.refs_4_), channel_id=1, source_target_pairs={{0,2},{1,3},{2,4},{3,5},{4,6},{5,7},{6,0},{7,1},{8,10},{9,11},{10,... | collective-permute-start | bytes 786440 | tf_op jit(solution)/shard_map/ppermute | solution.py:38
  88.4 20.5 %collective-permute-start.28 = (bf16[128,1024]{1,0:T(8,128)(2,1)S(1)}, bf16[128,1024]{1,0:T(8,128)(2,1)}, u32[]{:S(2)}, u32[]{:S(2)}) collective-permute-start(bf16[128,1024]{1,0:T(8,128)(2,1)S(1)} %get-tuple-element.59.refs_5_.refs_4_), channel_id=1, source_target_pairs={{0,4},{1,5},{2,6},{3,7},{4,0},{5,1},{6,2},{7,3},{8,12},{9,13},{10,... | collective-permute-start | bytes 786440 | tf_op jit(solution)/shard_map/ppermute | solution.py:38
  91.5 17.3 %collective-permute-start.29 = (bf16[128,1024]{1,0:T(8,128)(2,1)S(1)}, bf16[128,1024]{1,0:T(8,128)(2,1)}, u32[]{:S(2)}, u32[]{:S(2)}) collective-permute-start(bf16[128,1024]{1,0:T(8,128)(2,1)S(1)} %get-tuple-element.59.refs_5_.refs_4_), channel_id=1, source_target_pairs={{0,6},{1,7},{2,0},{3,1},{4,2},{5,3},{6,4},{7,5},{8,14},{9,15},{10,... | collective-permute-start | bytes 786440 | tf_op jit(solution)/shard_map/ppermute | solution.py:38
  99.7 12.8 %collective-permute-start.24 = (bf16[144,1024]{1,0:T(8,128)(2,1)S(1)}, bf16[144,1024]{1,0:T(8,128)(2,1)S(1)}, u32[]{:S(2)}, u32[]{:S(2)}) collective-permute-start(bf16[144,1024]{1,0:T(8,128)(2,1)S(1)} %get-tuple-element.66.refs_1_.refs_4_), channel_id=1, source_target_pairs={{0,2},{1,3},{2,4},{3,5},{4,6},{5,7},{6,0},{7,1},{8,10},{9,11},{10,... | collective-permute-start | bytes 884744 | tf_op jit(solution)/shard_map/ppermute | solution.py:38
  117.3 21.5 %collective-permute-start.31 = (bf16[768,512]{1,0:T(8,128)(2,1)S(1)}, bf16[768,512]{1,0:T(8,128)(2,1)S(1)}, u32[]{:S(2)}, u32[]{:S(2)}) collective-permute-start(bf16[768,512]{1,0:T(8,128)(2,1)S(1)} %grad_far_sent.1.refs_10_), channel_id=1, source_target_pairs={{0,1},{1,0},{2,3},{3,2},{4,5},{5,4},{6,7},{7,6},{8,9},{9,8},{10,11... | collective-permute-start | bytes 2359304 | tf_op jit(solution)/shard_map/ppermute | solution.py:30
  (29 other events, 223.1 us)

commit v4 on v3

--- a/solution.py
+++ b/solution.py
@@ -14,6 +14,7 @@
 CHIP_IMAGES = 2 * IMAGES
 HALF = FEATS // 2
 STAT_ROWS = 16
+GRAD_SCALE = BATCH / (16.0 * (BATCH - 1))
 
 QUARTER = FEATS // 4
 VMEM = pl.BlockSpec(memory_space=pltpu.VMEM)
@@ -24,6 +25,14 @@
 def shift_row(block, dx, dz):
     pairs = [(2 * x + z, 2 * ((x + dx) % 4) + (z + dz) % 2) for x in range(4) for z in range(2)]
     return lax.ppermute(block, "row", pairs)
+
+
+def flip(block, z_lo, core):
+    pairs = []
+    for row in range(8):
+        for col in range(16):
+            pairs.append((16 * row + col, 16 * (row ^ z_lo) + (col ^ core)))
+    return lax.ppermute(block, ("row", "col"), pairs)
 
 
 def swap_cores(block):
@@ -54,7 +63,7 @@
         in_specs=[SMEM if a.dtype == jnp.int32 else VMEM for a in ins] + [ANY] * waits,
         out_specs=tuple(VMEM for _ in outs),
         scratch_shapes=scratch,
-        compiler_params=pltpu.CompilerParams(vmem_limit_bytes=26 * 2**20),
+        compiler_params=pltpu.CompilerParams(vmem_limit_bytes=16 * 2**20),
         cost_estimate=pl.CostEstimate(flops=flops, bytes_accessed=0, transcendentals=0),
         name=name,
     )(*ins, *after)
@@ -136,26 +145,62 @@
     return jnp.concatenate([line for line in lines if line.shape[0]], axis=0)
 
 
-def rows_kernel(own, sibling, rows_t, row_stats, rows):
+def rows_kernel(own, sibling, teacher, rows_t, row_stats, parts, rows):
     row_mean = (column_sum(own) + column_sum(sibling)) / CHIP_IMAGES
     squares = center_rows(rows, 0, own, row_mean) + center_rows(rows, IMAGES, sibling, row_mean)
     for at in range(0, FEATS, 128):
         rows_t[at:at + 128, :] = rows[:, at:at + 128].T
     row_stats[...] = jnp.concatenate([row_mean, squares, jnp.zeros((6, FEATS), F32)], axis=0)
 
-
-def center_own(own, sibling):
+    def body(i, total):
+        at = pl.ds(pl.multiple_of(i * 128, 128), 128)
+        diff = own[at, :].astype(F32) - teacher[at, :].astype(F32)
+        return total + jnp.sum((diff * diff).reshape(16, 8, FEATS), axis=0)
+
+    total = lax.fori_loop(0, IMAGES // 128, body, jnp.zeros((8, FEATS), F32))
+    lanes = lax.broadcasted_iota(jnp.int32, parts.shape, 1)
+    parts[...] = jnp.where(lanes == 1, jnp.sum(total, keepdims=True), 0.0)
+
+
+def center_own(own, sibling, teacher, after):
     return call(
         rows_kernel,
-        [shape((FEATS, CHIP_IMAGES), BF16), shape((8, FEATS), F32)],
-        [own, sibling],
+        [shape((FEATS, CHIP_IMAGES), BF16), shape((8, FEATS), F32), shape((8, 128), F32)],
+        [own, sibling, teacher],
         [pltpu.VMEM((CHIP_IMAGES, FEATS), BF16)],
         "center_own",
-    )
-
-
-def products(rows_t, columns, at, step):
-    return jnp.dot(rows_t[...], columns[:, at:at + step], preferred_element_type=F32)
+        after,
+    )
+
+
+def join_kernel(first, second, out):
+    out[0:IMAGES, :] = first[...]
+    out[IMAGES:CHIP_IMAGES, :] = second[...]
+
+
+def join(first, second, after=()):
+    return call(
+        join_kernel, [shape((CHIP_IMAGES, HALF), BF16)], [first, second], [], "join", after
+    )[0]
+
+
+def base_kernel(student, teacher, row_stats, out):
+    mean, spread = row_stats[0:1, :], row_stats[1:2, :]
+    scale = jnp.where(spread < 1.0, 25.0 * BATCH / 64.0 / (spread * (BATCH - 1)), 0.0)
+
+    def body(i, carry):
+        at = pl.ds(pl.multiple_of(i * 64, 64), 64)
+        value = student[at, :].astype(F32)
+        diff = value - teacher[at, :].astype(F32)
+        out[at, :] = (25.0 / 32.0) * diff - scale * (value - mean)
+        return carry
+
+    lax.fori_loop(0, IMAGES // 64, body, 0)
+
+
+def base_part(student, teacher, row_stats, after):
+    ins = [student, teacher, row_stats]
+    return call(base_kernel, [shape((IMAGES, FEATS), F32)], ins, [], "base", after)[0]
 
 
 def partial_kernel(places, width, count, with_rows, *refs):
@@ -190,7 +235,7 @@
         [pltpu.VMEM((FEATS, width), F32)],
         name,
         after,
-        flops=2 * CHIP_IMAGES * FEATS * width,
+        flops=40 * CHIP_IMAGES * FEATS * width,
     )
     return pieces, columns, stats
 
@@ -214,7 +259,9 @@
     return stats[first:first + 1] + stats[first + 1:first + 2] + stats[first + 2:first + 3]
 
 
-def combine_y_kernel(with_rows, place, own, one, two, three_on, plane, message, local, *row_local):
+def combine_y_kernel(
+    with_rows, place, parts, own, one, two, three_on, plane, message, local, *row_local
+):
     width = own.shape[1]
     columns = jnp.zeros((4, width), F32)
     rows = jnp.zeros((4, FEATS), F32)
@@ -243,18 +290,19 @@
     if with_rows:
         row_lines, row_local[0][0:4, :] = rounded(rows)
         square_lines, row_local[0][4:5, :] = rounded(squares)
-        lines = lines + padded(row_lines + square_lines, width)
+        part_lines, _ = rounded(parts[0:1, :])
+        lines = lines + padded(row_lines + square_lines, width) + padded(part_lines, width)
     block = filled(lines, width)
     message[QUARTER:QUARTER + block.shape[0], :] = block.astype(BF16)
 
 
-def combine_y(place, pieces, with_rows, name, after):
+def combine_y(place, parts, pieces, with_rows, name, after=()):
     width = pieces[0].shape[1]
     rows = QUARTER + (2 if with_rows else 1) * STAT_ROWS
     outs = [shape((QUARTER, width), BF16), shape((rows, width), BF16), shape((8, width), F32)]
     outs += [shape((8, FEATS), F32)] if with_rows else []
     return call(
-        functools.partial(combine_y_kernel, with_rows), outs, [place] + pieces, [], name, after
+        functools.partial(combine_y_kernel, with_rows), outs, [place, parts] + pieces, [], name, after
     )
 
 
@@ -273,6 +321,7 @@
     row_offsets = rows
     if with_rows:
         row_offsets, row_stats = more
+        other_parts = three(stats[:, 0:128], 27)
         stats = stats[:, 0:FEATS]
         theirs = stats[12:16] + stats[16:20] + stats[20:24]
         row_off, row_mean = spread_out(all_chips(place, rows[0:4, :], theirs))
@@ -280,7 +329,8 @@
         squares = squares + CHIP_IMAGES * jnp.sum(row_off * row_off, axis=0, keepdims=True)
         variance = squares / (BATCH - 1)
         row_offsets[...] = row_off
-        row_stats[...] = jnp.concatenate([row_mean, variance, jnp.zeros((6, FEATS), F32)], axis=0)
+        spread = jnp.sqrt(variance + 0.0001)
+        row_stats[...] = jnp.concatenate([row_mean, spread, jnp.zeros((6, FEATS), F32)], axis=0)
     block = pl.multiple_of(place[2] * QUARTER, QUARTER)
     term = mean_term(row_offsets[:, pl.ds(block, QUARTER)], col_off)
     covar = plane[...].astype(F32) + received[0:QUARTER, :].astype(F32)
@@ -291,7 +341,11 @@
         on_diagonal = (col_ids < HALF) & (row_ids == col_ids + place[1] * HALF)
         covar = jnp.where(on_diagonal, F32(0.0), covar)
     lanes = lax.broadcasted_iota(jnp.int32, part.shape, 1)
-    part[...] = parts[...] + jnp.where(lanes == 0, jnp.sum(covar * covar, keepdims=True), 0.0)
+    found = jnp.where(lanes == 0, jnp.sum(covar * covar, keepdims=True), 0.0)
+    if with_rows:
+        var_part = jnp.sum(jnp.maximum(0.0, 1.0 - spread), keepdims=True) / 8
+        found = found + jnp.where(lanes == 2, var_part, 0.0) + other_parts
+    part[...] = parts[...] + found
     masked[0:QUARTER, :] = covar.astype(BF16)
     if not with_rows:
         block = filled(padded(split3(part[0:1, :]), covar.shape[1]), covar.shape[1])
@@ -321,6 +375,30 @@
     )[0]
 
 
+def x_kernel(place, own, one, two, three_on, out):
+    total = jnp.zeros((8, 128), F32)
+    for x in range(4):
+        block = own[...]
+        for d, other in ((1, one), (2, two), (3, three_on)):
+            block = jnp.where((place[4] + 4 - d) % 4 == x, other[...], block)
+        total = total + block
+    out[...] = total
+
+
+def loss_kernel(own, other_z, other_core, other_both, out):
+    total = (own[...] + other_z[...]) + (other_core[...] + other_both[...])
+    loss = total[:, 0:1] + 25.0 * (total[:, 1:2] / BATCH + total[:, 2:3])
+    out[...] = jnp.broadcast_to(loss / (8 * FEATS), out.shape)
+
+
+def sum_x(place, blocks):
+    return call(x_kernel, [shape((8, 128), F32)], [place] + blocks, [], "sum_x")[0]
+
+
+def loss_of(blocks):
+    return call(loss_kernel, [shape((8, 128), F32)], blocks, [], "loss")[0]
+
+
 def shift_term(stats, means, masked):
     lines = filled(split3(stats[0:1, :] - means[0:1, :]), stats.shape[1]).astype(BF16)
     rows = lax.dot_general(
@@ -336,7 +414,7 @@
 
 
 def grad_kernel(
-    first, rows, add, place, columns, stats, means, own, one, two, three_on, *rest
+    first, rows, add, with_base, place, columns, stats, means, own, one, two, three_on, *rest
 ):
     out, masked = rest[-2:]
     for d, piece in enumerate((own, one, two, three_on)):
@@ -347,14 +425,19 @@
         product = times_masked(columns, at, masked) + shift
         if add:
             product = product + rest[0][at:at + 256, :]
+        if with_base:
+            product = GRAD_SCALE * product + rest[1][at:at + 256, :]
         out[at - first:at - first + 256, :] = product.astype(out.dtype)
 
 
-def grad_part(place, inputs, pieces, previous, first, rows, dtype, name, after=()):
+def grad_part(place, inputs, pieces, previous, first, rows, dtype, name, after=(), base=None):
     columns, stats, means = inputs
-    ins = [place, columns, stats, means] + pieces + ([] if previous is None else [previous])
+    ins = [place, columns, stats, means] + pieces
+    ins += [a for a in (previous, base) if a is not None]
     return call(
-        functools.partial(grad_kernel, first, rows, previous is not None),
+        functools.partial(
+            grad_kernel, first, rows, previous is not None, base is not None
+        ),
         [shape((rows, FEATS), dtype)],
         ins,
         [pltpu.VMEM((FEATS, columns.shape[1]), BF16)],
@@ -368,94 +451,74 @@
     col_index = lax.axis_index("col")
     core = col_index % 2
     chip = col_index // 2
-    place = jnp.stack([chip, core, chip % 4, chip // 4]).astype(jnp.int32)
+    place = jnp.stack([chip, core, chip % 4, chip // 4, row_index // 2]).astype(jnp.int32)
 
     sibling = swap_cores(student)
     own_a = lax.dynamic_slice_in_dim(student, core * HALF, HALF, 1)
     x_lo_a = shift_row(own_a, 1, 0)
     x_hi_a = shift_row(own_a, -1, 0)
-    z_own_a = shift_row(own_a, 0, 1)
     own_b = lax.dynamic_slice_in_dim(sibling, core * HALF, HALF, 1)
     x_lo_b = shift_row(own_b, 1, 0)
     x_hi_b = shift_row(own_b, -1, 0)
+    z_own_a = shift_row(own_a, 0, 1)
     z_own_b = shift_row(own_b, 0, 1)
+    rows_t, own_stats, parts = center_own(student, sibling, teacher, [x_lo_a])
+    x_lo_a, x_lo_b = lax.optimization_barrier((x_lo_a, x_lo_b))
     x_far_a = shift_row(x_lo_a, 1, 0)
     x_far_b = shift_row(x_hi_b, -1, 0)
-    z_lo_a = shift_row(z_own_a, 1, 0)
-    z_hi_a = shift_row(z_own_a, -1, 0)
-    z_lo_b = shift_row(z_own_b, 1, 0)
-    z_hi_b = shift_row(z_own_b, -1, 0)
-    z_far_a = shift_row(x_far_a, 0, 1)
-    z_far_b = shift_row(x_far_b, 0, 1)
     near = [own_a, own_b, x_lo_a, x_lo_b, x_hi_a, x_hi_b, z_own_a, z_own_b]
 
-    rows_t, own_stats = center_own(student, sibling)
     near_sums, near_columns, near_stats = partial_sums(
-        place, rows_t, own_stats, near, True, "partial_near", [x_far_a]
-    )
-    near_sums, z_lo_a, z_hi_a = lax.optimization_barrier((near_sums, z_lo_a, z_hi_a))
-    far = [x_far_a, x_far_b, z_lo_a, z_lo_b, z_hi_a, z_hi_b, z_far_a, z_far_b]
+        place, rows_t, own_stats, near, True, "partial_near"
+    )
+    z_own = join(z_own_a, z_own_b, [near_stats])
+    z_lo = shift_row(z_own, 1, 0)
+    z_hi = shift_row(z_own, -1, 0)
+    x_far = join(x_far_a, x_far_b, [z_own])
+    z_far = shift_row(x_far, 0, 1)
+    far = [x_far, z_lo, z_hi, z_far]
     near_sums[1:] = [shift_y(near_sums[d], d) for d in (1, 2, 3)]
     far_sums, far_columns, far_stats = partial_sums(
         place, rows_t, own_stats, far, False, "partial_far"
     )
     far_sums[1:] = [shift_y(far_sums[d], d) for d in (1, 2, 3)]
 
-    floats = student.astype(F32)
-    diff = floats - teacher.astype(F32)
-    lanes = lax.broadcasted_iota(jnp.int32, (8, 128), 1)
-    parts = jnp.where(lanes == 1, jnp.sum(diff * diff), F32(0.0))
-    parts = parts + swap_z_hi(parts)
-
     plane, message, local, row_local = combine_y(
-        place, near_sums, True, "combine_y_near", [far_sums[0]]
+        place, parts, near_sums, True, "combine_y_near", [far_sums[0]]
+    )
+    far_plane, far_message, far_local = combine_y(
+        place, parts, far_sums, False, "combine_y_far", [plane]
     )
     near_masked, parts, near_means, row_offsets, row_stats = combine_z(
-        place, plane, local, row_local, swap_z_hi(message), parts, True, "combine_z_near"
+        place, plane, local, row_local, swap_z_hi(message), parts, True,
+        "combine_z_near",
+        [far_plane],
     )
     near_pieces = [near_masked] + [shift_y(near_masked, d) for d in (1, 2, 3)]
-    average = row_stats[0]
-    spread = jnp.sqrt(row_stats[1] + 0.0001)
-    hinge = jnp.where(spread < 1.0, (floats - average) / (spread * (BATCH - 1)), F32(0.0))
-    base = lax.optimization_barrier(25.0 * diff / 32.0 - 25.0 * BATCH / 64.0 * hinge)
-    var_part = jnp.sum(jnp.maximum(0.0, 1.0 - spread)) / 8
-    parts = jnp.where(lanes == 2, var_part, parts)
-
-    plane, message, local = combine_y(place, far_sums, False, "combine_y_far", [near_masked])
     far_masked, _, far_means = combine_z(
-        place, plane, local, row_offsets, swap_z_hi(message), parts, False, "combine_z_far"
+        place, far_plane, far_local, row_offsets, swap_z_hi(far_message), parts, False,
+        "combine_z_far", near_pieces[1:],
     )
     far_pieces = [far_masked] + [shift_y(far_masked, d) for d in (1, 2, 3)]
 
+    base = base_part(student, teacher, row_stats, [far_masked])
     near_inputs = (near_columns, near_stats, near_means)
     far_inputs = (far_columns, far_stats, far_means)
     grads = grad_part(
         place, near_inputs, near_pieces, None, 0, CHIP_IMAGES, F32, "grad_near", [base]
     )
     parts = sum_parts(place, far_pieces, [grads])
-    steps = [parts]
-    for axis, bit in (("row", 2), ("row", 4), ("row", 1), ("col", 1)):
-        size = 8 if axis == "row" else 16
-        parts = parts + lax.ppermute(parts, axis, [(i, i ^ bit) for i in range(size)])
-        steps.append(parts)
-    totals = parts[0]
     outgoing = grad_part(
-        place, far_inputs, far_pieces, grads, IMAGES, IMAGES, BF16, "grad_far_sent", [steps[0]]
+        place, far_inputs, far_pieces, grads, IMAGES, IMAGES, BF16, "grad_far_sent", [parts]
     )
     incoming = swap_cores(outgoing)
+    row_parts = sum_x(place, [parts] + [shift_row(parts, dx, 0) for dx in (1, 2, 3)])
     kept = grad_part(
-        place, far_inputs, far_pieces, grads, 0, IMAGES, F32, "grad_far_kept", [steps[1], outgoing]
-    )
-
-    cov_sum, inv_sum, var_sum = totals[0], totals[1], totals[2]
-    total_feats = 8 * FEATS
-    total_loss = (
-        25.0 * inv_sum / (BATCH * total_feats)
-        + 25.0 * var_sum / total_feats
-        + cov_sum / total_feats
-    )
-    gradient = base + BATCH / (16.0 * (BATCH - 1)) * (kept + incoming.astype(F32))
-    return (gradient, total_loss)
+        place, far_inputs, far_pieces, grads, 0, IMAGES, F32, "grad_far_kept",
+        [row_parts, outgoing], base,
+    )
+    total_loss = loss_of([row_parts] + [flip(row_parts, *way) for way in ((1, 0), (0, 1), (1, 1))])
+    return (kept + GRAD_SCALE * incoming.astype(F32), total_loss[0, 0])
 
 
 def solution(mesh):

time: 142 us -> 133 us (0.937)
  waiting for transfers between devices: 36.5 us -> 55.8 us
  starting transfers between devices: 60.5 us -> 47.3 us
  other arithmetic: 7.75 us -> 1.41 us
  local copies, waits for them, and re-layouts: 8.25 us -> 3.4 us
  between operations: 4.55 us -> 0.82 us
    ppermute x12, waiting for transfers between devices: 6.45 us -> 32.6 us  [shift_y(): return lax.ppermute(block, 'col', pairs)]
    ppermute x12, starting transfers between devices: 27.1 us -> 16.3 us  [shift_y(): return lax.ppermute(block, 'col', pairs)]
    ppermute x4 -> x3, waiting for transfers between devices: 8.05 us -> 0.01 us  [flip(): return lax.ppermute(block, ('row', 'col'), pairs)]
    unnamed x36 -> x8, local copies, waits for them, and re-layouts: 6.62 us -> 1.75 us
    ppermute x2, starting transfers between devices: 6.19 us -> 2.07 us  [swap_cores(): return lax.ppermute(block, 'col', [(i, i ^ 1) for i in range(16)])]
    ppermute x14, starting transfers between devices: 16.3 us -> 18.5 us  [shift_row(): return lax.ppermute(block, 'row', pairs)]
    sub x1 -> x0, other arithmetic: 1.98 us -> none  [per_device(): 25.0 * diff / 32.0 - 25.0 * BATCH / 64.0 * hinge]
    reduce_sum x2 -> x0, other arithmetic: 1.63 us -> none  [the longest x1 1.01 us: per_device(): parts = jnp.where(lanes == 1, jnp.sum(diff * diff), F32(0.0))]
  transfers between devices with their start and end apart: 35 -> 33, of which waited for: 10 -> 14; matrix products, arithmetic and copies ran while one was open for 6% -> 1% of each run, Pallas kernels for 15% -> 15%
where the time goes in v4:
time: 133 us
  waiting for transfers between devices  55.8 us (42%)
  starting transfers between devices  47.3 us (36%)
  Pallas kernels  24.3 us (18%)
  local copies, waits for them, and re-layouts  3.4 us (3%)
  other arithmetic  1.41 us (1%)
    ppermute x12, waiting for transfers between devices, shift_y(): return lax.ppermute(block, 'col', pairs)  32.6 us
    pallas_call x16, Pallas kernels, call(): pl.pallas_call(kernel, out_shape=tuple(outs), in_specs=[SMEM if a.dtype =...  24.3 us
    ppermute x14, waiting for transfers between devices, shift_row(): return lax.ppermute(block, 'row', pairs)  23.2 us
    ppermute x14, starting transfers between devices, shift_row(): return lax.ppermute(block, 'row', pairs)  18.5 us
    ppermute x12, starting transfers between devices, shift_y(): return lax.ppermute(block, 'col', pairs)  16.3 us
    ppermute x2, starting transfers between devices, swap_z_hi(): return lax.ppermute(block, 'col', [(i, i ^ 8) for i in range(16)])  7.46 us
    ppermute x3, starting transfers between devices, flip(): return lax.ppermute(block, ('row', 'col'), pairs)  2.93 us
  transfers between devices with their start and end apart: 33, of which 14 were waited for; matrix products, arithmetic and copies ran while one was open for 1% of the time, Pallas kernels for 15%

profile of v4, /device:TPU:1, one launch (start us, length us, event | category | flops | bytes accessed | tf_op | source)
XLA Modules:
  0.0 133.1 jit_solution(11710017915692532821)
XLA Ops:
  10.0 5.0 %collective-permute-done.1.refs_3_.refs_5_ = bf16[768,256]{1,0:T(8,128)(2,1)S(1)} collective-permute-done((bf16[768,256]{1,0:T(8,128)(2,1)S(1)}, bf16[768,256]{1,0:T(8,128)(2,1)S(1)}, u32[]{:S(2)}, u32[]{:S(2)}) %collective-permute-start.1) | collective-permute-done | bytes 393248 | tf_op jit(solution)/shard_map/ppermute | solution.py:27
  20.4 3.2 %collective-permute-done.2.refs_6_ = bf16[768,256]{1,0:T(8,128)(2,1)} collective-permute-done((bf16[768,256]{1,0:T(8,128)(2,1)S(1)}, bf16[768,256]{1,0:T(8,128)(2,1)}, u32[]{:S(2)}, u32[]{:S(2)}) %collective-permute-start.2) | collective-permute-done | bytes 393248 | tf_op jit(solution)/shard_map/ppermute | solution.py:27
  23.7 2.6 %collective-permute-start.5 = (bf16[768,256]{1,0:T(8,128)(2,1)}, bf16[768,256]{1,0:T(8,128)(2,1)S(1)}, u32[]{:S(2)}, u32[]{:S(2)}) collective-permute-start(bf16[768,256]{1,0:T(8,128)(2,1)} %collective-permute-done.4.refs_8_), channel_id=1, source_target_pairs={{0,96},{16,112},{32,0},{48,16},{64,32},{80,48},{96,64},{112,80},{1... | collective-permute-start | bytes 1179656 | tf_op jit(solution)/shard_map/ppermute | solution.py:27
  27.3 4.5 %partial_near.1 = (f32[144,1024]{1,0:T(8,128)S(1)}, bf16[144,1024]{1,0:T(8,128)(2,1)S(1)}, bf16[144,1024]{1,0:T(8,128)(2,1)S(1)}, bf16[144,1024]{1,0:T(8,128)(2,...) custom-call(s32[5]{0:T(128)S(1)} %stack.23.refs_0_, bf16[512,1536]{1,0:T(8,128)(2,1)S(1)} %get-tuple-element.33.refs_1_, ...), custom_call_target="tpu_custom_call" | custom-call | flops 32212254720 | tf_op jit(solution)/shard_map/partial_near/pallas_call | solution.py:60
  37.6 2.6 %collective-permute-start.16 = (bf16[144,1024]{1,0:T(8,128)(2,1)S(1)}, bf16[144,1024]{1,0:T(8,128)(2,1)S(1)}, u32[]{:S(2)}, u32[]{:S(2)}) collective-permute-start(bf16[144,1024]{1,0:T(8,128)(2,1)S(1)} %get-tuple-element.47), channel_id=1, source_target_pairs={{0,4},{1,5},{2,6},{3,7},{4,0},{5,1},{6,2},{7,3},{8,12},{9,13},{10,... | collective-permute-start | bytes 884744 | tf_op jit(solution)/shard_map/ppermute | solution.py:47
  40.2 10.5 %collective-permute-done.10.refs_5_ = bf16[1536,256]{1,0:T(8,128)(2,1)S(1)} collective-permute-done((bf16[1536,256]{1,0:T(8,128)(2,1)S(1)}, bf16[1536,256]{1,0:T(8,128)(2,1)S(1)}, u32[]{:S(2)}, u32[]{:S(2)}) %collective-permute-start.10) | collective-permute-done | bytes 786464 | tf_op jit(solution)/shard_map/ppermute | solution.py:27
  50.7 2.7 %collective-permute-start.17 = (bf16[144,1024]{1,0:T(8,128)(2,1)S(1)}, bf16[144,1024]{1,0:T(8,128)(2,1)S(1)}, u32[]{:S(2)}, u32[]{:S(2)}) collective-permute-start(bf16[144,1024]{1,0:T(8,128)(2,1)S(1)} %get-tuple-element.48), channel_id=1, source_target_pairs={{0,6},{1,7},{2,0},{3,1},{4,2},{5,3},{6,4},{7,5},{8,14},{9,15},{10,... | collective-permute-start | bytes 884744 | tf_op jit(solution)/shard_map/ppermute | solution.py:47
  53.5 3.7 %partial_far.1 = (f32[144,1024]{1,0:T(8,128)S(1)}, bf16[144,1024]{1,0:T(8,128)(2,1)S(1)}, bf16[144,1024]{1,0:T(8,128)(2,1)S(1)}, bf16[144,1024]{1,0:T(8,128)(2,1...) custom-call(s32[5]{0:T(128)S(1)} %stack.23.refs_0_, bf16[512,1536]{1,0:T(8,128)(2,1)S(1)} %get-tuple-element.33.refs_1_, ...), custom_call_target="tpu_custom_call" | custom-call | flops 32212254720 | tf_op jit(solution)/shard_map/partial_far/pallas_call | solution.py:60
  59.7 3.5 %collective-permute-start.18 = (bf16[160,1024]{1,0:T(8,128)(2,1)S(1)}, bf16[160,1024]{1,0:T(8,128)(2,1)S(1)}, u32[]{:S(2)}, u32[]{:S(2)}) collective-permute-start(bf16[160,1024]{1,0:T(8,128)(2,1)S(1)} %get-tuple-element.54), channel_id=1, source_target_pairs={{0,8},{1,9},{2,10},{3,11},{4,12},{5,13},{6,14},{7,15},{8,0},{9,1},... | collective-permute-start | bytes 983048 | tf_op jit(solution)/shard_map/ppermute | solution.py:51
  63.2 2.1 %collective-permute-start.14 = (bf16[144,1024]{1,0:T(8,128)(2,1)S(1)}, bf16[144,1024]{1,0:T(8,128)(2,1)S(1)}, u32[]{:S(2)}, u32[]{:S(2)}) collective-permute-start(bf16[144,1024]{1,0:T(8,128)(2,1)S(1)} %get-tuple-element.44), channel_id=1, source_target_pairs={{0,6},{1,7},{2,0},{3,1},{4,2},{5,3},{6,4},{7,5},{8,14},{9,15},{10,... | collective-permute-start | bytes 884744 | tf_op jit(solution)/shard_map/ppermute | solution.py:47
  65.3 2.6 %collective-permute-done.12.refs_3_ = bf16[144,1024]{1,0:T(8,128)(2,1)S(1)} collective-permute-done((bf16[144,1024]{1,0:T(8,128)(2,1)S(1)}, bf16[144,1024]{1,0:T(8,128)(2,1)S(1)}, u32[]{:S(2)}, u32[]{:S(2)}) %collective-permute-start.12) | collective-permute-done | bytes 294944 | tf_op jit(solution)/shard_map/ppermute | solution.py:47
  68.4 3.3 %collective-permute-done.14.refs_5_ = bf16[144,1024]{1,0:T(8,128)(2,1)S(1)} collective-permute-done((bf16[144,1024]{1,0:T(8,128)(2,1)S(1)}, bf16[144,1024]{1,0:T(8,128)(2,1)S(1)}, u32[]{:S(2)}, u32[]{:S(2)}) %collective-permute-start.14) | collective-permute-done | bytes 294944 | tf_op jit(solution)/shard_map/ppermute | solution.py:47
  72.5 4.0 %collective-permute-start.19 = (bf16[144,1024]{1,0:T(8,128)(2,1)S(1)}, bf16[144,1024]{1,0:T(8,128)(2,1)S(1)}, u32[]{:S(2)}, u32[]{:S(2)}) collective-permute-start(bf16[144,1024]{1,0:T(8,128)(2,1)S(1)} %get-tuple-element.56), channel_id=1, source_target_pairs={{0,8},{1,9},{2,10},{3,11},{4,12},{5,13},{6,14},{7,15},{8,0},{9,1},... | collective-permute-start | bytes 884744 | tf_op jit(solution)/shard_map/ppermute | solution.py:51
  77.9 3.7 %collective-permute-start.22 = (bf16[128,1024]{1,0:T(8,128)(2,1)S(1)}, bf16[128,1024]{1,0:T(8,128)(2,1)S(1)}, u32[]{:S(2)}, u32[]{:S(2)}) collective-permute-start(bf16[128,1024]{1,0:T(8,128)(2,1)S(1)} %get-tuple-element.58.refs_4_), channel_id=1, source_target_pairs={{0,6},{1,7},{2,0},{3,1},{4,2},{5,3},{6,4},{7,5},{8,14},{9,15},{10,... | collective-permute-start | bytes 786440 | tf_op jit(solution)/shard_map/ppermute | solution.py:47
  82.2 9.7 %collective-permute-done.22.refs_8_.refs_7_ = bf16[128,1024]{1,0:T(8,128)(2,1)S(1)} collective-permute-done((bf16[128,1024]{1,0:T(8,128)(2,1)S(1)}, bf16[128,1024]{1,0:T(8,128)(2,1)S(1)}, u32[]{:S(2)}, u32[]{:S(2)}) %collective-permute-start.22) | collective-permute-done | bytes 262176 | tf_op jit(solution)/shard_map/ppermute | solution.py:47
  91.9 4.3 %collective-permute-done.20.refs_6_.refs_5_ = bf16[128,1024]{1,0:T(8,128)(2,1)S(1)} collective-permute-done((bf16[128,1024]{1,0:T(8,128)(2,1)S(1)}, bf16[128,1024]{1,0:T(8,128)(2,1)S(1)}, u32[]{:S(2)}, u32[]{:S(2)}) %collective-permute-start.20) | collective-permute-done | bytes 262176 | tf_op jit(solution)/shard_map/ppermute | solution.py:47
  96.2 2.0 %combine_z_far.1 = (bf16[144,1024]{1,0:T(8,128)(2,1)S(1)}, f32[8,128]{1,0:T(8,128)}, f32[8,1024]{1,0:T(8,128)S(1)}) custom-call(s32[5]{0:T(128)S(1)} %stack.23.refs_0_, bf16[128,1024]{1,0:T(8,128)(2,1)S(1)} %get-tuple-element.50.refs_6_.refs_1_, f32[8,1024]{1,0:T(8,128)S(1)} %get-tuple-element.51.refs_2_, f32[8,512]{1,0:T(8,128)S(1)} %get-tuple-element.55.refs_3_, ...), custom_call_target="tpu_custom_call" | custom-call | tf_op jit(solution)/shard_map/combine_z_far/pallas_call | solution.py:60
  100.1 2.7 %grad_near.1.refs_5_.refs_8_ = f32[1536,512]{1,0:T(8,128)S(1)} custom-call(s32[5]{0:T(128)S(1)} %stack.23.refs_0_, bf16[1536,1024]{1,0:T(8,128)(2,1)S(1)} %get-tuple-element.61.refs_1_, f32[8,1024]{1,0:T(8,128)S(1)} %get-tuple-element.37.refs_2_, f32[8,1024]{1,0:T(8,128)S(1)} %get-tuple-element.62.refs_3_, bf16[128,1024]{1,0:T(8,128)(2,1)S(1)} %get-tuple-element.58.refs_4_, ...), custom_call_target="tpu_custom_call" | custom-call | tf_op jit(solution)/shard_map/grad_near/pallas_call | solution.py:60
  102.9 3.0 %collective-permute-done.25.refs_4_.refs_7_ = bf16[144,1024]{1,0:T(8,128)(2,1)S(1)} collective-permute-done((bf16[144,1024]{1,0:T(8,128)(2,1)S(1)}, bf16[144,1024]{1,0:T(8,128)(2,1)S(1)}, u32[]{:S(2)}, u32[]{:S(2)}) %collective-permute-start.25) | collective-permute-done | bytes 294944 | tf_op jit(solution)/shard_map/ppermute | solution.py:47
  106.5 8.4 %collective-permute-done.23.refs_2_.refs_5_ = bf16[144,1024]{1,0:T(8,128)(2,1)S(1)} collective-permute-done((bf16[144,1024]{1,0:T(8,128)(2,1)S(1)}, bf16[144,1024]{1,0:T(8,128)(2,1)S(1)}, u32[]{:S(2)}, u32[]{:S(2)}) %collective-permute-start.23) | collective-permute-done | bytes 294944 | tf_op jit(solution)/shard_map/ppermute | solution.py:47
  118.1 3.4 %collective-permute-start.28 = (f32[8,128]{1,0:T(8,128)S(1)}, f32[8,128]{1,0:T(8,128)S(1)}, u32[]{:S(2)}, u32[]{:S(2)}) collective-permute-start(f32[8,128]{1,0:T(8,128)S(1)} %sum_parts.1.refs_1_.refs_9_), channel_id=1, source_target_pairs={{0,96},{16,112},{32,0},{48,16},{64,32},{80,48},{96,64},{112,80},{1... | collective-permute-start | bytes 12296 | tf_op jit(solution)/shard_map/ppermute | solution.py:27
  122.2 3.2 %collective-permute-done.27.refs_3_ = f32[8,128]{1,0:T(8,128)S(1)} collective-permute-done((f32[8,128]{1,0:T(8,128)S(1)}, f32[8,128]{1,0:T(8,128)S(1)}, u32[]{:S(2)}, u32[]{:S(2)}) %collective-permute-start.27) | collective-permute-done | bytes 4128 | tf_op jit(solution)/shard_map/ppermute | solution.py:27
  126.0 2.0 %collective-permute-start.32 = (f32[8,128]{1,0:T(8,128)S(1)}, f32[8,128]{1,0:T(8,128)S(1)}, u32[]{:S(2)}, u32[]{:S(2)}) collective-permute-start(f32[8,128]{1,0:T(8,128)S(1)} %sum_x.1.refs_10_.refs_0_), channel_id=1, source_target_pairs={{0,17},{1,16},{2,19},{3,18},{4,21},{5,20},{6,23},{7,22},{8,25},{9,... | collective-permute-start | bytes 12296 | tf_op jit(solution)/shard_map/ppermute | solution.py:35
  129.0 2.0 %grad_far_kept.1 = f32[768,512]{1,0:T(8,128)S(1)} custom-call(s32[5]{0:T(128)S(1)} %stack.23.refs_0_, bf16[1536,1024]{1,0:T(8,128)(2,1)S(1)} %get-tuple-element.38.refs_1_, f32[8,1024]{1,0:T(8,128)S(1)} %get-tuple-element.39.refs_2_, f32[8,1024]{1,0:T(8,128)S(1)} %get-tuple-element.59.refs_3_, ...), custom_call_target="tpu_custom_call" | custom-call | tf_op jit(solution)/shard_map/grad_far_kept/pallas_call | solution.py:60
  (71 shorter events, 37.5 us)
Async XLA Ops:
  3.2 11.9 %collective-permute-start.1 = (bf16[768,256]{1,0:T(8,128)(2,1)S(1)}, bf16[768,256]{1,0:T(8,128)(2,1)S(1)}, u32[]{:S(2)}, u32[]{:S(2)}) collective-permute-start(bf16[768,256]{1,0:T(8,128)(2,1)S(1)} %constant_dynamic-slice_fusion.1.refs_3_), channel_id=1, source_target_pairs={{0,32},{16,48},{32,64},{48,80},{64,96},{80,112},{96,0},{112,16},{1... | collective-permute-start | bytes 1179656 | tf_op jit(solution)/shard_map/ppermute | solution.py:27
  4.6 19.0 %collective-permute-start.2 = (bf16[768,256]{1,0:T(8,128)(2,1)S(1)}, bf16[768,256]{1,0:T(8,128)(2,1)}, u32[]{:S(2)}, u32[]{:S(2)}) collective-permute-start(bf16[768,256]{1,0:T(8,128)(2,1)S(1)} %constant_dynamic-slice_fusion.refs_4_), channel_id=1, source_target_pairs={{0,32},{16,48},{32,64},{48,80},{64,96},{80,112},{96,0},{112,16},{1... | collective-permute-start | bytes 1179656 | tf_op jit(solution)/shard_map/ppermute | solution.py:27
  5.9 17.8 %collective-permute-start.4 = (bf16[768,256]{1,0:T(8,128)(2,1)S(1)}, bf16[768,256]{1,0:T(8,128)(2,1)}, u32[]{:S(2)}, u32[]{:S(2)}) collective-permute-start(bf16[768,256]{1,0:T(8,128)(2,1)S(1)} %constant_dynamic-slice_fusion.refs_4_), channel_id=1, source_target_pairs={{0,96},{16,112},{32,0},{48,16},{64,32},{80,48},{96,64},{112,80},{1... | collective-permute-start | bytes 1179656 | tf_op jit(solution)/shard_map/ppermute | solution.py:27
  7.3 18.9 %collective-permute-start.8 = (bf16[768,256]{1,0:T(8,128)(2,1)S(1)}, bf16[768,256]{1,0:T(8,128)(2,1)}, u32[]{:S(2)}, u32[]{:S(2)}) collective-permute-start(bf16[768,256]{1,0:T(8,128)(2,1)S(1)} %constant_dynamic-slice_fusion.1.refs_3_), channel_id=1, source_target_pairs={{0,96},{16,112},{32,0},{48,16},{64,32},{80,48},{96,64},{112,80},{1... | collective-permute-start | bytes 1179656 | tf_op jit(solution)/shard_map/ppermute | solution.py:27
  8.4 17.9 %collective-permute-start.6 = (bf16[768,256]{1,0:T(8,128)(2,1)S(1)}, bf16[768,256]{1,0:T(8,128)(2,1)S(1)}, u32[]{:S(2)}, u32[]{:S(2)}) collective-permute-start(bf16[768,256]{1,0:T(8,128)(2,1)S(1)} %constant_dynamic-slice_fusion.1.refs_3_), channel_id=1, source_target_pairs={{0,16},{16,0},{32,48},{48,32},{64,80},{80,64},{96,112},{112,96},{1... | collective-permute-start | bytes 1179656 | tf_op jit(solution)/shard_map/ppermute | solution.py:27
  15.8 11.6 %collective-permute-start.7 = (bf16[768,256]{1,0:T(8,128)(2,1)S(1)}, bf16[768,256]{1,0:T(8,128)(2,1)}, u32[]{:S(2)}, u32[]{:S(2)}) collective-permute-start(bf16[768,256]{1,0:T(8,128)(2,1)S(1)} %constant_dynamic-slice_fusion.refs_4_), channel_id=1, source_target_pairs={{0,16},{16,0},{32,48},{48,32},{64,80},{80,64},{96,112},{112,96},{1... | collective-permute-start | bytes 1179656 | tf_op jit(solution)/shard_map/ppermute | solution.py:27
  23.6 10.9 %collective-permute-start.3 = (bf16[768,256]{1,0:T(8,128)(2,1)S(1)}, bf16[768,256]{1,0:T(8,128)(2,1)S(1)}, u32[]{:S(2)}, u32[]{:S(2)}) collective-permute-start(bf16[768,256]{1,0:T(8,128)(2,1)S(1)} %copy-done.3), channel_id=1, source_target_pairs={{0,32},{16,48},{32,64},{48,80},{64,96},{80,112},{96,0},{112,16},{1... | collective-permute-start | bytes 1179656 | tf_op jit(solution)/shard_map/ppermute | solution.py:27
  23.7 10.8 %collective-permute-start.5 = (bf16[768,256]{1,0:T(8,128)(2,1)}, bf16[768,256]{1,0:T(8,128)(2,1)S(1)}, u32[]{:S(2)}, u32[]{:S(2)}) collective-permute-start(bf16[768,256]{1,0:T(8,128)(2,1)} %collective-permute-done.4.refs_8_), channel_id=1, source_target_pairs={{0,96},{16,112},{32,0},{48,16},{64,32},{80,48},{96,64},{112,80},{1... | collective-permute-start | bytes 1179656 | tf_op jit(solution)/shard_map/ppermute | solution.py:27
  32.9 17.8 %collective-permute-start.10 = (bf16[1536,256]{1,0:T(8,128)(2,1)S(1)}, bf16[1536,256]{1,0:T(8,128)(2,1)S(1)}, u32[]{:S(2)}, u32[]{:S(2)}) collective-permute-start(bf16[1536,256]{1,0:T(8,128)(2,1)S(1)} %join.2.refs_2_), channel_id=1, source_target_pairs={{0,96},{16,112},{32,0},{48,16},{64,32},{80,48},{96,64},{112,80},{1... | collective-permute-start | bytes 2359304 | tf_op jit(solution)/shard_map/ppermute | solution.py:27
  33.0 20.5 %collective-permute-start.9 = (bf16[1536,256]{1,0:T(8,128)(2,1)S(1)}, bf16[1536,256]{1,0:T(8,128)(2,1)S(1)}, u32[]{:S(2)}, u32[]{:S(2)}) collective-permute-start(bf16[1536,256]{1,0:T(8,128)(2,1)S(1)} %join.2.refs_2_), channel_id=1, source_target_pairs={{0,32},{16,48},{32,64},{48,80},{64,96},{80,112},{96,0},{112,16},{1... | collective-permute-start | bytes 2359304 | tf_op jit(solution)/shard_map/ppermute | solution.py:27
  34.5 19.0 %collective-permute-start.11 = (bf16[1536,256]{1,0:T(8,128)(2,1)S(1)}, bf16[1536,256]{1,0:T(8,128)(2,1)S(1)}, u32[]{:S(2)}, u32[]{:S(2)}) collective-permute-start(bf16[1536,256]{1,0:T(8,128)(2,1)S(1)} %join.3.refs_3_), channel_id=1, source_target_pairs={{0,16},{16,0},{32,48},{48,32},{64,80},{80,64},{96,112},{112,96},{1... | collective-permute-start | bytes 2359304 | tf_op jit(solution)/shard_map/ppermute | solution.py:27
  36.3 22.6 %collective-permute-start.15 = (bf16[144,1024]{1,0:T(8,128)(2,1)S(1)}, bf16[144,1024]{1,0:T(8,128)(2,1)S(1)}, u32[]{:S(2)}, u32[]{:S(2)}) collective-permute-start(bf16[144,1024]{1,0:T(8,128)(2,1)S(1)} %get-tuple-element.46), channel_id=1, source_target_pairs={{0,2},{1,3},{2,4},{3,5},{4,6},{5,7},{6,0},{7,1},{8,10},{9,11},{10,... | collective-permute-start | bytes 884744 | tf_op jit(solution)/shard_map/ppermute | solution.py:47
  37.6 21.3 %collective-permute-start.16 = (bf16[144,1024]{1,0:T(8,128)(2,1)S(1)}, bf16[144,1024]{1,0:T(8,128)(2,1)S(1)}, u32[]{:S(2)}, u32[]{:S(2)}) collective-permute-start(bf16[144,1024]{1,0:T(8,128)(2,1)S(1)} %get-tuple-element.47), channel_id=1, source_target_pairs={{0,4},{1,5},{2,6},{3,7},{4,0},{5,1},{6,2},{7,3},{8,12},{9,13},{10,... | collective-permute-start | bytes 884744 | tf_op jit(solution)/shard_map/ppermute | solution.py:47
  57.2 10.7 %collective-permute-start.12 = (bf16[144,1024]{1,0:T(8,128)(2,1)S(1)}, bf16[144,1024]{1,0:T(8,128)(2,1)S(1)}, u32[]{:S(2)}, u32[]{:S(2)}) collective-permute-start(bf16[144,1024]{1,0:T(8,128)(2,1)S(1)} %get-tuple-element.42), channel_id=1, source_target_pairs={{0,2},{1,3},{2,4},{3,5},{4,6},{5,7},{6,0},{7,1},{8,10},{9,11},{10,... | collective-permute-start | bytes 884744 | tf_op jit(solution)/shard_map/ppermute | solution.py:47
  57.3 11.2 %collective-permute-start.13 = (bf16[144,1024]{1,0:T(8,128)(2,1)S(1)}, bf16[144,1024]{1,0:T(8,128)(2,1)S(1)}, u32[]{:S(2)}, u32[]{:S(2)}) collective-permute-start(bf16[144,1024]{1,0:T(8,128)(2,1)S(1)} %get-tuple-element.43), channel_id=1, source_target_pairs={{0,4},{1,5},{2,6},{3,7},{4,0},{5,1},{6,2},{7,3},{8,12},{9,13},{10,... | collective-permute-start | bytes 884744 | tf_op jit(solution)/shard_map/ppermute | solution.py:47
  59.7 16.8 %collective-permute-start.18 = (bf16[160,1024]{1,0:T(8,128)(2,1)S(1)}, bf16[160,1024]{1,0:T(8,128)(2,1)S(1)}, u32[]{:S(2)}, u32[]{:S(2)}) collective-permute-start(bf16[160,1024]{1,0:T(8,128)(2,1)S(1)} %get-tuple-element.54), channel_id=1, source_target_pairs={{0,8},{1,9},{2,10},{3,11},{4,12},{5,13},{6,14},{7,15},{8,0},{9,1},... | collective-permute-start | bytes 983048 | tf_op jit(solution)/shard_map/ppermute | solution.py:51
  63.2 8.6 %collective-permute-start.14 = (bf16[144,1024]{1,0:T(8,128)(2,1)S(1)}, bf16[144,1024]{1,0:T(8,128)(2,1)S(1)}, u32[]{:S(2)}, u32[]{:S(2)}) collective-permute-start(bf16[144,1024]{1,0:T(8,128)(2,1)S(1)} %get-tuple-element.44), channel_id=1, source_target_pairs={{0,6},{1,7},{2,0},{3,1},{4,2},{5,3},{6,4},{7,5},{8,14},{9,15},{10,... | collective-permute-start | bytes 884744 | tf_op jit(solution)/shard_map/ppermute | solution.py:47
  72.5 9.7 %collective-permute-start.19 = (bf16[144,1024]{1,0:T(8,128)(2,1)S(1)}, bf16[144,1024]{1,0:T(8,128)(2,1)S(1)}, u32[]{:S(2)}, u32[]{:S(2)}) collective-permute-start(bf16[144,1024]{1,0:T(8,128)(2,1)S(1)} %get-tuple-element.56), channel_id=1, source_target_pairs={{0,8},{1,9},{2,10},{3,11},{4,12},{5,13},{6,14},{7,15},{8,0},{9,1},... | collective-permute-start | bytes 884744 | tf_op jit(solution)/shard_map/ppermute | solution.py:51
  77.9 14.0 %collective-permute-start.22 = (bf16[128,1024]{1,0:T(8,128)(2,1)S(1)}, bf16[128,1024]{1,0:T(8,128)(2,1)S(1)}, u32[]{:S(2)}, u32[]{:S(2)}) collective-permute-start(bf16[128,1024]{1,0:T(8,128)(2,1)S(1)} %get-tuple-element.58.refs_4_), channel_id=1, source_target_pairs={{0,6},{1,7},{2,0},{3,1},{4,2},{5,3},{6,4},{7,5},{8,14},{9,15},{10,... | collective-permute-start | bytes 786440 | tf_op jit(solution)/shard_map/ppermute | solution.py:47
  81.5 10.4 %collective-permute-start.21 = (bf16[128,1024]{1,0:T(8,128)(2,1)S(1)}, bf16[128,1024]{1,0:T(8,128)(2,1)S(1)}, u32[]{:S(2)}, u32[]{:S(2)}) collective-permute-start(bf16[128,1024]{1,0:T(8,128)(2,1)S(1)} %get-tuple-element.58.refs_4_), channel_id=1, source_target_pairs={{0,4},{1,5},{2,6},{3,7},{4,0},{5,1},{6,2},{7,3},{8,12},{9,13},{10,... | collective-permute-start | bytes 786440 | tf_op jit(solution)/shard_map/ppermute | solution.py:47
  81.5 14.7 %collective-permute-start.20 = (bf16[128,1024]{1,0:T(8,128)(2,1)S(1)}, bf16[128,1024]{1,0:T(8,128)(2,1)S(1)}, u32[]{:S(2)}, u32[]{:S(2)}) collective-permute-start(bf16[128,1024]{1,0:T(8,128)(2,1)S(1)} %get-tuple-element.58.refs_4_), channel_id=1, source_target_pairs={{0,2},{1,3},{2,4},{3,5},{4,6},{5,7},{6,0},{7,1},{8,10},{9,11},{10,... | collective-permute-start | bytes 786440 | tf_op jit(solution)/shard_map/ppermute | solution.py:47
  98.2 8.3 %collective-permute-start.24 = (bf16[144,1024]{1,0:T(8,128)(2,1)S(1)}, bf16[144,1024]{1,0:T(8,128)(2,1)S(1)}, u32[]{:S(2)}, u32[]{:S(2)}) collective-permute-start(bf16[144,1024]{1,0:T(8,128)(2,1)S(1)} %get-tuple-element.60.refs_3_.refs_1_.refs_4_), channel_id=1, source_target_pairs={{0,4},{1,5},{2,6},{3,7},{4,0},{5,1},{6,2},{7,3},{8,12},{9,13},{10,... | collective-permute-start | bytes 884744 | tf_op jit(solution)/shard_map/ppermute | solution.py:47
  98.4 16.6 %collective-permute-start.23 = (bf16[144,1024]{1,0:T(8,128)(2,1)S(1)}, bf16[144,1024]{1,0:T(8,128)(2,1)S(1)}, u32[]{:S(2)}, u32[]{:S(2)}) collective-permute-start(bf16[144,1024]{1,0:T(8,128)(2,1)S(1)} %get-tuple-element.60.refs_3_.refs_1_.refs_4_), channel_id=1, source_target_pairs={{0,2},{1,3},{2,4},{3,5},{4,6},{5,7},{6,0},{7,1},{8,10},{9,11},{10,... | collective-permute-start | bytes 884744 | tf_op jit(solution)/shard_map/ppermute | solution.py:47
  117.5 14.2 %collective-permute-start.29 = (bf16[768,512]{1,0:T(8,128)(2,1)S(1)}, bf16[768,512]{1,0:T(8,128)(2,1)S(1)}, u32[]{:S(2)}, u32[]{:S(2)}) collective-permute-start(bf16[768,512]{1,0:T(8,128)(2,1)S(1)} %grad_far_sent.1.refs_11_), channel_id=1, source_target_pairs={{0,1},{1,0},{2,3},{3,2},{4,5},{5,4},{6,7},{7,6},{8,9},{9,8},{10,11... | collective-permute-start | bytes 2359304 | tf_op jit(solution)/shard_map/ppermute | solution.py:39
  (13 other events, 78.4 us)

commit v5 on v4

--- a/solution.py
+++ b/solution.py
@@ -45,6 +45,11 @@
         for z in range(2) for y in range(4) for core in range(2)
     ]
     return lax.ppermute(block, "col", pairs)
+
+
+def sent_round(block):
+    two, one, three_on = [shift_y(block, d) for d in (2, 1, 3)]
+    return [block, one, two, three_on]
 
 
 def swap_z_hi(block):
@@ -347,56 +352,51 @@
         found = found + jnp.where(lanes == 2, var_part, 0.0) + other_parts
     part[...] = parts[...] + found
     masked[0:QUARTER, :] = covar.astype(BF16)
-    if not with_rows:
-        block = filled(padded(split3(part[0:1, :]), covar.shape[1]), covar.shape[1])
-        masked[QUARTER:QUARTER + STAT_ROWS, :] = block.astype(BF16)
 
 
 def combine_z(place, plane, local, rows, received, parts, with_rows, name, after=()):
     width = plane.shape[1]
-    count = QUARTER + (0 if with_rows else STAT_ROWS)
-    outs = [shape((count, width), BF16), shape((8, 128), F32), shape((8, width), F32)]
+    outs = [shape((QUARTER, width), BF16), shape((8, 128), F32), shape((8, width), F32)]
     outs += [shape((8, FEATS), F32)] * 2 if with_rows else []
     ins = [place, plane, local, rows, received, parts]
     return call(functools.partial(combine_z_kernel, with_rows), outs, ins, [], name, after)
 
 
-def parts_kernel(place, own, one, two, three_on, out):
-    lines = jnp.zeros((4, 128), F32)
-    for d, piece in enumerate((own, one, two, three_on)):
-        here = lax.broadcasted_iota(jnp.int32, lines.shape, 0) == (place[2] + 4 - d) % 4
-        lines = jnp.where(here, three(piece[QUARTER:, 0:128].astype(F32), 0), lines)
-    out[...] = jnp.broadcast_to(jnp.sum(lines, axis=0, keepdims=True), out.shape)
-
-
-def sum_parts(place, pieces, after):
-    return call(
-        parts_kernel, [shape((8, 128), F32)], [place] + pieces, [], "sum_parts", after
-    )[0]
-
-
-def x_kernel(place, own, one, two, three_on, out):
-    total = jnp.zeros((8, 128), F32)
-    for x in range(4):
-        block = own[...]
-        for d, other in ((1, one), (2, two), (3, three_on)):
-            block = jnp.where((place[4] + 4 - d) % 4 == x, other[...], block)
-        total = total + block
-    out[...] = total
-
-
-def loss_kernel(own, other_z, other_core, other_both, out):
-    total = (own[...] + other_z[...]) + (other_core[...] + other_both[...])
+def add_kernel(one, two, out):
+    out[...] = one[...] + two[...]
+
+
+def add_four_kernel(one, two, three_on, four, out):
+    out[...] = (one[...] + two[...]) + (three_on[...] + four[...])
+
+
+def loss_kernel(one, two, three_on, four, out):
+    total = (one[...] + two[...]) + (three_on[...] + four[...])
     loss = total[:, 0:1] + 25.0 * (total[:, 1:2] / BATCH + total[:, 2:3])
     out[...] = jnp.broadcast_to(loss / (8 * FEATS), out.shape)
 
 
-def sum_x(place, blocks):
-    return call(x_kernel, [shape((8, 128), F32)], [place] + blocks, [], "sum_x")[0]
-
-
-def loss_of(blocks):
-    return call(loss_kernel, [shape((8, 128), F32)], blocks, [], "loss")[0]
+def flip(parts, row_bits, col_bits):
+    if not row_bits:
+        return lax.ppermute(parts, "col", [(i, i ^ col_bits) for i in range(16)])
+    if not col_bits:
+        return lax.ppermute(parts, "row", [(i, i ^ row_bits) for i in range(8)])
+    pairs = [
+        (16 * row + col, 16 * (row ^ row_bits) + (col ^ col_bits))
+        for row in range(8) for col in range(16)
+    ]
+    return lax.ppermute(parts, ("row", "col"), pairs)
+
+
+def pair_sum(parts, row_bits, col_bits, after=()):
+    ins = [parts, flip(parts, row_bits, col_bits)]
+    return call(add_kernel, [shape((8, 128), F32)], ins, [], "pair_sum", after)[0]
+
+
+def four_sum(parts, first, second, body, name, after=()):
+    both = (first[0] | second[0], first[1] | second[1])
+    ins = [parts] + [flip(parts, *bits) for bits in (first, second, both)]
+    return call(body, [shape((8, 128), F32)], ins, [], name, after)[0]
 
 
 def shift_term(stats, means, masked):
@@ -477,11 +477,14 @@
     x_far = join(x_far_a, x_far_b, [z_own])
     z_far = shift_row(x_far, 0, 1)
     far = [x_far, z_lo, z_hi, z_far]
-    near_sums[1:] = [shift_y(near_sums[d], d) for d in (1, 2, 3)]
+    near_sums[1], near_sums[3] = shift_y(near_sums[1], 1), shift_y(near_sums[3], 3)
+    near_sums = list(lax.optimization_barrier(tuple(near_sums)))
+    near_sums[2] = shift_y(near_sums[2], 2)
     far_sums, far_columns, far_stats = partial_sums(
         place, rows_t, own_stats, far, False, "partial_far"
     )
-    far_sums[1:] = [shift_y(far_sums[d], d) for d in (1, 2, 3)]
+    for d in (1, 3, 2):
+        far_sums[d] = shift_y(far_sums[d], d)
 
     plane, message, local, row_local = combine_y(
         place, parts, near_sums, True, "combine_y_near", [far_sums[0]]
@@ -494,12 +497,12 @@
         "combine_z_near",
         [far_plane],
     )
-    near_pieces = [near_masked] + [shift_y(near_masked, d) for d in (1, 2, 3)]
-    far_masked, _, far_means = combine_z(
+    near_pieces = sent_round(near_masked)
+    far_masked, parts, far_means = combine_z(
         place, far_plane, far_local, row_offsets, swap_z_hi(far_message), parts, False,
         "combine_z_far", near_pieces[1:],
     )
-    far_pieces = [far_masked] + [shift_y(far_masked, d) for d in (1, 2, 3)]
+    far_pieces = sent_round(far_masked)
 
     base = base_part(student, teacher, row_stats, [far_masked])
     near_inputs = (near_columns, near_stats, near_means)
@@ -507,17 +510,16 @@
     grads = grad_part(
         place, near_inputs, near_pieces, None, 0, CHIP_IMAGES, F32, "grad_near", [base]
     )
-    parts = sum_parts(place, far_pieces, [grads])
+    parts = pair_sum(pair_sum(parts, 2, 0), 4, 0)
     outgoing = grad_part(
         place, far_inputs, far_pieces, grads, IMAGES, IMAGES, BF16, "grad_far_sent", [parts]
     )
     incoming = swap_cores(outgoing)
-    row_parts = sum_x(place, [parts] + [shift_row(parts, dx, 0) for dx in (1, 2, 3)])
     kept = grad_part(
-        place, far_inputs, far_pieces, grads, 0, IMAGES, F32, "grad_far_kept",
-        [row_parts, outgoing], base,
-    )
-    total_loss = loss_of([row_parts] + [flip(row_parts, *way) for way in ((1, 0), (0, 1), (1, 1))])
+        place, far_inputs, far_pieces, grads, 0, IMAGES, F32, "grad_far_kept", [outgoing], base
+    )
+    parts = four_sum(parts, (1, 0), (0, 1), add_four_kernel, "four_sum")
+    total_loss = four_sum(parts, (0, 2), (0, 4), loss_kernel, "loss", [kept])
     return (kept + GRAD_SCALE * incoming.astype(F32), total_loss[0, 0])
 
 

time: 133 us -> 125 us (0.940); the launches traced: 133 us -> 123 us
  waiting for transfers between devices: 55.8 us -> 39.4 us
  starting transfers between devices: 47.3 us -> 55.5 us
  Pallas kernels: 24.3 us -> 22.8 us
    ppermute x12, waiting for transfers between devices: 32.6 us -> 20.8 us  [shift_y(): return lax.ppermute(block, 'col', pairs)]
    ppermute x14 -> x11, waiting for transfers between devices: 23.2 us -> 14.5 us  [shift_row(): return lax.ppermute(block, 'row', pairs)]
    ppermute x3 -> x8, starting transfers between devices: 2.93 us -> 11.3 us  [the longest x3 6.8 us: flip(): return lax.ppermute(parts, 'row', [(i, i ^ row_bits) for i in range(8)])]
    ppermute x14 -> x11, starting transfers between devices: 18.5 us -> 14.5 us  [shift_row(): return lax.ppermute(block, 'row', pairs)]
    ppermute x3 -> x8, waiting for transfers between devices: 0.01 us -> 4.03 us  [the longest x3 1.61 us: flip(): return lax.ppermute(parts, 'row', [(i, i ^ row_bits) for i in range(8)])]
    ppermute x2, starting transfers between devices: 2.07 us -> 5.68 us  [swap_cores(): return lax.ppermute(block, 'col', [(i, i ^ 1) for i in range(16)])]
    ppermute x12, starting transfers between devices: 16.3 us -> 19.5 us  [shift_y(): return lax.ppermute(block, 'col', pairs)]
    ppermute x2, starting transfers between devices: 7.46 us -> 4.47 us  [swap_z_hi(): return lax.ppermute(block, 'col', [(i, i ^ 8) for i in range(16)])]
  transfers between devices with their start and end apart: 33 -> 35, of which waited for: 14 -> 16; matrix products, arithmetic and copies ran while one was open for 1% -> 1% of each run, Pallas kernels for 15% -> 16%
where the time goes in v5:
time: 125 us; the launch traced here: 123 us
  starting transfers between devices  55.5 us (44%)
  waiting for transfers between devices  39.4 us (32%)
  Pallas kernels  22.8 us (18%)
  local copies, waits for them, and re-layouts  3.4 us (3%)
  other arithmetic  1.41 us (1%)
    pallas_call x17, Pallas kernels, call(): pl.pallas_call(kernel, out_shape=tuple(outs), in_specs=[SMEM if a.dtype =...  22.8 us
    ppermute x12, waiting for transfers between devices, shift_y(): return lax.ppermute(block, 'col', pairs)  20.8 us
    ppermute x12, starting transfers between devices, shift_y(): return lax.ppermute(block, 'col', pairs)  19.5 us
    ppermute x11, starting transfers between devices, shift_row(): return lax.ppermute(block, 'row', pairs)  14.5 us
    ppermute x11, waiting for transfers between devices, shift_row(): return lax.ppermute(block, 'row', pairs)  14.5 us
    ppermute x3, starting transfers between devices, flip(): return lax.ppermute(parts, 'row', [(i, i ^ row_bits) for i in range(8)])  6.8 us
    ppermute x2, starting transfers between devices, swap_cores(): return lax.ppermute(block, 'col', [(i, i ^ 1) for i in range(16)])  5.68 us
    ppermute x2, starting transfers between devices, swap_z_hi(): return lax.ppermute(block, 'col', [(i, i ^ 8) for i in range(16)])  4.47 us
  transfers between devices with their start and end apart: 35, of which 16 were waited for; matrix products, arithmetic and copies ran while one was open for 1% of the time, Pallas kernels for 16%

profile of v5, /device:TPU:1, one launch (start us, length us, event | category | flops | bytes accessed | tf_op | source)
XLA Modules:
  0.0 123.3 jit_solution(12572206097956584376)
XLA Ops:
  10.0 5.0 %collective-permute-done.1.refs_3_.refs_5_ = bf16[768,256]{1,0:T(8,128)(2,1)S(1)} collective-permute-done((bf16[768,256]{1,0:T(8,128)(2,1)S(1)}, bf16[768,256]{1,0:T(8,128)(2,1)S(1)}, u32[]{:S(2)}, u32[]{:S(2)}) %collective-permute-start.1) | collective-permute-done | bytes 393248 | tf_op jit(solution)/shard_map/ppermute | solution.py:27
  18.6 1.8 %center_own.1 = (bf16[512,1536]{1,0:T(8,128)(2,1)S(1)}, f32[8,512]{1,0:T(8,128)S(1)}, f32[8,128]{1,0:T(8,128)S(1)}) custom-call(bf16[768,512]{1,0:T(8,128)(2,1)S(1)} %copy-done, bf16[768,512]{1,0:T(8,128)(2,1)S(1)} %collective-permute-done.refs_1_, bf16[768,512]{1,0:T(8,128)(2,1)S(1)} %copy-done.1, bf16[768,256]{1,0:T(8,128)(2,1)S(1)} %copy-done.3), custom_call_target="tpu_custom_call" | custom-call | tf_op jit(solution)/shard_map/center_own/pallas_call | solution.py:65
  20.4 3.2 %collective-permute-done.2.refs_6_ = bf16[768,256]{1,0:T(8,128)(2,1)} collective-permute-done((bf16[768,256]{1,0:T(8,128)(2,1)S(1)}, bf16[768,256]{1,0:T(8,128)(2,1)}, u32[]{:S(2)}, u32[]{:S(2)}) %collective-permute-start.2) | collective-permute-done | bytes 393248 | tf_op jit(solution)/shard_map/ppermute | solution.py:27
  23.7 2.6 %collective-permute-start.5 = (bf16[768,256]{1,0:T(8,128)(2,1)}, bf16[768,256]{1,0:T(8,128)(2,1)S(1)}, u32[]{:S(2)}, u32[]{:S(2)}) collective-permute-start(bf16[768,256]{1,0:T(8,128)(2,1)} %collective-permute-done.4.refs_8_), channel_id=1, source_target_pairs={{0,96},{16,112},{32,0},{48,16},{64,32},{80,48},{96,64},{112,80},{1... | collective-permute-start | bytes 1179656 | tf_op jit(solution)/shard_map/ppermute | solution.py:27
  27.3 4.5 %partial_near.1 = (f32[144,1024]{1,0:T(8,128)S(1)}, bf16[144,1024]{1,0:T(8,128)(2,1)S(1)}, bf16[144,1024]{1,0:T(8,128)(2,1)S(1)}, bf16[144,1024]{1,0:T(8,128)(2,...) custom-call(s32[5]{0:T(128)S(1)} %stack.23.refs_0_, bf16[512,1536]{1,0:T(8,128)(2,1)S(1)} %get-tuple-element.38.refs_1_, ...), custom_call_target="tpu_custom_call" | custom-call | flops 32212254720 | tf_op jit(solution)/shard_map/partial_near/pallas_call | solution.py:65
  39.0 4.4 %collective-permute-done.15.refs_3_ = bf16[144,1024]{1,0:T(8,128)(2,1)S(1)} collective-permute-done((bf16[144,1024]{1,0:T(8,128)(2,1)S(1)}, bf16[144,1024]{1,0:T(8,128)(2,1)S(1)}, u32[]{:S(2)}, u32[]{:S(2)}) %collective-permute-start.15) | collective-permute-done | bytes 294944 | tf_op jit(solution)/shard_map/ppermute | solution.py:47
  43.5 2.6 %collective-permute-start.17 = (bf16[144,1024]{1,0:T(8,128)(2,1)S(1)}, bf16[144,1024]{1,0:T(8,128)(2,1)S(1)}, u32[]{:S(2)}, u32[]{:S(2)}) collective-permute-start(bf16[144,1024]{1,0:T(8,128)(2,1)S(1)} %get-tuple-element.56), channel_id=1, source_target_pairs={{0,4},{1,5},{2,6},{3,7},{4,0},{5,1},{6,2},{7,3},{8,12},{9,13},{10,... | collective-permute-start | bytes 884744 | tf_op jit(solution)/shard_map/ppermute | solution.py:47
  46.1 4.7 %collective-permute-done.10.refs_5_ = bf16[1536,256]{1,0:T(8,128)(2,1)S(1)} collective-permute-done((bf16[1536,256]{1,0:T(8,128)(2,1)S(1)}, bf16[1536,256]{1,0:T(8,128)(2,1)S(1)}, u32[]{:S(2)}, u32[]{:S(2)}) %collective-permute-start.10) | collective-permute-done | bytes 786464 | tf_op jit(solution)/shard_map/ppermute | solution.py:27
  51.3 3.7 %partial_far.1 = (f32[144,1024]{1,0:T(8,128)S(1)}, bf16[144,1024]{1,0:T(8,128)(2,1)S(1)}, bf16[144,1024]{1,0:T(8,128)(2,1)S(1)}, bf16[144,1024]{1,0:T(8,128)(2,1...) custom-call(s32[5]{0:T(128)S(1)} %stack.23.refs_0_, bf16[512,1536]{1,0:T(8,128)(2,1)S(1)} %get-tuple-element.38.refs_1_, ...), custom_call_target="tpu_custom_call" | custom-call | flops 32212254720 | tf_op jit(solution)/shard_map/partial_far/pallas_call | solution.py:65
  56.4 2.6 %collective-permute-start.13 = (bf16[144,1024]{1,0:T(8,128)(2,1)S(1)}, bf16[144,1024]{1,0:T(8,128)(2,1)S(1)}, u32[]{:S(2)}, u32[]{:S(2)}) collective-permute-start(bf16[144,1024]{1,0:T(8,128)(2,1)S(1)} %get-tuple-element.48), channel_id=1, source_target_pairs={{0,4},{1,5},{2,6},{3,7},{4,0},{5,1},{6,2},{7,3},{8,12},{9,13},{10,... | collective-permute-start | bytes 884744 | tf_op jit(solution)/shard_map/ppermute | solution.py:47
  59.7 3.2 %collective-permute-start.18 = (bf16[160,1024]{1,0:T(8,128)(2,1)S(1)}, bf16[160,1024]{1,0:T(8,128)(2,1)S(1)}, u32[]{:S(2)}, u32[]{:S(2)}) collective-permute-start(bf16[160,1024]{1,0:T(8,128)(2,1)S(1)} %get-tuple-element.63), channel_id=1, source_target_pairs={{0,8},{1,9},{2,10},{3,11},{4,12},{5,13},{6,14},{7,15},{8,0},{9,1},... | collective-permute-start | bytes 983048 | tf_op jit(solution)/shard_map/ppermute | solution.py:56
  64.0 4.9 %collective-permute-done.13.refs_4_ = bf16[144,1024]{1,0:T(8,128)(2,1)S(1)} collective-permute-done((bf16[144,1024]{1,0:T(8,128)(2,1)S(1)}, bf16[144,1024]{1,0:T(8,128)(2,1)S(1)}, u32[]{:S(2)}, u32[]{:S(2)}) %collective-permute-start.13) | collective-permute-done | bytes 294944 | tf_op jit(solution)/shard_map/ppermute | solution.py:47
  73.6 3.7 %collective-permute-start.22 = (bf16[128,1024]{1,0:T(8,128)(2,1)S(1)}, bf16[128,1024]{1,0:T(8,128)(2,1)S(1)}, u32[]{:S(2)}, u32[]{:S(2)}) collective-permute-start(bf16[128,1024]{1,0:T(8,128)(2,1)S(1)} %get-tuple-element.67.refs_4_), channel_id=1, source_target_pairs={{0,6},{1,7},{2,0},{3,1},{4,2},{5,3},{6,4},{7,5},{8,14},{9,15},{10,... | collective-permute-start | bytes 786440 | tf_op jit(solution)/shard_map/ppermute | solution.py:47
  77.3 2.8 %collective-permute-start.21 = (bf16[128,1024]{1,0:T(8,128)(2,1)S(1)}, bf16[128,1024]{1,0:T(8,128)(2,1)S(1)}, u32[]{:S(2)}, u32[]{:S(2)}) collective-permute-start(bf16[128,1024]{1,0:T(8,128)(2,1)S(1)} %get-tuple-element.67.refs_4_), channel_id=1, source_target_pairs={{0,4},{1,5},{2,6},{3,7},{4,0},{5,1},{6,2},{7,3},{8,12},{9,13},{10,... | collective-permute-start | bytes 786440 | tf_op jit(solution)/shard_map/ppermute | solution.py:47
  80.2 2.3 %collective-permute-done.22.refs_8_.refs_7_ = bf16[128,1024]{1,0:T(8,128)(2,1)S(1)} collective-permute-done((bf16[128,1024]{1,0:T(8,128)(2,1)S(1)}, bf16[128,1024]{1,0:T(8,128)(2,1)S(1)}, u32[]{:S(2)}, u32[]{:S(2)}) %collective-permute-start.22) | collective-permute-done | bytes 262176 | tf_op jit(solution)/shard_map/ppermute | solution.py:47
  84.1 6.2 %collective-permute-done.20.refs_6_.refs_5_ = bf16[128,1024]{1,0:T(8,128)(2,1)S(1)} collective-permute-done((bf16[128,1024]{1,0:T(8,128)(2,1)S(1)}, bf16[128,1024]{1,0:T(8,128)(2,1)S(1)}, u32[]{:S(2)}, u32[]{:S(2)}) %collective-permute-start.20) | collective-permute-done | bytes 262176 | tf_op jit(solution)/shard_map/ppermute | solution.py:47
  92.0 2.3 %collective-permute-start.24 = (bf16[128,1024]{1,0:T(8,128)(2,1)S(1)}, bf16[128,1024]{1,0:T(8,128)(2,1)S(1)}, u32[]{:S(2)}, u32[]{:S(2)}) collective-permute-start(bf16[128,1024]{1,0:T(8,128)(2,1)S(1)} %get-tuple-element.69.refs_3_.refs_4_), channel_id=1, source_target_pairs={{0,4},{1,5},{2,6},{3,7},{4,0},{5,1},{6,2},{7,3},{8,12},{9,13},{10,... | collective-permute-start | bytes 786440 | tf_op jit(solution)/shard_map/ppermute | solution.py:47
  94.3 2.4 %collective-permute-start.26 = (f32[8,128]{1,0:T(8,128)S(1)}, f32[8,128]{1,0:T(8,128)S(1)}, u32[]{:S(2)}, u32[]{:S(2)}) collective-permute-start(f32[8,128]{1,0:T(8,128)S(1)} %get-tuple-element.73.refs_0_), channel_id=1, source_target_pairs={{0,32},{16,48},{32,0},{48,16},{64,96},{80,112},{96,64},{112,80},{1... | collective-permute-start | bytes 12296 | tf_op jit(solution)/shard_map/ppermute | solution.py:383
  98.0 3.4 %collective-permute-start.27 = (f32[8,128]{1,0:T(8,128)S(1)}, f32[8,128]{1,0:T(8,128)S(1)}, u32[]{:S(2)}, u32[]{:S(2)}) collective-permute-start(f32[8,128]{1,0:T(8,128)S(1)} %pair_sum.2.refs_0_), channel_id=1, source_target_pairs={{0,64},{16,80},{32,96},{48,112},{64,0},{80,16},{96,32},{112,48},{1... | collective-permute-start | bytes 12296 | tf_op jit(solution)/shard_map/ppermute | solution.py:383
  101.8 2.8 %grad_near.1.refs_8_ = f32[1536,512]{1,0:T(8,128)S(1)} custom-call(s32[5]{0:T(128)S(1)} %stack.23.refs_0_, bf16[1536,1024]{1,0:T(8,128)(2,1)S(1)} %get-tuple-element.70.refs_1_, f32[8,1024]{1,0:T(8,128)S(1)} %get-tuple-element.42.refs_2_, f32[8,1024]{1,0:T(8,128)S(1)} %get-tuple-element.71.refs_3_, bf16[128,1024]{1,0:T(8,128)(2,1)S(1)} %get-tuple-element.67.refs_4_, ...), custom_call_target="tpu_custom_call" | custom-call | tf_op jit(solution)/shard_map/grad_near/pallas_call | solution.py:65
  104.7 2.0 %grad_far_sent.1.refs_10_ = bf16[768,512]{1,0:T(8,128)(2,1)S(1)} custom-call(s32[5]{0:T(128)S(1)} %stack.23.refs_0_, bf16[1536,1024]{1,0:T(8,128)(2,1)S(1)} %get-tuple-element.43.refs_1_, f32[8,1024]{1,0:T(8,128)S(1)} %get-tuple-element.44.refs_2_, f32[8,1024]{1,0:T(8,128)S(1)} %get-tuple-element.68.refs_3_, ...), custom_call_target="tpu_custom_call" | custom-call | tf_op jit(solution)/shard_map/grad_far_sent/pallas_call | solution.py:65
  106.7 4.2 %collective-permute-start.28 = (bf16[768,512]{1,0:T(8,128)(2,1)S(1)}, bf16[768,512]{1,0:T(8,128)(2,1)S(1)}, u32[]{:S(2)}, u32[]{:S(2)}) collective-permute-start(bf16[768,512]{1,0:T(8,128)(2,1)S(1)} %grad_far_sent.1.refs_10_), channel_id=1, source_target_pairs={{0,1},{1,0},{2,3},{3,2},{4,5},{5,4},{6,7},{7,6},{8,9},{9,8},{10,11... | collective-permute-start | bytes 2359304 | tf_op jit(solution)/shard_map/ppermute | solution.py:39
  114.3 3.0 %collective-permute-start.34 = (f32[8,128]{1,0:T(8,128)S(1)}, f32[8,128]{1,0:T(8,128)S(1)}, u32[]{:S(2)}, u32[]{:S(2)}) collective-permute-start(f32[8,128]{1,0:T(8,128)S(1)} %four_sum.1.refs_0_), channel_id=1, source_target_pairs={{0,6},{1,7},{2,4},{3,5},{4,2},{5,3},{6,0},{7,1},{8,14},{9,15},{10,... | collective-permute-start | bytes 12296 | tf_op jit(solution)/shard_map/ppermute | solution.py:381
  117.9 2.0 %grad_far_kept.1.refs_4_ = f32[768,512]{1,0:T(8,128)S(1)} custom-call(s32[5]{0:T(128)S(1)} %stack.23.refs_0_, bf16[1536,1024]{1,0:T(8,128)(2,1)S(1)} %get-tuple-element.43.refs_1_, f32[8,1024]{1,0:T(8,128)S(1)} %get-tuple-element.44.refs_2_, f32[8,1024]{1,0:T(8,128)S(1)} %get-tuple-element.68.refs_3_, ...), custom_call_target="tpu_custom_call" | custom-call | tf_op jit(solution)/shard_map/grad_far_kept/pallas_call | solution.py:65
  (76 shorter events, 42.2 us)
Async XLA Ops:
  3.2 11.9 %collective-permute-start.1 = (bf16[768,256]{1,0:T(8,128)(2,1)S(1)}, bf16[768,256]{1,0:T(8,128)(2,1)S(1)}, u32[]{:S(2)}, u32[]{:S(2)}) collective-permute-start(bf16[768,256]{1,0:T(8,128)(2,1)S(1)} %constant_dynamic-slice_fusion.1.refs_3_), channel_id=1, source_target_pairs={{0,32},{16,48},{32,64},{48,80},{64,96},{80,112},{96,0},{112,16},{1... | collective-permute-start | bytes 1179656 | tf_op jit(solution)/shard_map/ppermute | solution.py:27
  4.6 19.0 %collective-permute-start.2 = (bf16[768,256]{1,0:T(8,128)(2,1)S(1)}, bf16[768,256]{1,0:T(8,128)(2,1)}, u32[]{:S(2)}, u32[]{:S(2)}) collective-permute-start(bf16[768,256]{1,0:T(8,128)(2,1)S(1)} %constant_dynamic-slice_fusion.refs_4_), channel_id=1, source_target_pairs={{0,32},{16,48},{32,64},{48,80},{64,96},{80,112},{96,0},{112,16},{1... | collective-permute-start | bytes 1179656 | tf_op jit(solution)/shard_map/ppermute | solution.py:27
  5.9 17.8 %collective-permute-start.4 = (bf16[768,256]{1,0:T(8,128)(2,1)S(1)}, bf16[768,256]{1,0:T(8,128)(2,1)}, u32[]{:S(2)}, u32[]{:S(2)}) collective-permute-start(bf16[768,256]{1,0:T(8,128)(2,1)S(1)} %constant_dynamic-slice_fusion.refs_4_), channel_id=1, source_target_pairs={{0,96},{16,112},{32,0},{48,16},{64,32},{80,48},{96,64},{112,80},{1... | collective-permute-start | bytes 1179656 | tf_op jit(solution)/shard_map/ppermute | solution.py:27
  7.3 18.9 %collective-permute-start.8 = (bf16[768,256]{1,0:T(8,128)(2,1)S(1)}, bf16[768,256]{1,0:T(8,128)(2,1)}, u32[]{:S(2)}, u32[]{:S(2)}) collective-permute-start(bf16[768,256]{1,0:T(8,128)(2,1)S(1)} %constant_dynamic-slice_fusion.1.refs_3_), channel_id=1, source_target_pairs={{0,96},{16,112},{32,0},{48,16},{64,32},{80,48},{96,64},{112,80},{1... | collective-permute-start | bytes 1179656 | tf_op jit(solution)/shard_map/ppermute | solution.py:27
  8.4 17.9 %collective-permute-start.6 = (bf16[768,256]{1,0:T(8,128)(2,1)S(1)}, bf16[768,256]{1,0:T(8,128)(2,1)S(1)}, u32[]{:S(2)}, u32[]{:S(2)}) collective-permute-start(bf16[768,256]{1,0:T(8,128)(2,1)S(1)} %constant_dynamic-slice_fusion.1.refs_3_), channel_id=1, source_target_pairs={{0,16},{16,0},{32,48},{48,32},{64,80},{80,64},{96,112},{112,96},{1... | collective-permute-start | bytes 1179656 | tf_op jit(solution)/shard_map/ppermute | solution.py:27
  15.8 11.6 %collective-permute-start.7 = (bf16[768,256]{1,0:T(8,128)(2,1)S(1)}, bf16[768,256]{1,0:T(8,128)(2,1)}, u32[]{:S(2)}, u32[]{:S(2)}) collective-permute-start(bf16[768,256]{1,0:T(8,128)(2,1)S(1)} %constant_dynamic-slice_fusion.refs_4_), channel_id=1, source_target_pairs={{0,16},{16,0},{32,48},{48,32},{64,80},{80,64},{96,112},{112,96},{1... | collective-permute-start | bytes 1179656 | tf_op jit(solution)/shard_map/ppermute | solution.py:27
  23.6 10.9 %collective-permute-start.3 = (bf16[768,256]{1,0:T(8,128)(2,1)S(1)}, bf16[768,256]{1,0:T(8,128)(2,1)S(1)}, u32[]{:S(2)}, u32[]{:S(2)}) collective-permute-start(bf16[768,256]{1,0:T(8,128)(2,1)S(1)} %copy-done.3), channel_id=1, source_target_pairs={{0,32},{16,48},{32,64},{48,80},{64,96},{80,112},{96,0},{112,16},{1... | collective-permute-start | bytes 1179656 | tf_op jit(solution)/shard_map/ppermute | solution.py:27
  23.7 10.8 %collective-permute-start.5 = (bf16[768,256]{1,0:T(8,128)(2,1)}, bf16[768,256]{1,0:T(8,128)(2,1)S(1)}, u32[]{:S(2)}, u32[]{:S(2)}) collective-permute-start(bf16[768,256]{1,0:T(8,128)(2,1)} %collective-permute-done.4.refs_8_), channel_id=1, source_target_pairs={{0,96},{16,112},{32,0},{48,16},{64,32},{80,48},{96,64},{112,80},{1... | collective-permute-start | bytes 1179656 | tf_op jit(solution)/shard_map/ppermute | solution.py:27
  32.9 17.8 %collective-permute-start.10 = (bf16[1536,256]{1,0:T(8,128)(2,1)S(1)}, bf16[1536,256]{1,0:T(8,128)(2,1)S(1)}, u32[]{:S(2)}, u32[]{:S(2)}) collective-permute-start(bf16[1536,256]{1,0:T(8,128)(2,1)S(1)} %join.2.refs_2_), channel_id=1, source_target_pairs={{0,96},{16,112},{32,0},{48,16},{64,32},{80,48},{96,64},{112,80},{1... | collective-permute-start | bytes 2359304 | tf_op jit(solution)/shard_map/ppermute | solution.py:27
  33.0 18.3 %collective-permute-start.9 = (bf16[1536,256]{1,0:T(8,128)(2,1)S(1)}, bf16[1536,256]{1,0:T(8,128)(2,1)S(1)}, u32[]{:S(2)}, u32[]{:S(2)}) collective-permute-start(bf16[1536,256]{1,0:T(8,128)(2,1)S(1)} %join.2.refs_2_), channel_id=1, source_target_pairs={{0,32},{16,48},{32,64},{48,80},{64,96},{80,112},{96,0},{112,16},{1... | collective-permute-start | bytes 2359304 | tf_op jit(solution)/shard_map/ppermute | solution.py:27
  34.5 16.7 %collective-permute-start.11 = (bf16[1536,256]{1,0:T(8,128)(2,1)S(1)}, bf16[1536,256]{1,0:T(8,128)(2,1)S(1)}, u32[]{:S(2)}, u32[]{:S(2)}) collective-permute-start(bf16[1536,256]{1,0:T(8,128)(2,1)S(1)} %join.3.refs_3_), channel_id=1, source_target_pairs={{0,16},{16,0},{32,48},{48,32},{64,80},{80,64},{96,112},{112,96},{1... | collective-permute-start | bytes 2359304 | tf_op jit(solution)/shard_map/ppermute | solution.py:27
  36.3 7.1 %collective-permute-start.15 = (bf16[144,1024]{1,0:T(8,128)(2,1)S(1)}, bf16[144,1024]{1,0:T(8,128)(2,1)S(1)}, u32[]{:S(2)}, u32[]{:S(2)}) collective-permute-start(bf16[144,1024]{1,0:T(8,128)(2,1)S(1)} %get-tuple-element.51), channel_id=1, source_target_pairs={{0,2},{1,3},{2,4},{3,5},{4,6},{5,7},{6,0},{7,1},{8,10},{9,11},{10,... | collective-permute-start | bytes 884744 | tf_op jit(solution)/shard_map/ppermute | solution.py:47
  43.5 15.5 %collective-permute-start.17 = (bf16[144,1024]{1,0:T(8,128)(2,1)S(1)}, bf16[144,1024]{1,0:T(8,128)(2,1)S(1)}, u32[]{:S(2)}, u32[]{:S(2)}) collective-permute-start(bf16[144,1024]{1,0:T(8,128)(2,1)S(1)} %get-tuple-element.56), channel_id=1, source_target_pairs={{0,4},{1,5},{2,6},{3,7},{4,0},{5,1},{6,2},{7,3},{8,12},{9,13},{10,... | collective-permute-start | bytes 884744 | tf_op jit(solution)/shard_map/ppermute | solution.py:47
  55.0 9.0 %collective-permute-start.12 = (bf16[144,1024]{1,0:T(8,128)(2,1)S(1)}, bf16[144,1024]{1,0:T(8,128)(2,1)S(1)}, u32[]{:S(2)}, u32[]{:S(2)}) collective-permute-start(bf16[144,1024]{1,0:T(8,128)(2,1)S(1)} %get-tuple-element.47), channel_id=1, source_target_pairs={{0,2},{1,3},{2,4},{3,5},{4,6},{5,7},{6,0},{7,1},{8,10},{9,11},{10,... | collective-permute-start | bytes 884744 | tf_op jit(solution)/shard_map/ppermute | solution.py:47
  56.4 12.5 %collective-permute-start.13 = (bf16[144,1024]{1,0:T(8,128)(2,1)S(1)}, bf16[144,1024]{1,0:T(8,128)(2,1)S(1)}, u32[]{:S(2)}, u32[]{:S(2)}) collective-permute-start(bf16[144,1024]{1,0:T(8,128)(2,1)S(1)} %get-tuple-element.48), channel_id=1, source_target_pairs={{0,4},{1,5},{2,6},{3,7},{4,0},{5,1},{6,2},{7,3},{8,12},{9,13},{10,... | collective-permute-start | bytes 884744 | tf_op jit(solution)/shard_map/ppermute | solution.py:47
  59.7 12.5 %collective-permute-start.18 = (bf16[160,1024]{1,0:T(8,128)(2,1)S(1)}, bf16[160,1024]{1,0:T(8,128)(2,1)S(1)}, u32[]{:S(2)}, u32[]{:S(2)}) collective-permute-start(bf16[160,1024]{1,0:T(8,128)(2,1)S(1)} %get-tuple-element.63), channel_id=1, source_target_pairs={{0,8},{1,9},{2,10},{3,11},{4,12},{5,13},{6,14},{7,15},{8,0},{9,1},... | collective-permute-start | bytes 983048 | tf_op jit(solution)/shard_map/ppermute | solution.py:56
  62.9 7.3 %collective-permute-start.14 = (bf16[144,1024]{1,0:T(8,128)(2,1)S(1)}, bf16[144,1024]{1,0:T(8,128)(2,1)S(1)}, u32[]{:S(2)}, u32[]{:S(2)}) collective-permute-start(bf16[144,1024]{1,0:T(8,128)(2,1)S(1)} %get-tuple-element.49), channel_id=1, source_target_pairs={{0,6},{1,7},{2,0},{3,1},{4,2},{5,3},{6,4},{7,5},{8,14},{9,15},{10,... | collective-permute-start | bytes 884744 | tf_op jit(solution)/shard_map/ppermute | solution.py:47
  70.9 9.3 %collective-permute-start.19 = (bf16[144,1024]{1,0:T(8,128)(2,1)S(1)}, bf16[144,1024]{1,0:T(8,128)(2,1)S(1)}, u32[]{:S(2)}, u32[]{:S(2)}) collective-permute-start(bf16[144,1024]{1,0:T(8,128)(2,1)S(1)} %get-tuple-element.65), channel_id=1, source_target_pairs={{0,8},{1,9},{2,10},{3,11},{4,12},{5,13},{6,14},{7,15},{8,0},{9,1},... | collective-permute-start | bytes 884744 | tf_op jit(solution)/shard_map/ppermute | solution.py:56
  73.6 8.9 %collective-permute-start.22 = (bf16[128,1024]{1,0:T(8,128)(2,1)S(1)}, bf16[128,1024]{1,0:T(8,128)(2,1)S(1)}, u32[]{:S(2)}, u32[]{:S(2)}) collective-permute-start(bf16[128,1024]{1,0:T(8,128)(2,1)S(1)} %get-tuple-element.67.refs_4_), channel_id=1, source_target_pairs={{0,6},{1,7},{2,0},{3,1},{4,2},{5,3},{6,4},{7,5},{8,14},{9,15},{10,... | collective-permute-start | bytes 786440 | tf_op jit(solution)/shard_map/ppermute | solution.py:47
  80.2 10.1 %collective-permute-start.20 = (bf16[128,1024]{1,0:T(8,128)(2,1)S(1)}, bf16[128,1024]{1,0:T(8,128)(2,1)S(1)}, u32[]{:S(2)}, u32[]{:S(2)}) collective-permute-start(bf16[128,1024]{1,0:T(8,128)(2,1)S(1)} %get-tuple-element.67.refs_4_), channel_id=1, source_target_pairs={{0,2},{1,3},{2,4},{3,5},{4,6},{5,7},{6,0},{7,1},{8,10},{9,11},{10,... | collective-permute-start | bytes 786440 | tf_op jit(solution)/shard_map/ppermute | solution.py:47
  91.7 12.9 %collective-permute-start.25 = (bf16[128,1024]{1,0:T(8,128)(2,1)S(1)}, bf16[128,1024]{1,0:T(8,128)(2,1)S(1)}, u32[]{:S(2)}, u32[]{:S(2)}) collective-permute-start(bf16[128,1024]{1,0:T(8,128)(2,1)S(1)} %get-tuple-element.69.refs_3_.refs_4_), channel_id=1, source_target_pairs={{0,6},{1,7},{2,0},{3,1},{4,2},{5,3},{6,4},{7,5},{8,14},{9,15},{10,... | collective-permute-start | bytes 786440 | tf_op jit(solution)/shard_map/ppermute | solution.py:47
  92.0 12.7 %collective-permute-start.24 = (bf16[128,1024]{1,0:T(8,128)(2,1)S(1)}, bf16[128,1024]{1,0:T(8,128)(2,1)S(1)}, u32[]{:S(2)}, u32[]{:S(2)}) collective-permute-start(bf16[128,1024]{1,0:T(8,128)(2,1)S(1)} %get-tuple-element.69.refs_3_.refs_4_), channel_id=1, source_target_pairs={{0,4},{1,5},{2,6},{3,7},{4,0},{5,1},{6,2},{7,3},{8,12},{9,13},{10,... | collective-permute-start | bytes 786440 | tf_op jit(solution)/shard_map/ppermute | solution.py:47
  94.3 10.5 %collective-permute-start.23 = (bf16[128,1024]{1,0:T(8,128)(2,1)S(1)}, bf16[128,1024]{1,0:T(8,128)(2,1)S(1)}, u32[]{:S(2)}, u32[]{:S(2)}) collective-permute-start(bf16[128,1024]{1,0:T(8,128)(2,1)S(1)} %get-tuple-element.69.refs_3_.refs_4_), channel_id=1, source_target_pairs={{0,2},{1,3},{2,4},{3,5},{4,6},{5,7},{6,0},{7,1},{8,10},{9,11},{10,... | collective-permute-start | bytes 786440 | tf_op jit(solution)/shard_map/ppermute | solution.py:47
  106.7 15.2 %collective-permute-start.28 = (bf16[768,512]{1,0:T(8,128)(2,1)S(1)}, bf16[768,512]{1,0:T(8,128)(2,1)S(1)}, u32[]{:S(2)}, u32[]{:S(2)}) collective-permute-start(bf16[768,512]{1,0:T(8,128)(2,1)S(1)} %grad_far_sent.1.refs_10_), channel_id=1, source_target_pairs={{0,1},{1,0},{2,3},{3,2},{4,5},{5,4},{6,7},{7,6},{8,9},{9,8},{10,11... | collective-permute-start | bytes 2359304 | tf_op jit(solution)/shard_map/ppermute | solution.py:39
  (15 other events, 84.2 us)

commit v6 on v5

--- a/solution.py
+++ b/solution.py
@@ -17,6 +17,7 @@
 GRAD_SCALE = BATCH / (16.0 * (BATCH - 1))
 
 QUARTER = FEATS // 4
+UPPER = QUARTER // 2
 VMEM = pl.BlockSpec(memory_space=pltpu.VMEM)
 SMEM = pl.BlockSpec(memory_space=pltpu.SMEM)
 ANY = pl.BlockSpec(memory_space=pl.ANY)
@@ -265,7 +266,7 @@
 
 
 def combine_y_kernel(
-    with_rows, place, parts, own, one, two, three_on, plane, message, local, *row_local
+    with_rows, place, parts, own, one, two, three_on, plane, upper, message, local, *row_local
 ):
     width = own.shape[1]
     columns = jnp.zeros((4, width), F32)
@@ -290,7 +291,8 @@
         return [high, middle, low], high + middle + low
 
     plane[...] = total.astype(BF16)
-    message[0:QUARTER, :] = total.astype(BF16)
+    upper[...] = total[0:UPPER].astype(BF16)
+    message[0:QUARTER - UPPER, :] = total[UPPER:].astype(BF16)
     lines, local[0:4, :] = rounded(columns)
     if with_rows:
         row_lines, row_local[0][0:4, :] = rounded(rows)
@@ -298,13 +300,14 @@
         part_lines, _ = rounded(parts[0:1, :])
         lines = lines + padded(row_lines + square_lines, width) + padded(part_lines, width)
     block = filled(lines, width)
-    message[QUARTER:QUARTER + block.shape[0], :] = block.astype(BF16)
+    message[QUARTER - UPPER:, :] = block.astype(BF16)
 
 
 def combine_y(place, parts, pieces, with_rows, name, after=()):
     width = pieces[0].shape[1]
-    rows = QUARTER + (2 if with_rows else 1) * STAT_ROWS
-    outs = [shape((QUARTER, width), BF16), shape((rows, width), BF16), shape((8, width), F32)]
+    rows = QUARTER - UPPER + (2 if with_rows else 1) * STAT_ROWS
+    outs = [shape((QUARTER, width), BF16), shape((UPPER, width), BF16)]
+    outs += [shape((rows, width), BF16), shape((8, width), F32)]
     outs += [shape((8, FEATS), F32)] if with_rows else []
     return call(
         functools.partial(combine_y_kernel, with_rows), outs, [place, parts] + pieces, [], name, after
@@ -317,9 +320,9 @@
 
 
 def combine_z_kernel(
-    with_rows, place, plane, local, rows, received, parts, masked, part, means, *more
+    with_rows, place, plane, local, rows, upper, received, parts, masked, part, means, *more
 ):
-    stats = received[QUARTER:, :].astype(F32)
+    stats = received[QUARTER - UPPER:, :].astype(F32)
     theirs = stats[0:4] + stats[4:8] + stats[8:12]
     col_off, col_mean = spread_out(all_chips(place, local[0:4, :], theirs))
     means[...] = jnp.broadcast_to(col_mean, means.shape)
@@ -338,7 +341,8 @@
         row_stats[...] = jnp.concatenate([row_mean, spread, jnp.zeros((6, FEATS), F32)], axis=0)
     block = pl.multiple_of(place[2] * QUARTER, QUARTER)
     term = mean_term(row_offsets[:, pl.ds(block, QUARTER)], col_off)
-    covar = plane[...].astype(F32) + received[0:QUARTER, :].astype(F32)
+    other = [upper[...].astype(F32), received[0:QUARTER - UPPER, :].astype(F32)]
+    covar = plane[...].astype(F32) + jnp.concatenate(other, axis=0)
     covar = (covar + term) / (BATCH - 1)
     if with_rows:
         row_ids = place[2] * QUARTER + lax.broadcasted_iota(jnp.int32, covar.shape, 0)
@@ -354,11 +358,11 @@
     masked[0:QUARTER, :] = covar.astype(BF16)
 
 
-def combine_z(place, plane, local, rows, received, parts, with_rows, name, after=()):
+def combine_z(place, plane, local, rows, upper, received, parts, with_rows, name, after=()):
     width = plane.shape[1]
     outs = [shape((QUARTER, width), BF16), shape((8, 128), F32), shape((8, width), F32)]
     outs += [shape((8, FEATS), F32)] * 2 if with_rows else []
-    ins = [place, plane, local, rows, received, parts]
+    ins = [place, plane, local, rows, upper, received, parts]
     return call(functools.partial(combine_z_kernel, with_rows), outs, ins, [], name, after)
 
 
@@ -372,8 +376,8 @@
 
 def loss_kernel(one, two, three_on, four, out):
     total = (one[...] + two[...]) + (three_on[...] + four[...])
-    loss = total[:, 0:1] + 25.0 * (total[:, 1:2] / BATCH + total[:, 2:3])
-    out[...] = jnp.broadcast_to(loss / (8 * FEATS), out.shape)
+    loss = total[0:1, 0:1] + 25.0 * (total[0:1, 1:2] / BATCH + total[0:1, 2:3])
+    out[...] = loss / (8 * FEATS)
 
 
 def flip(parts, row_bits, col_bits):
@@ -393,10 +397,10 @@
     return call(add_kernel, [shape((8, 128), F32)], ins, [], "pair_sum", after)[0]
 
 
-def four_sum(parts, first, second, body, name, after=()):
+def four_sum(parts, first, second, body, name, out=(8, 128), after=()):
     both = (first[0] | second[0], first[1] | second[1])
     ins = [parts] + [flip(parts, *bits) for bits in (first, second, both)]
-    return call(body, [shape((8, 128), F32)], ins, [], name, after)[0]
+    return call(body, [shape(out, F32)], ins, [], name, after)[0]
 
 
 def shift_term(stats, means, masked):
@@ -483,23 +487,23 @@
     far_sums, far_columns, far_stats = partial_sums(
         place, rows_t, own_stats, far, False, "partial_far"
     )
+    plane, upper, message, local, row_local = combine_y(
+        place, parts, near_sums, True, "combine_y_near", [far_sums[0]]
+    )
+    *far_sums, plane = lax.optimization_barrier((*far_sums, plane))
     for d in (1, 3, 2):
         far_sums[d] = shift_y(far_sums[d], d)
-
-    plane, message, local, row_local = combine_y(
-        place, parts, near_sums, True, "combine_y_near", [far_sums[0]]
-    )
-    far_plane, far_message, far_local = combine_y(
-        place, parts, far_sums, False, "combine_y_far", [plane]
-    )
     near_masked, parts, near_means, row_offsets, row_stats = combine_z(
-        place, plane, local, row_local, swap_z_hi(message), parts, True,
-        "combine_z_near",
-        [far_plane],
+        place, plane, local, row_local, swap_z_hi(upper), swap_z_hi(message), parts, True,
+        "combine_z_near", [far_sums[1]],
     )
     near_pieces = sent_round(near_masked)
+    far_plane, far_upper, far_message, far_local = combine_y(
+        place, parts, far_sums, False, "combine_y_far", [near_masked]
+    )
     far_masked, parts, far_means = combine_z(
-        place, far_plane, far_local, row_offsets, swap_z_hi(far_message), parts, False,
+        place, far_plane, far_local, row_offsets, swap_z_hi(far_upper), swap_z_hi(far_message),
+        parts, False,
         "combine_z_far", near_pieces[1:],
     )
     far_pieces = sent_round(far_masked)
@@ -519,7 +523,7 @@
         place, far_inputs, far_pieces, grads, 0, IMAGES, F32, "grad_far_kept", [outgoing], base
     )
     parts = four_sum(parts, (1, 0), (0, 1), add_four_kernel, "four_sum")
-    total_loss = four_sum(parts, (0, 2), (0, 4), loss_kernel, "loss", [kept])
+    total_loss = four_sum(parts, (0, 2), (0, 4), loss_kernel, "loss", (1, 1), [kept])
     return (kept + GRAD_SCALE * incoming.astype(F32), total_loss[0, 0])
 
 

time: 125 us -> 120 us (0.960)
  waiting for transfers between devices: 39.4 us -> 31.7 us
  starting transfers between devices: 55.5 us -> 58.6 us
    ppermute x12, waiting for transfers between devices: 20.8 us -> 4.45 us  [shift_y(): return lax.ppermute(block, 'col', pairs)]
    ppermute x2 -> x4, waiting for transfers between devices: 0.01 us -> 9.43 us  [swap_z_hi(): return lax.ppermute(block, 'col', [(i, i ^ 8) for i in range(16)])]
    ppermute x2, starting transfers between devices: 5.68 us -> 9.96 us  [swap_cores(): return lax.ppermute(block, 'col', [(i, i ^ 1) for i in range(16)])]
    ppermute x3, starting transfers between devices: 6.8 us -> 4.27 us  [flip(): return lax.ppermute(parts, 'row', [(i, i ^ row_bits) for i in range(8)])]
    ppermute x2 -> x4, starting transfers between devices: 4.47 us -> 6.14 us  [swap_z_hi(): return lax.ppermute(block, 'col', [(i, i ^ 8) for i in range(16)])]
  transfers between devices with their start and end apart: 35 -> 37, of which waited for: 16 -> 13; matrix products, arithmetic and copies ran while one was open for 1% -> 1% of each run, Pallas kernels for 16% -> 16%
where the time goes in v6:
time: 120 us; the launch traced here: 119 us
  starting transfers between devices  58.6 us (49%)
  waiting for transfers between devices  31.7 us (26%)
  Pallas kernels  23.2 us (19%)
  local copies, waits for them, and re-layouts  2.88 us (2%)
  other arithmetic  1.41 us (1%)
    pallas_call x17, Pallas kernels, call(): pl.pallas_call(kernel, out_shape=tuple(outs), in_specs=[SMEM if a.dtype =...  23.2 us
    ppermute x12, starting transfers between devices, shift_y(): return lax.ppermute(block, 'col', pairs)  19.6 us
    ppermute x11, starting transfers between devices, shift_row(): return lax.ppermute(block, 'row', pairs)  14.5 us
    ppermute x11, waiting for transfers between devices, shift_row(): return lax.ppermute(block, 'row', pairs)  14.5 us
    ppermute x2, starting transfers between devices, swap_cores(): return lax.ppermute(block, 'col', [(i, i ^ 1) for i in range(16)])  9.96 us
    ppermute x4, waiting for transfers between devices, swap_z_hi(): return lax.ppermute(block, 'col', [(i, i ^ 8) for i in range(16)])  9.43 us
    ppermute x4, starting transfers between devices, swap_z_hi(): return lax.ppermute(block, 'col', [(i, i ^ 8) for i in range(16)])  6.14 us
    ppermute x12, waiting for transfers between devices, shift_y(): return lax.ppermute(block, 'col', pairs)  4.45 us
  transfers between devices with their start and end apart: 37, of which 13 were waited for; matrix products, arithmetic and copies ran while one was open for 1% of the time, Pallas kernels for 16%

profile of v6, /device:TPU:1, one launch (start us, length us, event | category | flops | bytes accessed | tf_op | source)
XLA Modules:
  0.0 118.7 jit_solution(4723782185300930605)
XLA Ops:
  10.0 5.0 %collective-permute-done.1.refs_3_.refs_5_ = bf16[768,256]{1,0:T(8,128)(2,1)S(1)} collective-permute-done((bf16[768,256]{1,0:T(8,128)(2,1)S(1)}, bf16[768,256]{1,0:T(8,128)(2,1)S(1)}, u32[]{:S(2)}, u32[]{:S(2)}) %collective-permute-start.1) | collective-permute-done | bytes 393248 | tf_op jit(solution)/shard_map/ppermute | solution.py:28
  15.8 1.7 %collective-permute-start.7 = (bf16[768,256]{1,0:T(8,128)(2,1)S(1)}, bf16[768,256]{1,0:T(8,128)(2,1)}, u32[]{:S(2)}, u32[]{:S(2)}) collective-permute-start(bf16[768,256]{1,0:T(8,128)(2,1)S(1)} %constant_dynamic-slice_fusion.refs_4_), channel_id=1, source_target_pairs={{0,16},{16,0},{32,48},{48,32},{64,80},{80,64},{96,112},{112,96},{1... | collective-permute-start | bytes 1179656 | tf_op jit(solution)/shard_map/ppermute | solution.py:28
  18.6 1.8 %center_own.1 = (bf16[512,1536]{1,0:T(8,128)(2,1)S(1)}, f32[8,512]{1,0:T(8,128)S(1)}, f32[8,128]{1,0:T(8,128)S(1)}) custom-call(bf16[768,512]{1,0:T(8,128)(2,1)S(1)} %copy-done, bf16[768,512]{1,0:T(8,128)(2,1)S(1)} %collective-permute-done.refs_1_, bf16[768,512]{1,0:T(8,128)(2,1)S(1)} %copy-done.1, bf16[768,256]{1,0:T(8,128)(2,1)S(1)} %copy-done.3), custom_call_target="tpu_custom_call" | custom-call | tf_op jit(solution)/shard_map/center_own/pallas_call | solution.py:66
  20.4 3.2 %collective-permute-done.2.refs_6_ = bf16[768,256]{1,0:T(8,128)(2,1)} collective-permute-done((bf16[768,256]{1,0:T(8,128)(2,1)S(1)}, bf16[768,256]{1,0:T(8,128)(2,1)}, u32[]{:S(2)}, u32[]{:S(2)}) %collective-permute-start.2) | collective-permute-done | bytes 393248 | tf_op jit(solution)/shard_map/ppermute | solution.py:28
  23.7 2.6 %collective-permute-start.5 = (bf16[768,256]{1,0:T(8,128)(2,1)}, bf16[768,256]{1,0:T(8,128)(2,1)S(1)}, u32[]{:S(2)}, u32[]{:S(2)}) collective-permute-start(bf16[768,256]{1,0:T(8,128)(2,1)} %collective-permute-done.4.refs_8_), channel_id=1, source_target_pairs={{0,96},{16,112},{32,0},{48,16},{64,32},{80,48},{96,64},{112,80},{1... | collective-permute-start | bytes 1179656 | tf_op jit(solution)/shard_map/ppermute | solution.py:28
  27.3 4.5 %partial_near.1 = (f32[144,1024]{1,0:T(8,128)S(1)}, bf16[144,1024]{1,0:T(8,128)(2,1)S(1)}, bf16[144,1024]{1,0:T(8,128)(2,1)S(1)}, bf16[144,1024]{1,0:T(8,128)(2,...) custom-call(s32[5]{0:T(128)S(1)} %stack.23.refs_0_, bf16[512,1536]{1,0:T(8,128)(2,1)S(1)} %get-tuple-element.45.refs_1_, ...), custom_call_target="tpu_custom_call" | custom-call | flops 32212254720 | tf_op jit(solution)/shard_map/partial_near/pallas_call | solution.py:66
  34.5 1.8 %collective-permute-start.11 = (bf16[1536,256]{1,0:T(8,128)(2,1)S(1)}, bf16[1536,256]{1,0:T(8,128)(2,1)S(1)}, u32[]{:S(2)}, u32[]{:S(2)}) collective-permute-start(bf16[1536,256]{1,0:T(8,128)(2,1)S(1)} %join.3.refs_3_), channel_id=1, source_target_pairs={{0,16},{16,0},{32,48},{48,32},{64,80},{80,64},{96,112},{112,96},{1... | collective-permute-start | bytes 2359304 | tf_op jit(solution)/shard_map/ppermute | solution.py:28
  39.0 4.4 %collective-permute-done.12.refs_3_ = bf16[144,1024]{1,0:T(8,128)(2,1)S(1)} collective-permute-done((bf16[144,1024]{1,0:T(8,128)(2,1)S(1)}, bf16[144,1024]{1,0:T(8,128)(2,1)S(1)}, u32[]{:S(2)}, u32[]{:S(2)}) %collective-permute-start.12) | collective-permute-done | bytes 294944 | tf_op jit(solution)/shard_map/ppermute | solution.py:48
  43.5 2.6 %collective-permute-start.14 = (bf16[144,1024]{1,0:T(8,128)(2,1)S(1)}, bf16[144,1024]{1,0:T(8,128)(2,1)S(1)}, u32[]{:S(2)}, u32[]{:S(2)}) collective-permute-start(bf16[144,1024]{1,0:T(8,128)(2,1)S(1)} %get-tuple-element.63), channel_id=1, source_target_pairs={{0,4},{1,5},{2,6},{3,7},{4,0},{5,1},{6,2},{7,3},{8,12},{9,13},{10,... | collective-permute-start | bytes 884744 | tf_op jit(solution)/shard_map/ppermute | solution.py:48
  46.1 4.6 %collective-permute-done.10.refs_5_ = bf16[1536,256]{1,0:T(8,128)(2,1)S(1)} collective-permute-done((bf16[1536,256]{1,0:T(8,128)(2,1)S(1)}, bf16[1536,256]{1,0:T(8,128)(2,1)S(1)}, u32[]{:S(2)}, u32[]{:S(2)}) %collective-permute-start.10) | collective-permute-done | bytes 786464 | tf_op jit(solution)/shard_map/ppermute | solution.py:28
  51.2 3.7 %partial_far.1 = (f32[144,1024]{1,0:T(8,128)S(1)}, bf16[144,1024]{1,0:T(8,128)(2,1)S(1)}, bf16[144,1024]{1,0:T(8,128)(2,1)S(1)}, bf16[144,1024]{1,0:T(8,128)(2,1...) custom-call(s32[5]{0:T(128)S(1)} %stack.23.refs_0_, bf16[512,1536]{1,0:T(8,128)(2,1)S(1)} %get-tuple-element.45.refs_1_, ...), custom_call_target="tpu_custom_call" | custom-call | flops 32212254720 | tf_op jit(solution)/shard_map/partial_far/pallas_call | solution.py:66
  57.1 3.1 %collective-permute-start.16 = (bf16[96,1024]{1,0:T(8,128)(2,1)S(1)}, bf16[96,1024]{1,0:T(8,128)(2,1)S(1)}, u32[]{:S(2)}, u32[]{:S(2)}) collective-permute-start(bf16[96,1024]{1,0:T(8,128)(2,1)S(1)} %get-tuple-element.70), channel_id=1, source_target_pairs={{0,8},{1,9},{2,10},{3,11},{4,12},{5,13},{6,14},{7,15},{8,0},{9,1},... | collective-permute-start | bytes 589832 | tf_op jit(solution)/shard_map/ppermute | solution.py:57
  60.2 2.6 %collective-permute-start.18 = (bf16[144,1024]{1,0:T(8,128)(2,1)S(1)}, bf16[144,1024]{1,0:T(8,128)(2,1)S(1)}, u32[]{:S(2)}, u32[]{:S(2)}) collective-permute-start(bf16[144,1024]{1,0:T(8,128)(2,1)S(1)} %get-tuple-element.74), channel_id=1, source_target_pairs={{0,4},{1,5},{2,6},{3,7},{4,0},{5,1},{6,2},{7,3},{8,12},{9,13},{10,... | collective-permute-start | bytes 884744 | tf_op jit(solution)/shard_map/ppermute | solution.py:48
  63.9 5.3 %collective-permute-done.15.refs_4_ = bf16[64,1024]{1,0:T(8,128)(2,1)S(1)} collective-permute-done((bf16[64,1024]{1,0:T(8,128)(2,1)S(1)}, bf16[64,1024]{1,0:T(8,128)(2,1)S(1)}, u32[]{:S(2)}, u32[]{:S(2)}) %collective-permute-start.15) | collective-permute-done | bytes 131104 | tf_op jit(solution)/shard_map/ppermute | solution.py:57
  74.4 3.0 %collective-permute-start.20 = (bf16[64,1024]{1,0:T(8,128)(2,1)S(1)}, bf16[64,1024]{1,0:T(8,128)(2,1)S(1)}, u32[]{:S(2)}, u32[]{:S(2)}) collective-permute-start(bf16[64,1024]{1,0:T(8,128)(2,1)S(1)} %get-tuple-element.80), channel_id=1, source_target_pairs={{0,8},{1,9},{2,10},{3,11},{4,12},{5,13},{6,14},{7,15},{8,0},{9,1},... | collective-permute-start | bytes 393224 | tf_op jit(solution)/shard_map/ppermute | solution.py:57
  77.3 4.1 %collective-permute-done.20.refs_4_ = bf16[64,1024]{1,0:T(8,128)(2,1)S(1)} collective-permute-done((bf16[64,1024]{1,0:T(8,128)(2,1)S(1)}, bf16[64,1024]{1,0:T(8,128)(2,1)S(1)}, u32[]{:S(2)}, u32[]{:S(2)}) %collective-permute-start.20) | collective-permute-done | bytes 131104 | tf_op jit(solution)/shard_map/ppermute | solution.py:57
  82.9 4.3 %collective-permute-start.27 = (bf16[128,1024]{1,0:T(8,128)(2,1)S(1)}, bf16[128,1024]{1,0:T(8,128)(2,1)S(1)}, u32[]{:S(2)}, u32[]{:S(2)}) collective-permute-start(bf16[128,1024]{1,0:T(8,128)(2,1)S(1)} %get-tuple-element.83.refs_3_.refs_4_), channel_id=1, source_target_pairs={{0,6},{1,7},{2,0},{3,1},{4,2},{5,3},{6,4},{7,5},{8,14},{9,15},{10,... | collective-permute-start | bytes 786440 | tf_op jit(solution)/shard_map/ppermute | solution.py:48
  87.2 1.9 %collective-permute-start.26 = (bf16[128,1024]{1,0:T(8,128)(2,1)S(1)}, bf16[128,1024]{1,0:T(8,128)(2,1)S(1)}, u32[]{:S(2)}, u32[]{:S(2)}) collective-permute-start(bf16[128,1024]{1,0:T(8,128)(2,1)S(1)} %get-tuple-element.83.refs_3_.refs_4_), channel_id=1, source_target_pairs={{0,4},{1,5},{2,6},{3,7},{4,0},{5,1},{6,2},{7,3},{8,12},{9,13},{10,... | collective-permute-start | bytes 786440 | tf_op jit(solution)/shard_map/ppermute | solution.py:48
  91.6 2.3 %collective-permute-start.29 = (f32[8,128]{1,0:T(8,128)S(1)}, f32[8,128]{1,0:T(8,128)S(1)}, u32[]{:S(2)}, u32[]{:S(2)}) collective-permute-start(f32[8,128]{1,0:T(8,128)S(1)} %pair_sum.2.refs_0_), channel_id=1, source_target_pairs={{0,64},{16,80},{32,96},{48,112},{64,0},{80,16},{96,32},{112,48},{1... | collective-permute-start | bytes 12296 | tf_op jit(solution)/shard_map/ppermute | solution.py:387
  94.3 2.8 %grad_near.1.refs_8_ = f32[1536,512]{1,0:T(8,128)S(1)} custom-call(s32[5]{0:T(128)S(1)} %stack.23.refs_0_, bf16[1536,1024]{1,0:T(8,128)(2,1)S(1)} %get-tuple-element.84.refs_1_, f32[8,1024]{1,0:T(8,128)S(1)} %get-tuple-element.49.refs_2_, f32[8,1024]{1,0:T(8,128)S(1)} %get-tuple-element.85.refs_3_, bf16[128,1024]{1,0:T(8,128)(2,1)S(1)} %get-tuple-element.76.refs_6_.refs_4_, ...), custom_call_target="tpu_custom_call" | custom-call | tf_op jit(solution)/shard_map/grad_near/pallas_call | solution.py:66
  97.2 2.0 %grad_far_sent.1.refs_10_ = bf16[768,512]{1,0:T(8,128)(2,1)S(1)} custom-call(s32[5]{0:T(128)S(1)} %stack.23.refs_0_, bf16[1536,1024]{1,0:T(8,128)(2,1)S(1)} %get-tuple-element.50.refs_1_, f32[8,1024]{1,0:T(8,128)S(1)} %get-tuple-element.51.refs_2_, f32[8,1024]{1,0:T(8,128)S(1)} %get-tuple-element.82.refs_3_, ...), custom_call_target="tpu_custom_call" | custom-call | tf_op jit(solution)/shard_map/grad_far_sent/pallas_call | solution.py:66
  99.1 8.5 %collective-permute-start.30 = (bf16[768,512]{1,0:T(8,128)(2,1)S(1)}, bf16[768,512]{1,0:T(8,128)(2,1)S(1)}, u32[]{:S(2)}, u32[]{:S(2)}) collective-permute-start(bf16[768,512]{1,0:T(8,128)(2,1)S(1)} %grad_far_sent.1.refs_10_), channel_id=1, source_target_pairs={{0,1},{1,0},{2,3},{3,2},{4,5},{5,4},{6,7},{7,6},{8,9},{9,8},{10,11... | collective-permute-start | bytes 2359304 | tf_op jit(solution)/shard_map/ppermute | solution.py:40
  112.4 1.8 %collective-permute-start.35 = (f32[8,128]{1,0:T(8,128)S(1)}, f32[8,128]{1,0:T(8,128)S(1)}, u32[]{:S(2)}, u32[]{:S(2)}) collective-permute-start(f32[8,128]{1,0:T(8,128)S(1)} %four_sum.1.refs_0_), channel_id=1, source_target_pairs={{0,4},{1,5},{2,6},{3,7},{4,0},{5,1},{6,2},{7,3},{8,12},{9,13},{10,... | collective-permute-start | bytes 12296 | tf_op jit(solution)/shard_map/ppermute | solution.py:385
  114.1 2.0 %grad_far_kept.1.refs_4_ = f32[768,512]{1,0:T(8,128)S(1)} custom-call(s32[5]{0:T(128)S(1)} %stack.23.refs_0_, bf16[1536,1024]{1,0:T(8,128)(2,1)S(1)} %get-tuple-element.50.refs_1_, f32[8,1024]{1,0:T(8,128)S(1)} %get-tuple-element.51.refs_2_, f32[8,1024]{1,0:T(8,128)S(1)} %get-tuple-element.82.refs_3_, ...), custom_call_target="tpu_custom_call" | custom-call | tf_op jit(solution)/shard_map/grad_far_kept/pallas_call | solution.py:66
  (79 shorter events, 38.2 us)
Async XLA Ops:
  3.2 11.9 %collective-permute-start.1 = (bf16[768,256]{1,0:T(8,128)(2,1)S(1)}, bf16[768,256]{1,0:T(8,128)(2,1)S(1)}, u32[]{:S(2)}, u32[]{:S(2)}) collective-permute-start(bf16[768,256]{1,0:T(8,128)(2,1)S(1)} %constant_dynamic-slice_fusion.1.refs_3_), channel_id=1, source_target_pairs={{0,32},{16,48},{32,64},{48,80},{64,96},{80,112},{96,0},{112,16},{1... | collective-permute-start | bytes 1179656 | tf_op jit(solution)/shard_map/ppermute | solution.py:28
  4.6 19.0 %collective-permute-start.2 = (bf16[768,256]{1,0:T(8,128)(2,1)S(1)}, bf16[768,256]{1,0:T(8,128)(2,1)}, u32[]{:S(2)}, u32[]{:S(2)}) collective-permute-start(bf16[768,256]{1,0:T(8,128)(2,1)S(1)} %constant_dynamic-slice_fusion.refs_4_), channel_id=1, source_target_pairs={{0,32},{16,48},{32,64},{48,80},{64,96},{80,112},{96,0},{112,16},{1... | collective-permute-start | bytes 1179656 | tf_op jit(solution)/shard_map/ppermute | solution.py:28
  5.9 17.8 %collective-permute-start.4 = (bf16[768,256]{1,0:T(8,128)(2,1)S(1)}, bf16[768,256]{1,0:T(8,128)(2,1)}, u32[]{:S(2)}, u32[]{:S(2)}) collective-permute-start(bf16[768,256]{1,0:T(8,128)(2,1)S(1)} %constant_dynamic-slice_fusion.refs_4_), channel_id=1, source_target_pairs={{0,96},{16,112},{32,0},{48,16},{64,32},{80,48},{96,64},{112,80},{1... | collective-permute-start | bytes 1179656 | tf_op jit(solution)/shard_map/ppermute | solution.py:28
  7.3 18.9 %collective-permute-start.8 = (bf16[768,256]{1,0:T(8,128)(2,1)S(1)}, bf16[768,256]{1,0:T(8,128)(2,1)}, u32[]{:S(2)}, u32[]{:S(2)}) collective-permute-start(bf16[768,256]{1,0:T(8,128)(2,1)S(1)} %constant_dynamic-slice_fusion.1.refs_3_), channel_id=1, source_target_pairs={{0,96},{16,112},{32,0},{48,16},{64,32},{80,48},{96,64},{112,80},{1... | collective-permute-start | bytes 1179656 | tf_op jit(solution)/shard_map/ppermute | solution.py:28
  8.4 17.9 %collective-permute-start.6 = (bf16[768,256]{1,0:T(8,128)(2,1)S(1)}, bf16[768,256]{1,0:T(8,128)(2,1)S(1)}, u32[]{:S(2)}, u32[]{:S(2)}) collective-permute-start(bf16[768,256]{1,0:T(8,128)(2,1)S(1)} %constant_dynamic-slice_fusion.1.refs_3_), channel_id=1, source_target_pairs={{0,16},{16,0},{32,48},{48,32},{64,80},{80,64},{96,112},{112,96},{1... | collective-permute-start | bytes 1179656 | tf_op jit(solution)/shard_map/ppermute | solution.py:28
  15.8 11.6 %collective-permute-start.7 = (bf16[768,256]{1,0:T(8,128)(2,1)S(1)}, bf16[768,256]{1,0:T(8,128)(2,1)}, u32[]{:S(2)}, u32[]{:S(2)}) collective-permute-start(bf16[768,256]{1,0:T(8,128)(2,1)S(1)} %constant_dynamic-slice_fusion.refs_4_), channel_id=1, source_target_pairs={{0,16},{16,0},{32,48},{48,32},{64,80},{80,64},{96,112},{112,96},{1... | collective-permute-start | bytes 1179656 | tf_op jit(solution)/shard_map/ppermute | solution.py:28
  23.6 10.9 %collective-permute-start.3 = (bf16[768,256]{1,0:T(8,128)(2,1)S(1)}, bf16[768,256]{1,0:T(8,128)(2,1)S(1)}, u32[]{:S(2)}, u32[]{:S(2)}) collective-permute-start(bf16[768,256]{1,0:T(8,128)(2,1)S(1)} %copy-done.3), channel_id=1, source_target_pairs={{0,32},{16,48},{32,64},{48,80},{64,96},{80,112},{96,0},{112,16},{1... | collective-permute-start | bytes 1179656 | tf_op jit(solution)/shard_map/ppermute | solution.py:28
  23.7 10.8 %collective-permute-start.5 = (bf16[768,256]{1,0:T(8,128)(2,1)}, bf16[768,256]{1,0:T(8,128)(2,1)S(1)}, u32[]{:S(2)}, u32[]{:S(2)}) collective-permute-start(bf16[768,256]{1,0:T(8,128)(2,1)} %collective-permute-done.4.refs_8_), channel_id=1, source_target_pairs={{0,96},{16,112},{32,0},{48,16},{64,32},{80,48},{96,64},{112,80},{1... | collective-permute-start | bytes 1179656 | tf_op jit(solution)/shard_map/ppermute | solution.py:28
  32.9 17.8 %collective-permute-start.10 = (bf16[1536,256]{1,0:T(8,128)(2,1)S(1)}, bf16[1536,256]{1,0:T(8,128)(2,1)S(1)}, u32[]{:S(2)}, u32[]{:S(2)}) collective-permute-start(bf16[1536,256]{1,0:T(8,128)(2,1)S(1)} %join.2.refs_2_), channel_id=1, source_target_pairs={{0,96},{16,112},{32,0},{48,16},{64,32},{80,48},{96,64},{112,80},{1... | collective-permute-start | bytes 2359304 | tf_op jit(solution)/shard_map/ppermute | solution.py:28
  33.0 18.2 %collective-permute-start.9 = (bf16[1536,256]{1,0:T(8,128)(2,1)S(1)}, bf16[1536,256]{1,0:T(8,128)(2,1)S(1)}, u32[]{:S(2)}, u32[]{:S(2)}) collective-permute-start(bf16[1536,256]{1,0:T(8,128)(2,1)S(1)} %join.2.refs_2_), channel_id=1, source_target_pairs={{0,32},{16,48},{32,64},{48,80},{64,96},{80,112},{96,0},{112,16},{1... | collective-permute-start | bytes 2359304 | tf_op jit(solution)/shard_map/ppermute | solution.py:28
  34.5 16.7 %collective-permute-start.11 = (bf16[1536,256]{1,0:T(8,128)(2,1)S(1)}, bf16[1536,256]{1,0:T(8,128)(2,1)S(1)}, u32[]{:S(2)}, u32[]{:S(2)}) collective-permute-start(bf16[1536,256]{1,0:T(8,128)(2,1)S(1)} %join.3.refs_3_), channel_id=1, source_target_pairs={{0,16},{16,0},{32,48},{48,32},{64,80},{80,64},{96,112},{112,96},{1... | collective-permute-start | bytes 2359304 | tf_op jit(solution)/shard_map/ppermute | solution.py:28
  43.5 11.5 %collective-permute-start.14 = (bf16[144,1024]{1,0:T(8,128)(2,1)S(1)}, bf16[144,1024]{1,0:T(8,128)(2,1)S(1)}, u32[]{:S(2)}, u32[]{:S(2)}) collective-permute-start(bf16[144,1024]{1,0:T(8,128)(2,1)S(1)} %get-tuple-element.63), channel_id=1, source_target_pairs={{0,4},{1,5},{2,6},{3,7},{4,0},{5,1},{6,2},{7,3},{8,12},{9,13},{10,... | collective-permute-start | bytes 884744 | tf_op jit(solution)/shard_map/ppermute | solution.py:48
  55.7 13.5 %collective-permute-start.17 = (bf16[144,1024]{1,0:T(8,128)(2,1)S(1)}, bf16[144,1024]{1,0:T(8,128)(2,1)S(1)}, u32[]{:S(2)}, u32[]{:S(2)}) collective-permute-start(bf16[144,1024]{1,0:T(8,128)(2,1)S(1)} %get-tuple-element.71), channel_id=1, source_target_pairs={{0,2},{1,3},{2,4},{3,5},{4,6},{5,7},{6,0},{7,1},{8,10},{9,11},{10,... | collective-permute-start | bytes 884744 | tf_op jit(solution)/shard_map/ppermute | solution.py:48
  57.1 12.1 %collective-permute-start.16 = (bf16[96,1024]{1,0:T(8,128)(2,1)S(1)}, bf16[96,1024]{1,0:T(8,128)(2,1)S(1)}, u32[]{:S(2)}, u32[]{:S(2)}) collective-permute-start(bf16[96,1024]{1,0:T(8,128)(2,1)S(1)} %get-tuple-element.70), channel_id=1, source_target_pairs={{0,8},{1,9},{2,10},{3,11},{4,12},{5,13},{6,14},{7,15},{8,0},{9,1},... | collective-permute-start | bytes 589832 | tf_op jit(solution)/shard_map/ppermute | solution.py:57
  60.2 13.4 %collective-permute-start.18 = (bf16[144,1024]{1,0:T(8,128)(2,1)S(1)}, bf16[144,1024]{1,0:T(8,128)(2,1)S(1)}, u32[]{:S(2)}, u32[]{:S(2)}) collective-permute-start(bf16[144,1024]{1,0:T(8,128)(2,1)S(1)} %get-tuple-element.74), channel_id=1, source_target_pairs={{0,4},{1,5},{2,6},{3,7},{4,0},{5,1},{6,2},{7,3},{8,12},{9,13},{10,... | collective-permute-start | bytes 884744 | tf_op jit(solution)/shard_map/ppermute | solution.py:48
  62.8 10.8 %collective-permute-start.19 = (bf16[144,1024]{1,0:T(8,128)(2,1)S(1)}, bf16[144,1024]{1,0:T(8,128)(2,1)S(1)}, u32[]{:S(2)}, u32[]{:S(2)}) collective-permute-start(bf16[144,1024]{1,0:T(8,128)(2,1)S(1)} %get-tuple-element.75), channel_id=1, source_target_pairs={{0,6},{1,7},{2,0},{3,1},{4,2},{5,3},{6,4},{7,5},{8,14},{9,15},{10,... | collective-permute-start | bytes 884744 | tf_op jit(solution)/shard_map/ppermute | solution.py:48
  70.6 10.9 %collective-permute-start.24 = (bf16[128,1024]{1,0:T(8,128)(2,1)S(1)}, bf16[128,1024]{1,0:T(8,128)(2,1)S(1)}, u32[]{:S(2)}, u32[]{:S(2)}) collective-permute-start(bf16[128,1024]{1,0:T(8,128)(2,1)S(1)} %get-tuple-element.76.refs_6_.refs_4_), channel_id=1, source_target_pairs={{0,6},{1,7},{2,0},{3,1},{4,2},{5,3},{6,4},{7,5},{8,14},{9,15},{10,... | collective-permute-start | bytes 786440 | tf_op jit(solution)/shard_map/ppermute | solution.py:48
  71.9 9.6 %collective-permute-start.23 = (bf16[128,1024]{1,0:T(8,128)(2,1)S(1)}, bf16[128,1024]{1,0:T(8,128)(2,1)S(1)}, u32[]{:S(2)}, u32[]{:S(2)}) collective-permute-start(bf16[128,1024]{1,0:T(8,128)(2,1)S(1)} %get-tuple-element.76.refs_6_.refs_4_), channel_id=1, source_target_pairs={{0,4},{1,5},{2,6},{3,7},{4,0},{5,1},{6,2},{7,3},{8,12},{9,13},{10,... | collective-permute-start | bytes 786440 | tf_op jit(solution)/shard_map/ppermute | solution.py:48
  73.5 7.9 %collective-permute-start.22 = (bf16[128,1024]{1,0:T(8,128)(2,1)S(1)}, bf16[128,1024]{1,0:T(8,128)(2,1)S(1)}, u32[]{:S(2)}, u32[]{:S(2)}) collective-permute-start(bf16[128,1024]{1,0:T(8,128)(2,1)S(1)} %get-tuple-element.76.refs_6_.refs_4_), channel_id=1, source_target_pairs={{0,2},{1,3},{2,4},{3,5},{4,6},{5,7},{6,0},{7,1},{8,10},{9,11},{10,... | collective-permute-start | bytes 786440 | tf_op jit(solution)/shard_map/ppermute | solution.py:48
  74.3 7.2 %collective-permute-start.21 = (bf16[80,1024]{1,0:T(8,128)(2,1)S(1)}, bf16[80,1024]{1,0:T(8,128)(2,1)S(1)}, u32[]{:S(2)}, u32[]{:S(2)}) collective-permute-start(bf16[80,1024]{1,0:T(8,128)(2,1)S(1)} %get-tuple-element.81), channel_id=1, source_target_pairs={{0,8},{1,9},{2,10},{3,11},{4,12},{5,13},{6,14},{7,15},{8,0},{9,1},... | collective-permute-start | bytes 491528 | tf_op jit(solution)/shard_map/ppermute | solution.py:57
  82.9 14.3 %collective-permute-start.27 = (bf16[128,1024]{1,0:T(8,128)(2,1)S(1)}, bf16[128,1024]{1,0:T(8,128)(2,1)S(1)}, u32[]{:S(2)}, u32[]{:S(2)}) collective-permute-start(bf16[128,1024]{1,0:T(8,128)(2,1)S(1)} %get-tuple-element.83.refs_3_.refs_4_), channel_id=1, source_target_pairs={{0,6},{1,7},{2,0},{3,1},{4,2},{5,3},{6,4},{7,5},{8,14},{9,15},{10,... | collective-permute-start | bytes 786440 | tf_op jit(solution)/shard_map/ppermute | solution.py:48
  87.2 10.0 %collective-permute-start.26 = (bf16[128,1024]{1,0:T(8,128)(2,1)S(1)}, bf16[128,1024]{1,0:T(8,128)(2,1)S(1)}, u32[]{:S(2)}, u32[]{:S(2)}) collective-permute-start(bf16[128,1024]{1,0:T(8,128)(2,1)S(1)} %get-tuple-element.83.refs_3_.refs_4_), channel_id=1, source_target_pairs={{0,4},{1,5},{2,6},{3,7},{4,0},{5,1},{6,2},{7,3},{8,12},{9,13},{10,... | collective-permute-start | bytes 786440 | tf_op jit(solution)/shard_map/ppermute | solution.py:48
  89.1 8.0 %collective-permute-start.25 = (bf16[128,1024]{1,0:T(8,128)(2,1)S(1)}, bf16[128,1024]{1,0:T(8,128)(2,1)S(1)}, u32[]{:S(2)}, u32[]{:S(2)}) collective-permute-start(bf16[128,1024]{1,0:T(8,128)(2,1)S(1)} %get-tuple-element.83.refs_3_.refs_4_), channel_id=1, source_target_pairs={{0,2},{1,3},{2,4},{3,5},{4,6},{5,7},{6,0},{7,1},{8,10},{9,11},{10,... | collective-permute-start | bytes 786440 | tf_op jit(solution)/shard_map/ppermute | solution.py:48
  99.1 18.1 %collective-permute-start.30 = (bf16[768,512]{1,0:T(8,128)(2,1)S(1)}, bf16[768,512]{1,0:T(8,128)(2,1)S(1)}, u32[]{:S(2)}, u32[]{:S(2)}) collective-permute-start(bf16[768,512]{1,0:T(8,128)(2,1)S(1)} %grad_far_sent.1.refs_10_), channel_id=1, source_target_pairs={{0,1},{1,0},{2,3},{3,2},{4,5},{5,4},{6,7},{7,6},{8,9},{9,8},{10,11... | collective-permute-start | bytes 2359304 | tf_op jit(solution)/shard_map/ppermute | solution.py:40
  (17 other events, 93.1 us)

commit v7 on v6

--- a/solution.py
+++ b/solution.py
@@ -467,8 +467,8 @@
     z_own_a = shift_row(own_a, 0, 1)
     z_own_b = shift_row(own_b, 0, 1)
     rows_t, own_stats, parts = center_own(student, sibling, teacher, [x_lo_a])
-    x_lo_a, x_lo_b = lax.optimization_barrier((x_lo_a, x_lo_b))
-    x_far_a = shift_row(x_lo_a, 1, 0)
+    x_next, own_stats = lax.optimization_barrier((x_lo_a, own_stats))
+    x_far_a = shift_row(x_next, 1, 0)
     x_far_b = shift_row(x_hi_b, -1, 0)
     near = [own_a, own_b, x_lo_a, x_lo_b, x_hi_a, x_hi_b, z_own_a, z_own_b]
 
@@ -490,7 +490,6 @@
     plane, upper, message, local, row_local = combine_y(
         place, parts, near_sums, True, "combine_y_near", [far_sums[0]]
     )
-    *far_sums, plane = lax.optimization_barrier((*far_sums, plane))
     for d in (1, 3, 2):
         far_sums[d] = shift_y(far_sums[d], d)
     near_masked, parts, near_means, row_offsets, row_stats = combine_z(
@@ -523,8 +522,9 @@
         place, far_inputs, far_pieces, grads, 0, IMAGES, F32, "grad_far_kept", [outgoing], base
     )
     parts = four_sum(parts, (1, 0), (0, 1), add_four_kernel, "four_sum")
-    total_loss = four_sum(parts, (0, 2), (0, 4), loss_kernel, "loss", (1, 1), [kept])
-    return (kept + GRAD_SCALE * incoming.astype(F32), total_loss[0, 0])
+    gradient = kept + GRAD_SCALE * incoming.astype(F32)
+    total_loss = four_sum(parts, (0, 2), (0, 4), loss_kernel, "loss", (1, 1), [gradient])
+    return (gradient, total_loss[0, 0])
 
 
 def solution(mesh):

time: 120 us -> 118 us (0.983)
  starting transfers between devices: 58.6 us -> 55.9 us
  waiting for transfers between devices: 31.7 us -> 33.7 us
    ppermute x12, starting transfers between devices: 19.6 us -> 17.4 us  [shift_y(): return lax.ppermute(block, 'col', pairs)]
    ppermute x12, waiting for transfers between devices: 4.45 us -> 6.09 us  [shift_y(): return lax.ppermute(block, 'col', pairs)]
  transfers between devices with their start and end apart: 37 -> 37, of which waited for: 13 -> 12; matrix products, arithmetic and copies ran while one was open for 1% -> 1% of each run, Pallas kernels for 16% -> 16%
where the time goes in v7:
time: 118 us; the launch traced here: 117 us
  starting transfers between devices  55.9 us (47%)
  waiting for transfers between devices  33.7 us (29%)
  Pallas kernels  23.3 us (20%)
  local copies, waits for them, and re-layouts  3.18 us (3%)
    pallas_call x17, Pallas kernels, call(): pl.pallas_call(kernel, out_shape=tuple(outs), in_specs=[SMEM if a.dtype =...  23.3 us
    ppermute x12, starting transfers between devices, shift_y(): return lax.ppermute(block, 'col', pairs)  17.4 us
    ppermute x11, waiting for transfers between devices, shift_row(): return lax.ppermute(block, 'row', pairs)  14.3 us
    ppermute x11, starting transfers between devices, shift_row(): return lax.ppermute(block, 'row', pairs)  13.8 us
    ppermute x4, waiting for transfers between devices, swap_z_hi(): return lax.ppermute(block, 'col', [(i, i ^ 8) for i in range(16)])  9.93 us
    ppermute x2, starting transfers between devices, swap_cores(): return lax.ppermute(block, 'col', [(i, i ^ 1) for i in range(16)])  8.99 us
    ppermute x4, starting transfers between devices, swap_z_hi(): return lax.ppermute(block, 'col', [(i, i ^ 8) for i in range(16)])  6.67 us
    ppermute x12, waiting for transfers between devices, shift_y(): return lax.ppermute(block, 'col', pairs)  6.09 us
  transfers between devices with their start and end apart: 37, of which 12 were waited for; matrix products, arithmetic and copies ran while one was open for 1% of the time, Pallas kernels for 16%

profile of v7, /device:TPU:1, one launch (start us, length us, event | category | flops | bytes accessed | tf_op | source)
XLA Modules:
  0.0 117.3 jit_solution(2235337046741247772)
XLA Ops:
  9.2 5.8 %collective-permute-done.1.refs_3_.refs_5_ = bf16[768,256]{1,0:T(8,128)(2,1)S(1)} collective-permute-done((bf16[768,256]{1,0:T(8,128)(2,1)S(1)}, bf16[768,256]{1,0:T(8,128)(2,1)S(1)}, u32[]{:S(2)}, u32[]{:S(2)}) %collective-permute-start.1) | collective-permute-done | bytes 393248 | tf_op jit(solution)/shard_map/ppermute | solution.py:28
  15.8 1.7 %collective-permute-start.6 = (bf16[768,256]{1,0:T(8,128)(2,1)S(1)}, bf16[768,256]{1,0:T(8,128)(2,1)}, u32[]{:S(2)}, u32[]{:S(2)}) collective-permute-start(bf16[768,256]{1,0:T(8,128)(2,1)S(1)} %constant_dynamic-slice_fusion.refs_4_), channel_id=1, source_target_pairs={{0,16},{16,0},{32,48},{48,32},{64,80},{80,64},{96,112},{112,96},{1... | collective-permute-start | bytes 1179656 | tf_op jit(solution)/shard_map/ppermute | solution.py:28
  18.6 1.8 %center_own.1 = (bf16[512,1536]{1,0:T(8,128)(2,1)S(1)}, f32[8,512]{1,0:T(8,128)S(1)}, f32[8,128]{1,0:T(8,128)S(1)}) custom-call(bf16[768,512]{1,0:T(8,128)(2,1)S(1)} %copy-done.1, bf16[768,512]{1,0:T(8,128)(2,1)S(1)} %collective-permute-done.refs_1_, bf16[768,512]{1,0:T(8,128)(2,1)S(1)} %copy-done.2, bf16[768,256]{1,0:T(8,128)(2,1)S(1)} %copy-done.4), custom_call_target="tpu_custom_call" | custom-call | tf_op jit(solution)/shard_map/center_own/pallas_call | solution.py:66
  20.5 2.8 %collective-permute-done.3.refs_8_ = bf16[768,256]{1,0:T(8,128)(2,1)} collective-permute-done((bf16[768,256]{1,0:T(8,128)(2,1)S(1)}, bf16[768,256]{1,0:T(8,128)(2,1)}, u32[]{:S(2)}, u32[]{:S(2)}) %collective-permute-start.3) | collective-permute-done | bytes 393248 | tf_op jit(solution)/shard_map/ppermute | solution.py:28
  23.3 2.6 %collective-permute-start.4 = (bf16[768,256]{1,0:T(8,128)(2,1)}, bf16[768,256]{1,0:T(8,128)(2,1)S(1)}, u32[]{:S(2)}, u32[]{:S(2)}) collective-permute-start(bf16[768,256]{1,0:T(8,128)(2,1)} %collective-permute-done.3.refs_8_), channel_id=1, source_target_pairs={{0,96},{16,112},{32,0},{48,16},{64,32},{80,48},{96,64},{112,80},{1... | collective-permute-start | bytes 1179656 | tf_op jit(solution)/shard_map/ppermute | solution.py:28
  25.9 4.5 %partial_near.1 = (f32[144,1024]{1,0:T(8,128)S(1)}, bf16[144,1024]{1,0:T(8,128)(2,1)S(1)}, bf16[144,1024]{1,0:T(8,128)(2,1)S(1)}, bf16[144,1024]{1,0:T(8,128)(2,...) custom-call(s32[5]{0:T(128)S(1)} %stack.23.refs_0_, bf16[512,1536]{1,0:T(8,128)(2,1)S(1)} %get-tuple-element.40.refs_1_, ...), custom_call_target="tpu_custom_call" | custom-call | flops 32212254720 | tf_op jit(solution)/shard_map/partial_near/pallas_call | solution.py:66
  33.4 1.8 %collective-permute-start.11 = (bf16[1536,256]{1,0:T(8,128)(2,1)S(1)}, bf16[1536,256]{1,0:T(8,128)(2,1)S(1)}, u32[]{:S(2)}, u32[]{:S(2)}) collective-permute-start(bf16[1536,256]{1,0:T(8,128)(2,1)S(1)} %join.3.refs_3_), channel_id=1, source_target_pairs={{0,16},{16,0},{32,48},{48,32},{64,80},{80,64},{96,112},{112,96},{1... | collective-permute-start | bytes 2359304 | tf_op jit(solution)/shard_map/ppermute | solution.py:28
  38.0 4.4 %collective-permute-done.12.refs_3_ = bf16[144,1024]{1,0:T(8,128)(2,1)S(1)} collective-permute-done((bf16[144,1024]{1,0:T(8,128)(2,1)S(1)}, bf16[144,1024]{1,0:T(8,128)(2,1)S(1)}, u32[]{:S(2)}, u32[]{:S(2)}) %collective-permute-start.12) | collective-permute-done | bytes 294944 | tf_op jit(solution)/shard_map/ppermute | solution.py:48
  42.4 2.6 %collective-permute-start.14 = (bf16[144,1024]{1,0:T(8,128)(2,1)S(1)}, bf16[144,1024]{1,0:T(8,128)(2,1)S(1)}, u32[]{:S(2)}, u32[]{:S(2)}) collective-permute-start(bf16[144,1024]{1,0:T(8,128)(2,1)S(1)} %get-tuple-element.54), channel_id=1, source_target_pairs={{0,4},{1,5},{2,6},{3,7},{4,0},{5,1},{6,2},{7,3},{8,12},{9,13},{10,... | collective-permute-start | bytes 884744 | tf_op jit(solution)/shard_map/ppermute | solution.py:48
  45.0 5.1 %collective-permute-done.10.refs_5_ = bf16[1536,256]{1,0:T(8,128)(2,1)S(1)} collective-permute-done((bf16[1536,256]{1,0:T(8,128)(2,1)S(1)}, bf16[1536,256]{1,0:T(8,128)(2,1)S(1)}, u32[]{:S(2)}, u32[]{:S(2)}) %collective-permute-start.10) | collective-permute-done | bytes 786464 | tf_op jit(solution)/shard_map/ppermute | solution.py:28
  50.4 3.7 %partial_far.1 = (f32[144,1024]{1,0:T(8,128)S(1)}, bf16[144,1024]{1,0:T(8,128)(2,1)S(1)}, bf16[144,1024]{1,0:T(8,128)(2,1)S(1)}, bf16[144,1024]{1,0:T(8,128)(2,1...) custom-call(s32[5]{0:T(128)S(1)} %stack.23.refs_0_, bf16[512,1536]{1,0:T(8,128)(2,1)S(1)} %get-tuple-element.40.refs_1_, ...), custom_call_target="tpu_custom_call" | custom-call | flops 32212254720 | tf_op jit(solution)/shard_map/partial_far/pallas_call | solution.py:66
  56.2 3.5 %collective-permute-start.16 = (bf16[96,1024]{1,0:T(8,128)(2,1)S(1)}, bf16[96,1024]{1,0:T(8,128)(2,1)S(1)}, u32[]{:S(2)}, u32[]{:S(2)}) collective-permute-start(bf16[96,1024]{1,0:T(8,128)(2,1)S(1)} %get-tuple-element.61), channel_id=1, source_target_pairs={{0,8},{1,9},{2,10},{3,11},{4,12},{5,13},{6,14},{7,15},{8,0},{9,1},... | collective-permute-start | bytes 589832 | tf_op jit(solution)/shard_map/ppermute | solution.py:57
  59.7 2.6 %collective-permute-start.18 = (bf16[144,1024]{1,0:T(8,128)(2,1)S(1)}, bf16[144,1024]{1,0:T(8,128)(2,1)S(1)}, u32[]{:S(2)}, u32[]{:S(2)}) collective-permute-start(bf16[144,1024]{1,0:T(8,128)(2,1)S(1)} %get-tuple-element.64), channel_id=1, source_target_pairs={{0,4},{1,5},{2,6},{3,7},{4,0},{5,1},{6,2},{7,3},{8,12},{9,13},{10,... | collective-permute-start | bytes 884744 | tf_op jit(solution)/shard_map/ppermute | solution.py:48
  63.5 5.5 %collective-permute-done.15.refs_4_ = bf16[64,1024]{1,0:T(8,128)(2,1)S(1)} collective-permute-done((bf16[64,1024]{1,0:T(8,128)(2,1)S(1)}, bf16[64,1024]{1,0:T(8,128)(2,1)S(1)}, u32[]{:S(2)}, u32[]{:S(2)}) %collective-permute-start.15) | collective-permute-done | bytes 131104 | tf_op jit(solution)/shard_map/ppermute | solution.py:57
  74.0 2.6 %collective-permute-start.20 = (bf16[64,1024]{1,0:T(8,128)(2,1)S(1)}, bf16[64,1024]{1,0:T(8,128)(2,1)S(1)}, u32[]{:S(2)}, u32[]{:S(2)}) collective-permute-start(bf16[64,1024]{1,0:T(8,128)(2,1)S(1)} %get-tuple-element.70), channel_id=1, source_target_pairs={{0,8},{1,9},{2,10},{3,11},{4,12},{5,13},{6,14},{7,15},{8,0},{9,1},... | collective-permute-start | bytes 393224 | tf_op jit(solution)/shard_map/ppermute | solution.py:57
  76.6 4.4 %collective-permute-done.20.refs_4_ = bf16[64,1024]{1,0:T(8,128)(2,1)S(1)} collective-permute-done((bf16[64,1024]{1,0:T(8,128)(2,1)S(1)}, bf16[64,1024]{1,0:T(8,128)(2,1)S(1)}, u32[]{:S(2)}, u32[]{:S(2)}) %collective-permute-start.20) | collective-permute-done | bytes 131104 | tf_op jit(solution)/shard_map/ppermute | solution.py:57
  81.0 1.6 %collective-permute-done.22.refs_7_.refs_5_ = bf16[128,1024]{1,0:T(8,128)(2,1)S(1)} collective-permute-done((bf16[128,1024]{1,0:T(8,128)(2,1)S(1)}, bf16[128,1024]{1,0:T(8,128)(2,1)S(1)}, u32[]{:S(2)}, u32[]{:S(2)}) %collective-permute-start.22) | collective-permute-done | bytes 262176 | tf_op jit(solution)/shard_map/ppermute | solution.py:48
  84.0 3.1 %collective-permute-start.27 = (bf16[128,1024]{1,0:T(8,128)(2,1)S(1)}, bf16[128,1024]{1,0:T(8,128)(2,1)S(1)}, u32[]{:S(2)}, u32[]{:S(2)}) collective-permute-start(bf16[128,1024]{1,0:T(8,128)(2,1)S(1)} %get-tuple-element.73.refs_3_.refs_4_), channel_id=1, source_target_pairs={{0,6},{1,7},{2,0},{3,1},{4,2},{5,3},{6,4},{7,5},{8,14},{9,15},{10,... | collective-permute-start | bytes 786440 | tf_op jit(solution)/shard_map/ppermute | solution.py:48
  89.4 1.7 %collective-permute-done.28.refs_1_ = f32[8,128]{1,0:T(8,128)S(1)} collective-permute-done((f32[8,128]{1,0:T(8,128)S(1)}, f32[8,128]{1,0:T(8,128)S(1)}, u32[]{:S(2)}, u32[]{:S(2)}) %collective-permute-start.28) | collective-permute-done | bytes 4128 | tf_op jit(solution)/shard_map/ppermute | solution.py:387
  91.1 3.1 %collective-permute-start.29 = (f32[8,128]{1,0:T(8,128)S(1)}, f32[8,128]{1,0:T(8,128)S(1)}, u32[]{:S(2)}, u32[]{:S(2)}) collective-permute-start(f32[8,128]{1,0:T(8,128)S(1)} %pair_sum.2.refs_0_), channel_id=1, source_target_pairs={{0,64},{16,80},{32,96},{48,112},{64,0},{80,16},{96,32},{112,48},{1... | collective-permute-start | bytes 12296 | tf_op jit(solution)/shard_map/ppermute | solution.py:387
  94.7 2.8 %grad_near.1.refs_8_ = f32[1536,512]{1,0:T(8,128)S(1)} custom-call(s32[5]{0:T(128)S(1)} %stack.23.refs_0_, bf16[1536,1024]{1,0:T(8,128)(2,1)S(1)} %get-tuple-element.74.refs_1_, f32[8,1024]{1,0:T(8,128)S(1)} %get-tuple-element.44.refs_2_, f32[8,1024]{1,0:T(8,128)S(1)} %get-tuple-element.75.refs_3_, bf16[128,1024]{1,0:T(8,128)(2,1)S(1)} %get-tuple-element.66.refs_6_.refs_4_, ...), custom_call_target="tpu_custom_call" | custom-call | tf_op jit(solution)/shard_map/grad_near/pallas_call | solution.py:66
  97.5 2.0 %grad_far_sent.1.refs_10_ = bf16[768,512]{1,0:T(8,128)(2,1)S(1)} custom-call(s32[5]{0:T(128)S(1)} %stack.23.refs_0_, bf16[1536,1024]{1,0:T(8,128)(2,1)S(1)} %get-tuple-element.45.refs_1_, f32[8,1024]{1,0:T(8,128)S(1)} %get-tuple-element.46.refs_2_, f32[8,1024]{1,0:T(8,128)S(1)} %get-tuple-element.72.refs_3_, ...), custom_call_target="tpu_custom_call" | custom-call | tf_op jit(solution)/shard_map/grad_far_sent/pallas_call | solution.py:66
  99.5 7.5 %collective-permute-start.30 = (bf16[768,512]{1,0:T(8,128)(2,1)S(1)}, bf16[768,512]{1,0:T(8,128)(2,1)S(1)}, u32[]{:S(2)}, u32[]{:S(2)}) collective-permute-start(bf16[768,512]{1,0:T(8,128)(2,1)S(1)} %grad_far_sent.1.refs_10_), channel_id=1, source_target_pairs={{0,1},{1,0},{2,3},{3,2},{4,5},{5,4},{6,7},{7,6},{8,9},{9,8},{10,11... | collective-permute-start | bytes 2359304 | tf_op jit(solution)/shard_map/ppermute | solution.py:40
  113.8 2.0 %grad_far_kept.1 = f32[768,512]{1,0:T(8,128)S(1)} custom-call(s32[5]{0:T(128)S(1)} %stack.23.refs_0_, bf16[1536,1024]{1,0:T(8,128)(2,1)S(1)} %get-tuple-element.45.refs_1_, f32[8,1024]{1,0:T(8,128)S(1)} %get-tuple-element.46.refs_2_, f32[8,1024]{1,0:T(8,128)S(1)} %get-tuple-element.72.refs_3_, bf16[128,1024]{1,0:T(8,128)(2,1)S(1)} %get-tuple-element.73.refs_3_.refs_4_, ...), custom_call_target="tpu_custom_call" | custom-call | tf_op jit(solution)/shard_map/grad_far_kept/pallas_call | solution.py:66
  (81 shorter events, 37.1 us)
Async XLA Ops:
  3.2 11.9 %collective-permute-start.1 = (bf16[768,256]{1,0:T(8,128)(2,1)S(1)}, bf16[768,256]{1,0:T(8,128)(2,1)S(1)}, u32[]{:S(2)}, u32[]{:S(2)}) collective-permute-start(bf16[768,256]{1,0:T(8,128)(2,1)S(1)} %constant_dynamic-slice_fusion.1.refs_3_), channel_id=1, source_target_pairs={{0,32},{16,48},{32,64},{48,80},{64,96},{80,112},{96,0},{112,16},{1... | collective-permute-start | bytes 1179656 | tf_op jit(solution)/shard_map/ppermute | solution.py:28
  4.5 15.8 %collective-permute-start.8 = (bf16[768,256]{1,0:T(8,128)(2,1)S(1)}, bf16[768,256]{1,0:T(8,128)(2,1)}, u32[]{:S(2)}, u32[]{:S(2)}) collective-permute-start(bf16[768,256]{1,0:T(8,128)(2,1)S(1)} %constant_dynamic-slice_fusion.1.refs_3_), channel_id=1, source_target_pairs={{0,96},{16,112},{32,0},{48,16},{64,32},{80,48},{96,64},{112,80},{1... | collective-permute-start | bytes 1179656 | tf_op jit(solution)/shard_map/ppermute | solution.py:28
  6.0 17.4 %collective-permute-start.3 = (bf16[768,256]{1,0:T(8,128)(2,1)S(1)}, bf16[768,256]{1,0:T(8,128)(2,1)}, u32[]{:S(2)}, u32[]{:S(2)}) collective-permute-start(bf16[768,256]{1,0:T(8,128)(2,1)S(1)} %constant_dynamic-slice_fusion.refs_4_), channel_id=1, source_target_pairs={{0,96},{16,112},{32,0},{48,16},{64,32},{80,48},{96,64},{112,80},{1... | collective-permute-start | bytes 1179656 | tf_op jit(solution)/shard_map/ppermute | solution.py:28
  7.4 18.6 %collective-permute-start.5 = (bf16[768,256]{1,0:T(8,128)(2,1)S(1)}, bf16[768,256]{1,0:T(8,128)(2,1)S(1)}, u32[]{:S(2)}, u32[]{:S(2)}) collective-permute-start(bf16[768,256]{1,0:T(8,128)(2,1)S(1)} %constant_dynamic-slice_fusion.1.refs_3_), channel_id=1, source_target_pairs={{0,16},{16,0},{32,48},{48,32},{64,80},{80,64},{96,112},{112,96},{1... | collective-permute-start | bytes 1179656 | tf_op jit(solution)/shard_map/ppermute | solution.py:28
  9.0 16.9 %collective-permute-start.7 = (bf16[768,256]{1,0:T(8,128)(2,1)S(1)}, bf16[768,256]{1,0:T(8,128)(2,1)}, u32[]{:S(2)}, u32[]{:S(2)}) collective-permute-start(bf16[768,256]{1,0:T(8,128)(2,1)S(1)} %constant_dynamic-slice_fusion.refs_4_), channel_id=1, source_target_pairs={{0,32},{16,48},{32,64},{48,80},{64,96},{80,112},{96,0},{112,16},{1... | collective-permute-start | bytes 1179656 | tf_op jit(solution)/shard_map/ppermute | solution.py:28
  15.8 10.2 %collective-permute-start.6 = (bf16[768,256]{1,0:T(8,128)(2,1)S(1)}, bf16[768,256]{1,0:T(8,128)(2,1)}, u32[]{:S(2)}, u32[]{:S(2)}) collective-permute-start(bf16[768,256]{1,0:T(8,128)(2,1)S(1)} %constant_dynamic-slice_fusion.refs_4_), channel_id=1, source_target_pairs={{0,16},{16,0},{32,48},{48,32},{64,80},{80,64},{96,112},{112,96},{1... | collective-permute-start | bytes 1179656 | tf_op jit(solution)/shard_map/ppermute | solution.py:28
  20.4 12.7 %collective-permute-start.2 = (bf16[768,256]{1,0:T(8,128)(2,1)S(1)}, bf16[768,256]{1,0:T(8,128)(2,1)S(1)}, u32[]{:S(2)}, u32[]{:S(2)}) collective-permute-start(bf16[768,256]{1,0:T(8,128)(2,1)S(1)} %copy-done.4), channel_id=1, source_target_pairs={{0,32},{16,48},{32,64},{48,80},{64,96},{80,112},{96,0},{112,16},{1... | collective-permute-start | bytes 1179656 | tf_op jit(solution)/shard_map/ppermute | solution.py:28
  23.3 10.0 %collective-permute-start.4 = (bf16[768,256]{1,0:T(8,128)(2,1)}, bf16[768,256]{1,0:T(8,128)(2,1)S(1)}, u32[]{:S(2)}, u32[]{:S(2)}) collective-permute-start(bf16[768,256]{1,0:T(8,128)(2,1)} %collective-permute-done.3.refs_8_), channel_id=1, source_target_pairs={{0,96},{16,112},{32,0},{48,16},{64,32},{80,48},{96,64},{112,80},{1... | collective-permute-start | bytes 1179656 | tf_op jit(solution)/shard_map/ppermute | solution.py:28
  31.5 18.6 %collective-permute-start.10 = (bf16[1536,256]{1,0:T(8,128)(2,1)S(1)}, bf16[1536,256]{1,0:T(8,128)(2,1)S(1)}, u32[]{:S(2)}, u32[]{:S(2)}) collective-permute-start(bf16[1536,256]{1,0:T(8,128)(2,1)S(1)} %join.2.refs_2_), channel_id=1, source_target_pairs={{0,96},{16,112},{32,0},{48,16},{64,32},{80,48},{96,64},{112,80},{1... | collective-permute-start | bytes 2359304 | tf_op jit(solution)/shard_map/ppermute | solution.py:28
  32.5 17.8 %collective-permute-start.9 = (bf16[1536,256]{1,0:T(8,128)(2,1)S(1)}, bf16[1536,256]{1,0:T(8,128)(2,1)S(1)}, u32[]{:S(2)}, u32[]{:S(2)}) collective-permute-start(bf16[1536,256]{1,0:T(8,128)(2,1)S(1)} %join.2.refs_2_), channel_id=1, source_target_pairs={{0,32},{16,48},{32,64},{48,80},{64,96},{80,112},{96,0},{112,16},{1... | collective-permute-start | bytes 2359304 | tf_op jit(solution)/shard_map/ppermute | solution.py:28
  33.4 16.9 %collective-permute-start.11 = (bf16[1536,256]{1,0:T(8,128)(2,1)S(1)}, bf16[1536,256]{1,0:T(8,128)(2,1)S(1)}, u32[]{:S(2)}, u32[]{:S(2)}) collective-permute-start(bf16[1536,256]{1,0:T(8,128)(2,1)S(1)} %join.3.refs_3_), channel_id=1, source_target_pairs={{0,16},{16,0},{32,48},{48,32},{64,80},{80,64},{96,112},{112,96},{1... | collective-permute-start | bytes 2359304 | tf_op jit(solution)/shard_map/ppermute | solution.py:28
  42.4 13.0 %collective-permute-start.14 = (bf16[144,1024]{1,0:T(8,128)(2,1)S(1)}, bf16[144,1024]{1,0:T(8,128)(2,1)S(1)}, u32[]{:S(2)}, u32[]{:S(2)}) collective-permute-start(bf16[144,1024]{1,0:T(8,128)(2,1)S(1)} %get-tuple-element.54), channel_id=1, source_target_pairs={{0,4},{1,5},{2,6},{3,7},{4,0},{5,1},{6,2},{7,3},{8,12},{9,13},{10,... | collective-permute-start | bytes 884744 | tf_op jit(solution)/shard_map/ppermute | solution.py:48
  54.1 14.9 %collective-permute-start.17 = (bf16[144,1024]{1,0:T(8,128)(2,1)S(1)}, bf16[144,1024]{1,0:T(8,128)(2,1)S(1)}, u32[]{:S(2)}, u32[]{:S(2)}) collective-permute-start(bf16[144,1024]{1,0:T(8,128)(2,1)S(1)} %get-tuple-element.62), channel_id=1, source_target_pairs={{0,2},{1,3},{2,4},{3,5},{4,6},{5,7},{6,0},{7,1},{8,10},{9,11},{10,... | collective-permute-start | bytes 884744 | tf_op jit(solution)/shard_map/ppermute | solution.py:48
  56.2 12.8 %collective-permute-start.16 = (bf16[96,1024]{1,0:T(8,128)(2,1)S(1)}, bf16[96,1024]{1,0:T(8,128)(2,1)S(1)}, u32[]{:S(2)}, u32[]{:S(2)}) collective-permute-start(bf16[96,1024]{1,0:T(8,128)(2,1)S(1)} %get-tuple-element.61), channel_id=1, source_target_pairs={{0,8},{1,9},{2,10},{3,11},{4,12},{5,13},{6,14},{7,15},{8,0},{9,1},... | collective-permute-start | bytes 589832 | tf_op jit(solution)/shard_map/ppermute | solution.py:57
  59.7 13.1 %collective-permute-start.18 = (bf16[144,1024]{1,0:T(8,128)(2,1)S(1)}, bf16[144,1024]{1,0:T(8,128)(2,1)S(1)}, u32[]{:S(2)}, u32[]{:S(2)}) collective-permute-start(bf16[144,1024]{1,0:T(8,128)(2,1)S(1)} %get-tuple-element.64), channel_id=1, source_target_pairs={{0,4},{1,5},{2,6},{3,7},{4,0},{5,1},{6,2},{7,3},{8,12},{9,13},{10,... | collective-permute-start | bytes 884744 | tf_op jit(solution)/shard_map/ppermute | solution.py:48
  62.3 10.5 %collective-permute-start.19 = (bf16[144,1024]{1,0:T(8,128)(2,1)S(1)}, bf16[144,1024]{1,0:T(8,128)(2,1)S(1)}, u32[]{:S(2)}, u32[]{:S(2)}) collective-permute-start(bf16[144,1024]{1,0:T(8,128)(2,1)S(1)} %get-tuple-element.65), channel_id=1, source_target_pairs={{0,6},{1,7},{2,0},{3,1},{4,2},{5,3},{6,4},{7,5},{8,14},{9,15},{10,... | collective-permute-start | bytes 884744 | tf_op jit(solution)/shard_map/ppermute | solution.py:48
  70.4 10.6 %collective-permute-start.24 = (bf16[128,1024]{1,0:T(8,128)(2,1)S(1)}, bf16[128,1024]{1,0:T(8,128)(2,1)S(1)}, u32[]{:S(2)}, u32[]{:S(2)}) collective-permute-start(bf16[128,1024]{1,0:T(8,128)(2,1)S(1)} %get-tuple-element.66.refs_6_.refs_4_), channel_id=1, source_target_pairs={{0,6},{1,7},{2,0},{3,1},{4,2},{5,3},{6,4},{7,5},{8,14},{9,15},{10,... | collective-permute-start | bytes 786440 | tf_op jit(solution)/shard_map/ppermute | solution.py:48
  71.9 9.1 %collective-permute-start.23 = (bf16[128,1024]{1,0:T(8,128)(2,1)S(1)}, bf16[128,1024]{1,0:T(8,128)(2,1)S(1)}, u32[]{:S(2)}, u32[]{:S(2)}) collective-permute-start(bf16[128,1024]{1,0:T(8,128)(2,1)S(1)} %get-tuple-element.66.refs_6_.refs_4_), channel_id=1, source_target_pairs={{0,4},{1,5},{2,6},{3,7},{4,0},{5,1},{6,2},{7,3},{8,12},{9,13},{10,... | collective-permute-start | bytes 786440 | tf_op jit(solution)/shard_map/ppermute | solution.py:48
  72.6 10.1 %collective-permute-start.22 = (bf16[128,1024]{1,0:T(8,128)(2,1)S(1)}, bf16[128,1024]{1,0:T(8,128)(2,1)S(1)}, u32[]{:S(2)}, u32[]{:S(2)}) collective-permute-start(bf16[128,1024]{1,0:T(8,128)(2,1)S(1)} %get-tuple-element.66.refs_6_.refs_4_), channel_id=1, source_target_pairs={{0,2},{1,3},{2,4},{3,5},{4,6},{5,7},{6,0},{7,1},{8,10},{9,11},{10,... | collective-permute-start | bytes 786440 | tf_op jit(solution)/shard_map/ppermute | solution.py:48
  73.5 7.5 %collective-permute-start.21 = (bf16[80,1024]{1,0:T(8,128)(2,1)S(1)}, bf16[80,1024]{1,0:T(8,128)(2,1)S(1)}, u32[]{:S(2)}, u32[]{:S(2)}) collective-permute-start(bf16[80,1024]{1,0:T(8,128)(2,1)S(1)} %get-tuple-element.71), channel_id=1, source_target_pairs={{0,8},{1,9},{2,10},{3,11},{4,12},{5,13},{6,14},{7,15},{8,0},{9,1},... | collective-permute-start | bytes 491528 | tf_op jit(solution)/shard_map/ppermute | solution.py:57
  84.0 13.4 %collective-permute-start.27 = (bf16[128,1024]{1,0:T(8,128)(2,1)S(1)}, bf16[128,1024]{1,0:T(8,128)(2,1)S(1)}, u32[]{:S(2)}, u32[]{:S(2)}) collective-permute-start(bf16[128,1024]{1,0:T(8,128)(2,1)S(1)} %get-tuple-element.73.refs_3_.refs_4_), channel_id=1, source_target_pairs={{0,6},{1,7},{2,0},{3,1},{4,2},{5,3},{6,4},{7,5},{8,14},{9,15},{10,... | collective-permute-start | bytes 786440 | tf_op jit(solution)/shard_map/ppermute | solution.py:48
  87.1 10.4 %collective-permute-start.26 = (bf16[128,1024]{1,0:T(8,128)(2,1)S(1)}, bf16[128,1024]{1,0:T(8,128)(2,1)S(1)}, u32[]{:S(2)}, u32[]{:S(2)}) collective-permute-start(bf16[128,1024]{1,0:T(8,128)(2,1)S(1)} %get-tuple-element.73.refs_3_.refs_4_), channel_id=1, source_target_pairs={{0,4},{1,5},{2,6},{3,7},{4,0},{5,1},{6,2},{7,3},{8,12},{9,13},{10,... | collective-permute-start | bytes 786440 | tf_op jit(solution)/shard_map/ppermute | solution.py:48
  88.6 8.9 %collective-permute-start.25 = (bf16[128,1024]{1,0:T(8,128)(2,1)S(1)}, bf16[128,1024]{1,0:T(8,128)(2,1)S(1)}, u32[]{:S(2)}, u32[]{:S(2)}) collective-permute-start(bf16[128,1024]{1,0:T(8,128)(2,1)S(1)} %get-tuple-element.73.refs_3_.refs_4_), channel_id=1, source_target_pairs={{0,2},{1,3},{2,4},{3,5},{4,6},{5,7},{6,0},{7,1},{8,10},{9,11},{10,... | collective-permute-start | bytes 786440 | tf_op jit(solution)/shard_map/ppermute | solution.py:48
  99.5 16.4 %collective-permute-start.30 = (bf16[768,512]{1,0:T(8,128)(2,1)S(1)}, bf16[768,512]{1,0:T(8,128)(2,1)S(1)}, u32[]{:S(2)}, u32[]{:S(2)}) collective-permute-start(bf16[768,512]{1,0:T(8,128)(2,1)S(1)} %grad_far_sent.1.refs_10_), channel_id=1, source_target_pairs={{0,1},{1,0},{2,3},{3,2},{4,5},{5,4},{6,7},{7,6},{8,9},{9,8},{10,11... | collective-permute-start | bytes 2359304 | tf_op jit(solution)/shard_map/ppermute | solution.py:40
  (18 other events, 97.2 us)

commit v8 on v7

--- a/solution.py
+++ b/solution.py
@@ -266,7 +266,7 @@
 
 
 def combine_y_kernel(
-    with_rows, place, parts, own, one, two, three_on, plane, upper, message, local, *row_local
+    with_rows, place, parts, own, one, two, three_on, plane, message, local, *more
 ):
     width = own.shape[1]
     columns = jnp.zeros((4, width), F32)
@@ -291,24 +291,25 @@
         return [high, middle, low], high + middle + low
 
     plane[...] = total.astype(BF16)
-    upper[...] = total[0:UPPER].astype(BF16)
-    message[0:QUARTER - UPPER, :] = total[UPPER:].astype(BF16)
+    upper = 0 if with_rows else UPPER
+    message[0:QUARTER - upper, :] = total[upper:].astype(BF16)
+    if upper:
+        more[0][...] = total[0:upper].astype(BF16)
     lines, local[0:4, :] = rounded(columns)
     if with_rows:
-        row_lines, row_local[0][0:4, :] = rounded(rows)
-        square_lines, row_local[0][4:5, :] = rounded(squares)
+        row_lines, more[0][0:4, :] = rounded(rows)
+        square_lines, more[0][4:5, :] = rounded(squares)
         part_lines, _ = rounded(parts[0:1, :])
         lines = lines + padded(row_lines + square_lines, width) + padded(part_lines, width)
     block = filled(lines, width)
-    message[QUARTER - UPPER:, :] = block.astype(BF16)
+    message[QUARTER - upper:, :] = block.astype(BF16)
 
 
 def combine_y(place, parts, pieces, with_rows, name, after=()):
     width = pieces[0].shape[1]
-    rows = QUARTER - UPPER + (2 if with_rows else 1) * STAT_ROWS
-    outs = [shape((QUARTER, width), BF16), shape((UPPER, width), BF16)]
-    outs += [shape((rows, width), BF16), shape((8, width), F32)]
-    outs += [shape((8, FEATS), F32)] if with_rows else []
+    rows = QUARTER + 2 * STAT_ROWS if with_rows else QUARTER - UPPER + STAT_ROWS
+    outs = [shape((QUARTER, width), BF16), shape((rows, width), BF16), shape((8, width), F32)]
+    outs.append(shape((8, FEATS), F32) if with_rows else shape((UPPER, width), BF16))
     return call(
         functools.partial(combine_y_kernel, with_rows), outs, [place, parts] + pieces, [], name, after
     )
@@ -320,9 +321,13 @@
 
 
 def combine_z_kernel(
-    with_rows, place, plane, local, rows, upper, received, parts, masked, part, means, *more
+    with_rows, place, plane, local, rows, parts, received, *more
 ):
-    stats = received[QUARTER - UPPER:, :].astype(F32)
+    upper = 0 if with_rows else UPPER
+    if not with_rows:
+        other_upper, *more = more
+    masked, part, means, *more = more
+    stats = received[QUARTER - upper:, :].astype(F32)
     theirs = stats[0:4] + stats[4:8] + stats[8:12]
     col_off, col_mean = spread_out(all_chips(place, local[0:4, :], theirs))
     means[...] = jnp.broadcast_to(col_mean, means.shape)
@@ -341,8 +346,10 @@
         row_stats[...] = jnp.concatenate([row_mean, spread, jnp.zeros((6, FEATS), F32)], axis=0)
     block = pl.multiple_of(place[2] * QUARTER, QUARTER)
     term = mean_term(row_offsets[:, pl.ds(block, QUARTER)], col_off)
-    other = [upper[...].astype(F32), received[0:QUARTER - UPPER, :].astype(F32)]
-    covar = plane[...].astype(F32) + jnp.concatenate(other, axis=0)
+    other = received[0:QUARTER - upper, :].astype(F32)
+    if upper:
+        other = jnp.concatenate([other_upper[...].astype(F32), other], axis=0)
+    covar = plane[...].astype(F32) + other
     covar = (covar + term) / (BATCH - 1)
     if with_rows:
         row_ids = place[2] * QUARTER + lax.broadcasted_iota(jnp.int32, covar.shape, 0)
@@ -358,11 +365,11 @@
     masked[0:QUARTER, :] = covar.astype(BF16)
 
 
-def combine_z(place, plane, local, rows, upper, received, parts, with_rows, name, after=()):
+def combine_z(place, plane, local, rows, parts, received, with_rows, name, after=()):
     width = plane.shape[1]
     outs = [shape((QUARTER, width), BF16), shape((8, 128), F32), shape((8, width), F32)]
     outs += [shape((8, FEATS), F32)] * 2 if with_rows else []
-    ins = [place, plane, local, rows, upper, received, parts]
+    ins = [place, plane, local, rows, parts] + received
     return call(functools.partial(combine_z_kernel, with_rows), outs, ins, [], name, after)
 
 
@@ -487,23 +494,22 @@
     far_sums, far_columns, far_stats = partial_sums(
         place, rows_t, own_stats, far, False, "partial_far"
     )
-    plane, upper, message, local, row_local = combine_y(
+    plane, message, local, row_local = combine_y(
         place, parts, near_sums, True, "combine_y_near", [far_sums[0]]
     )
     for d in (1, 3, 2):
         far_sums[d] = shift_y(far_sums[d], d)
     near_masked, parts, near_means, row_offsets, row_stats = combine_z(
-        place, plane, local, row_local, swap_z_hi(upper), swap_z_hi(message), parts, True,
-        "combine_z_near", [far_sums[1]],
+        place, plane, local, row_local, parts, [swap_z_hi(message)], True, "combine_z_near",
+        [far_sums[1]],
     )
     near_pieces = sent_round(near_masked)
-    far_plane, far_upper, far_message, far_local = combine_y(
+    far_plane, far_message, far_local, far_upper = combine_y(
         place, parts, far_sums, False, "combine_y_far", [near_masked]
     )
     far_masked, parts, far_means = combine_z(
-        place, far_plane, far_local, row_offsets, swap_z_hi(far_upper), swap_z_hi(far_message),
-        parts, False,
-        "combine_z_far", near_pieces[1:],
+        place, far_plane, far_local, row_offsets, parts,
+        [swap_z_hi(far_message), swap_z_hi(far_upper)], False, "combine_z_far", [near_pieces[1], near_pieces[3]],
     )
     far_pieces = sent_round(far_masked)
 

time: 118 us -> 117 us (level)
  waiting for transfers between devices: 33.7 us -> 27.1 us
  starting transfers between devices: 55.9 us -> 61.5 us
    ppermute x4 -> x3, waiting for transfers between devices: 9.93 us -> 0.59 us  [swap_z_hi(): return lax.ppermute(block, 'col', [(i, i ^ 8) for i in range(16)])]
    ppermute x12, starting transfers between devices: 17.4 us -> 20.3 us  [shift_y(): return lax.ppermute(block, 'col', pairs)]
    ppermute x12, waiting for transfers between devices: 6.09 us -> 8.77 us  [shift_y(): return lax.ppermute(block, 'col', pairs)]
    ppermute x2, starting transfers between devices: 8.99 us -> 11.2 us  [swap_cores(): return lax.ppermute(block, 'col', [(i, i ^ 1) for i in range(16)])]
    ppermute x4 -> x3, starting transfers between devices: 6.67 us -> 6.57 us  [swap_z_hi(): return lax.ppermute(block, 'col', [(i, i ^ 8) for i in range(16)])]
  transfers between devices with their start and end apart: 37 -> 36, of which waited for: 12 -> 13; matrix products, arithmetic and copies ran while one was open for 1% -> 1% of each run, Pallas kernels for 16% -> 17%
where the time goes in v8:
time: 117 us; the launch traced here: 116 us
  starting transfers between devices  61.5 us (53%)
  waiting for transfers between devices  27.1 us (23%)
  Pallas kernels  23.4 us (20%)
  local copies, waits for them, and re-layouts  3.18 us (3%)
    pallas_call x17, Pallas kernels, call(): pl.pallas_call(kernel, out_shape=tuple(outs), in_specs=[SMEM if a.dtype =...  23.4 us
    ppermute x12, starting transfers between devices, shift_y(): return lax.ppermute(block, 'col', pairs)  20.3 us
    ppermute x11, waiting for transfers between devices, shift_row(): return lax.ppermute(block, 'row', pairs)  14.3 us
    ppermute x11, starting transfers between devices, shift_row(): return lax.ppermute(block, 'row', pairs)  13.8 us
    ppermute x2, starting transfers between devices, swap_cores(): return lax.ppermute(block, 'col', [(i, i ^ 1) for i in range(16)])  11.2 us
    ppermute x12, waiting for transfers between devices, shift_y(): return lax.ppermute(block, 'col', pairs)  8.77 us
    ppermute x3, starting transfers between devices, swap_z_hi(): return lax.ppermute(block, 'col', [(i, i ^ 8) for i in range(16)])  6.57 us
    ppermute x3, starting transfers between devices, flip(): return lax.ppermute(parts, 'row', [(i, i ^ row_bits) for i in range(8)])  5.24 us
  transfers between devices with their start and end apart: 36, of which 13 were waited for; matrix products, arithmetic and copies ran while one was open for 1% of the time, Pallas kernels for 17%

profile of v8, /device:TPU:1, one launch (start us, length us, event | category | flops | bytes accessed | tf_op | source)
XLA Modules:
  0.0 116.3 jit_solution(6572927762919697144)
XLA Ops:
  9.2 5.8 %collective-permute-done.1.refs_3_.refs_5_ = bf16[768,256]{1,0:T(8,128)(2,1)S(1)} collective-permute-done((bf16[768,256]{1,0:T(8,128)(2,1)S(1)}, bf16[768,256]{1,0:T(8,128)(2,1)S(1)}, u32[]{:S(2)}, u32[]{:S(2)}) %collective-permute-start.1) | collective-permute-done | bytes 393248 | tf_op jit(solution)/shard_map/ppermute | solution.py:28
  15.8 1.7 %collective-permute-start.6 = (bf16[768,256]{1,0:T(8,128)(2,1)S(1)}, bf16[768,256]{1,0:T(8,128)(2,1)}, u32[]{:S(2)}, u32[]{:S(2)}) collective-permute-start(bf16[768,256]{1,0:T(8,128)(2,1)S(1)} %constant_dynamic-slice_fusion.refs_4_), channel_id=1, source_target_pairs={{0,16},{16,0},{32,48},{48,32},{64,80},{80,64},{96,112},{112,96},{1... | collective-permute-start | bytes 1179656 | tf_op jit(solution)/shard_map/ppermute | solution.py:28
  18.6 1.8 %center_own.1 = (bf16[512,1536]{1,0:T(8,128)(2,1)S(1)}, f32[8,512]{1,0:T(8,128)S(1)}, f32[8,128]{1,0:T(8,128)S(1)}) custom-call(bf16[768,512]{1,0:T(8,128)(2,1)S(1)} %copy-done.1, bf16[768,512]{1,0:T(8,128)(2,1)S(1)} %collective-permute-done.refs_1_, bf16[768,512]{1,0:T(8,128)(2,1)S(1)} %copy-done.2, bf16[768,256]{1,0:T(8,128)(2,1)S(1)} %copy-done.4), custom_call_target="tpu_custom_call" | custom-call | tf_op jit(solution)/shard_map/center_own/pallas_call | solution.py:66
  20.5 2.8 %collective-permute-done.3.refs_8_ = bf16[768,256]{1,0:T(8,128)(2,1)} collective-permute-done((bf16[768,256]{1,0:T(8,128)(2,1)S(1)}, bf16[768,256]{1,0:T(8,128)(2,1)}, u32[]{:S(2)}, u32[]{:S(2)}) %collective-permute-start.3) | collective-permute-done | bytes 393248 | tf_op jit(solution)/shard_map/ppermute | solution.py:28
  23.3 2.6 %collective-permute-start.4 = (bf16[768,256]{1,0:T(8,128)(2,1)}, bf16[768,256]{1,0:T(8,128)(2,1)S(1)}, u32[]{:S(2)}, u32[]{:S(2)}) collective-permute-start(bf16[768,256]{1,0:T(8,128)(2,1)} %collective-permute-done.3.refs_8_), channel_id=1, source_target_pairs={{0,96},{16,112},{32,0},{48,16},{64,32},{80,48},{96,64},{112,80},{1... | collective-permute-start | bytes 1179656 | tf_op jit(solution)/shard_map/ppermute | solution.py:28
  25.9 4.5 %partial_near.1 = (f32[144,1024]{1,0:T(8,128)S(1)}, bf16[144,1024]{1,0:T(8,128)(2,1)S(1)}, bf16[144,1024]{1,0:T(8,128)(2,1)S(1)}, bf16[144,1024]{1,0:T(8,128)(2,...) custom-call(s32[5]{0:T(128)S(1)} %stack.23.refs_0_, bf16[512,1536]{1,0:T(8,128)(2,1)S(1)} %get-tuple-element.39.refs_1_, ...), custom_call_target="tpu_custom_call" | custom-call | flops 32212254720 | tf_op jit(solution)/shard_map/partial_near/pallas_call | solution.py:66
  33.4 1.8 %collective-permute-start.11 = (bf16[1536,256]{1,0:T(8,128)(2,1)S(1)}, bf16[1536,256]{1,0:T(8,128)(2,1)S(1)}, u32[]{:S(2)}, u32[]{:S(2)}) collective-permute-start(bf16[1536,256]{1,0:T(8,128)(2,1)S(1)} %join.3.refs_3_), channel_id=1, source_target_pairs={{0,16},{16,0},{32,48},{48,32},{64,80},{80,64},{96,112},{112,96},{1... | collective-permute-start | bytes 2359304 | tf_op jit(solution)/shard_map/ppermute | solution.py:28
  38.0 4.4 %collective-permute-done.12.refs_3_ = bf16[144,1024]{1,0:T(8,128)(2,1)S(1)} collective-permute-done((bf16[144,1024]{1,0:T(8,128)(2,1)S(1)}, bf16[144,1024]{1,0:T(8,128)(2,1)S(1)}, u32[]{:S(2)}, u32[]{:S(2)}) %collective-permute-start.12) | collective-permute-done | bytes 294944 | tf_op jit(solution)/shard_map/ppermute | solution.py:48
  42.4 2.6 %collective-permute-start.14 = (bf16[144,1024]{1,0:T(8,128)(2,1)S(1)}, bf16[144,1024]{1,0:T(8,128)(2,1)S(1)}, u32[]{:S(2)}, u32[]{:S(2)}) collective-permute-start(bf16[144,1024]{1,0:T(8,128)(2,1)S(1)} %get-tuple-element.53), channel_id=1, source_target_pairs={{0,4},{1,5},{2,6},{3,7},{4,0},{5,1},{6,2},{7,3},{8,12},{9,13},{10,... | collective-permute-start | bytes 884744 | tf_op jit(solution)/shard_map/ppermute | solution.py:48
  45.0 5.1 %collective-permute-done.10.refs_5_ = bf16[1536,256]{1,0:T(8,128)(2,1)S(1)} collective-permute-done((bf16[1536,256]{1,0:T(8,128)(2,1)S(1)}, bf16[1536,256]{1,0:T(8,128)(2,1)S(1)}, u32[]{:S(2)}, u32[]{:S(2)}) %collective-permute-start.10) | collective-permute-done | bytes 786464 | tf_op jit(solution)/shard_map/ppermute | solution.py:28
  50.4 3.7 %partial_far.1 = (f32[144,1024]{1,0:T(8,128)S(1)}, bf16[144,1024]{1,0:T(8,128)(2,1)S(1)}, bf16[144,1024]{1,0:T(8,128)(2,1)S(1)}, bf16[144,1024]{1,0:T(8,128)(2,1...) custom-call(s32[5]{0:T(128)S(1)} %stack.23.refs_0_, bf16[512,1536]{1,0:T(8,128)(2,1)S(1)} %get-tuple-element.39.refs_1_, ...), custom_call_target="tpu_custom_call" | custom-call | flops 32212254720 | tf_op jit(solution)/shard_map/partial_far/pallas_call | solution.py:66
  54.8 3.5 %collective-permute-start.15 = (bf16[160,1024]{1,0:T(8,128)(2,1)S(1)}, bf16[160,1024]{1,0:T(8,128)(2,1)S(1)}, u32[]{:S(2)}, u32[]{:S(2)}) collective-permute-start(bf16[160,1024]{1,0:T(8,128)(2,1)S(1)} %get-tuple-element.59), channel_id=1, source_target_pairs={{0,8},{1,9},{2,10},{3,11},{4,12},{5,13},{6,14},{7,15},{8,0},{9,1},... | collective-permute-start | bytes 983048 | tf_op jit(solution)/shard_map/ppermute | solution.py:57
  59.7 2.6 %collective-permute-start.17 = (bf16[144,1024]{1,0:T(8,128)(2,1)S(1)}, bf16[144,1024]{1,0:T(8,128)(2,1)S(1)}, u32[]{:S(2)}, u32[]{:S(2)}) collective-permute-start(bf16[144,1024]{1,0:T(8,128)(2,1)S(1)} %get-tuple-element.62), channel_id=1, source_target_pairs={{0,4},{1,5},{2,6},{3,7},{4,0},{5,1},{6,2},{7,3},{8,12},{9,13},{10,... | collective-permute-start | bytes 884744 | tf_op jit(solution)/shard_map/ppermute | solution.py:48
  63.3 2.2 %collective-permute-done.16.refs_6_.refs_3_ = bf16[144,1024]{1,0:T(8,128)(2,1)S(1)} collective-permute-done((bf16[144,1024]{1,0:T(8,128)(2,1)S(1)}, bf16[144,1024]{1,0:T(8,128)(2,1)S(1)}, u32[]{:S(2)}, u32[]{:S(2)}) %collective-permute-start.16) | collective-permute-done | bytes 294944 | tf_op jit(solution)/shard_map/ppermute | solution.py:48
  68.4 1.8 %collective-permute-done.17.refs_4_ = bf16[144,1024]{1,0:T(8,128)(2,1)S(1)} collective-permute-done((bf16[144,1024]{1,0:T(8,128)(2,1)S(1)}, bf16[144,1024]{1,0:T(8,128)(2,1)S(1)}, u32[]{:S(2)}, u32[]{:S(2)}) %collective-permute-start.17) | collective-permute-done | bytes 294944 | tf_op jit(solution)/shard_map/ppermute | solution.py:48
  71.4 2.6 %collective-permute-start.20 = (bf16[64,1024]{1,0:T(8,128)(2,1)S(1)}, bf16[64,1024]{1,0:T(8,128)(2,1)S(1)}, u32[]{:S(2)}, u32[]{:S(2)}) collective-permute-start(bf16[64,1024]{1,0:T(8,128)(2,1)S(1)} %get-tuple-element.69), channel_id=1, source_target_pairs={{0,8},{1,9},{2,10},{3,11},{4,12},{5,13},{6,14},{7,15},{8,0},{9,1},... | collective-permute-start | bytes 393224 | tf_op jit(solution)/shard_map/ppermute | solution.py:57
  74.0 3.8 %collective-permute-start.26 = (bf16[128,1024]{1,0:T(8,128)(2,1)S(1)}, bf16[128,1024]{1,0:T(8,128)(2,1)S(1)}, u32[]{:S(2)}, u32[]{:S(2)}) collective-permute-start(bf16[128,1024]{1,0:T(8,128)(2,1)S(1)} %get-tuple-element.64.refs_6_.refs_4_), channel_id=1, source_target_pairs={{0,4},{1,5},{2,6},{3,7},{4,0},{5,1},{6,2},{7,3},{8,12},{9,13},{10,... | collective-permute-start | bytes 786440 | tf_op jit(solution)/shard_map/ppermute | solution.py:48
  79.9 2.1 %collective-permute-start.25 = (bf16[128,1024]{1,0:T(8,128)(2,1)S(1)}, bf16[128,1024]{1,0:T(8,128)(2,1)S(1)}, u32[]{:S(2)}, u32[]{:S(2)}) collective-permute-start(bf16[128,1024]{1,0:T(8,128)(2,1)S(1)} %get-tuple-element.71.refs_3_.refs_4_), channel_id=1, source_target_pairs={{0,6},{1,7},{2,0},{3,1},{4,2},{5,3},{6,4},{7,5},{8,14},{9,15},{10,... | collective-permute-start | bytes 786440 | tf_op jit(solution)/shard_map/ppermute | solution.py:48
  82.0 2.5 %collective-permute-start.24 = (bf16[128,1024]{1,0:T(8,128)(2,1)S(1)}, bf16[128,1024]{1,0:T(8,128)(2,1)S(1)}, u32[]{:S(2)}, u32[]{:S(2)}) collective-permute-start(bf16[128,1024]{1,0:T(8,128)(2,1)S(1)} %get-tuple-element.71.refs_3_.refs_4_), channel_id=1, source_target_pairs={{0,4},{1,5},{2,6},{3,7},{4,0},{5,1},{6,2},{7,3},{8,12},{9,13},{10,... | collective-permute-start | bytes 786440 | tf_op jit(solution)/shard_map/ppermute | solution.py:48
  87.2 3.5 %collective-permute-start.28 = (f32[8,128]{1,0:T(8,128)S(1)}, f32[8,128]{1,0:T(8,128)S(1)}, u32[]{:S(2)}, u32[]{:S(2)}) collective-permute-start(f32[8,128]{1,0:T(8,128)S(1)} %pair_sum.2.refs_0_), channel_id=1, source_target_pairs={{0,64},{16,80},{32,96},{48,112},{64,0},{80,16},{96,32},{112,48},{1... | collective-permute-start | bytes 12296 | tf_op jit(solution)/shard_map/ppermute | solution.py:394
  91.1 2.8 %grad_near.1.refs_8_ = f32[1536,512]{1,0:T(8,128)S(1)} custom-call(s32[5]{0:T(128)S(1)} %stack.23.refs_0_, bf16[1536,1024]{1,0:T(8,128)(2,1)S(1)} %get-tuple-element.72.refs_1_, f32[8,1024]{1,0:T(8,128)S(1)} %get-tuple-element.43.refs_2_, f32[8,1024]{1,0:T(8,128)S(1)} %get-tuple-element.73.refs_3_, bf16[128,1024]{1,0:T(8,128)(2,1)S(1)} %get-tuple-element.64.refs_6_.refs_4_, ...), custom_call_target="tpu_custom_call" | custom-call | tf_op jit(solution)/shard_map/grad_near/pallas_call | solution.py:66
  94.3 2.0 %grad_far_sent.1.refs_10_ = bf16[768,512]{1,0:T(8,128)(2,1)S(1)} custom-call(s32[5]{0:T(128)S(1)} %stack.23.refs_0_, bf16[1536,1024]{1,0:T(8,128)(2,1)S(1)} %get-tuple-element.44.refs_1_, f32[8,1024]{1,0:T(8,128)S(1)} %get-tuple-element.45.refs_2_, f32[8,1024]{1,0:T(8,128)S(1)} %get-tuple-element.70.refs_3_, ...), custom_call_target="tpu_custom_call" | custom-call | tf_op jit(solution)/shard_map/grad_far_sent/pallas_call | solution.py:66
  96.3 9.7 %collective-permute-start.29 = (bf16[768,512]{1,0:T(8,128)(2,1)S(1)}, bf16[768,512]{1,0:T(8,128)(2,1)S(1)}, u32[]{:S(2)}, u32[]{:S(2)}) collective-permute-start(bf16[768,512]{1,0:T(8,128)(2,1)S(1)} %grad_far_sent.1.refs_10_), channel_id=1, source_target_pairs={{0,1},{1,0},{2,3},{3,2},{4,5},{5,4},{6,7},{7,6},{8,9},{9,8},{10,11... | collective-permute-start | bytes 2359304 | tf_op jit(solution)/shard_map/ppermute | solution.py:40
  112.8 2.0 %grad_far_kept.1 = f32[768,512]{1,0:T(8,128)S(1)} custom-call(s32[5]{0:T(128)S(1)} %stack.23.refs_0_, bf16[1536,1024]{1,0:T(8,128)(2,1)S(1)} %get-tuple-element.44.refs_1_, f32[8,1024]{1,0:T(8,128)S(1)} %get-tuple-element.45.refs_2_, f32[8,1024]{1,0:T(8,128)S(1)} %get-tuple-element.70.refs_3_, bf16[128,1024]{1,0:T(8,128)(2,1)S(1)} %get-tuple-element.71.refs_3_.refs_4_, ...), custom_call_target="tpu_custom_call" | custom-call | tf_op jit(solution)/shard_map/grad_far_kept/pallas_call | solution.py:66
  (79 shorter events, 37.6 us)
Async XLA Ops:
  3.2 11.9 %collective-permute-start.1 = (bf16[768,256]{1,0:T(8,128)(2,1)S(1)}, bf16[768,256]{1,0:T(8,128)(2,1)S(1)}, u32[]{:S(2)}, u32[]{:S(2)}) collective-permute-start(bf16[768,256]{1,0:T(8,128)(2,1)S(1)} %constant_dynamic-slice_fusion.1.refs_3_), channel_id=1, source_target_pairs={{0,32},{16,48},{32,64},{48,80},{64,96},{80,112},{96,0},{112,16},{1... | collective-permute-start | bytes 1179656 | tf_op jit(solution)/shard_map/ppermute | solution.py:28
  4.5 15.8 %collective-permute-start.8 = (bf16[768,256]{1,0:T(8,128)(2,1)S(1)}, bf16[768,256]{1,0:T(8,128)(2,1)}, u32[]{:S(2)}, u32[]{:S(2)}) collective-permute-start(bf16[768,256]{1,0:T(8,128)(2,1)S(1)} %constant_dynamic-slice_fusion.1.refs_3_), channel_id=1, source_target_pairs={{0,96},{16,112},{32,0},{48,16},{64,32},{80,48},{96,64},{112,80},{1... | collective-permute-start | bytes 1179656 | tf_op jit(solution)/shard_map/ppermute | solution.py:28
  6.0 17.4 %collective-permute-start.3 = (bf16[768,256]{1,0:T(8,128)(2,1)S(1)}, bf16[768,256]{1,0:T(8,128)(2,1)}, u32[]{:S(2)}, u32[]{:S(2)}) collective-permute-start(bf16[768,256]{1,0:T(8,128)(2,1)S(1)} %constant_dynamic-slice_fusion.refs_4_), channel_id=1, source_target_pairs={{0,96},{16,112},{32,0},{48,16},{64,32},{80,48},{96,64},{112,80},{1... | collective-permute-start | bytes 1179656 | tf_op jit(solution)/shard_map/ppermute | solution.py:28
  7.4 18.6 %collective-permute-start.5 = (bf16[768,256]{1,0:T(8,128)(2,1)S(1)}, bf16[768,256]{1,0:T(8,128)(2,1)S(1)}, u32[]{:S(2)}, u32[]{:S(2)}) collective-permute-start(bf16[768,256]{1,0:T(8,128)(2,1)S(1)} %constant_dynamic-slice_fusion.1.refs_3_), channel_id=1, source_target_pairs={{0,16},{16,0},{32,48},{48,32},{64,80},{80,64},{96,112},{112,96},{1... | collective-permute-start | bytes 1179656 | tf_op jit(solution)/shard_map/ppermute | solution.py:28
  9.0 16.9 %collective-permute-start.7 = (bf16[768,256]{1,0:T(8,128)(2,1)S(1)}, bf16[768,256]{1,0:T(8,128)(2,1)}, u32[]{:S(2)}, u32[]{:S(2)}) collective-permute-start(bf16[768,256]{1,0:T(8,128)(2,1)S(1)} %constant_dynamic-slice_fusion.refs_4_), channel_id=1, source_target_pairs={{0,32},{16,48},{32,64},{48,80},{64,96},{80,112},{96,0},{112,16},{1... | collective-permute-start | bytes 1179656 | tf_op jit(solution)/shard_map/ppermute | solution.py:28
  15.8 10.2 %collective-permute-start.6 = (bf16[768,256]{1,0:T(8,128)(2,1)S(1)}, bf16[768,256]{1,0:T(8,128)(2,1)}, u32[]{:S(2)}, u32[]{:S(2)}) collective-permute-start(bf16[768,256]{1,0:T(8,128)(2,1)S(1)} %constant_dynamic-slice_fusion.refs_4_), channel_id=1, source_target_pairs={{0,16},{16,0},{32,48},{48,32},{64,80},{80,64},{96,112},{112,96},{1... | collective-permute-start | bytes 1179656 | tf_op jit(solution)/shard_map/ppermute | solution.py:28
  20.4 12.7 %collective-permute-start.2 = (bf16[768,256]{1,0:T(8,128)(2,1)S(1)}, bf16[768,256]{1,0:T(8,128)(2,1)S(1)}, u32[]{:S(2)}, u32[]{:S(2)}) collective-permute-start(bf16[768,256]{1,0:T(8,128)(2,1)S(1)} %copy-done.4), channel_id=1, source_target_pairs={{0,32},{16,48},{32,64},{48,80},{64,96},{80,112},{96,0},{112,16},{1... | collective-permute-start | bytes 1179656 | tf_op jit(solution)/shard_map/ppermute | solution.py:28
  23.3 10.0 %collective-permute-start.4 = (bf16[768,256]{1,0:T(8,128)(2,1)}, bf16[768,256]{1,0:T(8,128)(2,1)S(1)}, u32[]{:S(2)}, u32[]{:S(2)}) collective-permute-start(bf16[768,256]{1,0:T(8,128)(2,1)} %collective-permute-done.3.refs_8_), channel_id=1, source_target_pairs={{0,96},{16,112},{32,0},{48,16},{64,32},{80,48},{96,64},{112,80},{1... | collective-permute-start | bytes 1179656 | tf_op jit(solution)/shard_map/ppermute | solution.py:28
  31.5 18.6 %collective-permute-start.10 = (bf16[1536,256]{1,0:T(8,128)(2,1)S(1)}, bf16[1536,256]{1,0:T(8,128)(2,1)S(1)}, u32[]{:S(2)}, u32[]{:S(2)}) collective-permute-start(bf16[1536,256]{1,0:T(8,128)(2,1)S(1)} %join.2.refs_2_), channel_id=1, source_target_pairs={{0,96},{16,112},{32,0},{48,16},{64,32},{80,48},{96,64},{112,80},{1... | collective-permute-start | bytes 2359304 | tf_op jit(solution)/shard_map/ppermute | solution.py:28
  32.5 17.8 %collective-permute-start.9 = (bf16[1536,256]{1,0:T(8,128)(2,1)S(1)}, bf16[1536,256]{1,0:T(8,128)(2,1)S(1)}, u32[]{:S(2)}, u32[]{:S(2)}) collective-permute-start(bf16[1536,256]{1,0:T(8,128)(2,1)S(1)} %join.2.refs_2_), channel_id=1, source_target_pairs={{0,32},{16,48},{32,64},{48,80},{64,96},{80,112},{96,0},{112,16},{1... | collective-permute-start | bytes 2359304 | tf_op jit(solution)/shard_map/ppermute | solution.py:28
  33.4 16.9 %collective-permute-start.11 = (bf16[1536,256]{1,0:T(8,128)(2,1)S(1)}, bf16[1536,256]{1,0:T(8,128)(2,1)S(1)}, u32[]{:S(2)}, u32[]{:S(2)}) collective-permute-start(bf16[1536,256]{1,0:T(8,128)(2,1)S(1)} %join.3.refs_3_), channel_id=1, source_target_pairs={{0,16},{16,0},{32,48},{48,32},{64,80},{80,64},{96,112},{112,96},{1... | collective-permute-start | bytes 2359304 | tf_op jit(solution)/shard_map/ppermute | solution.py:28
  35.2 7.1 %collective-permute-start.12 = (bf16[144,1024]{1,0:T(8,128)(2,1)S(1)}, bf16[144,1024]{1,0:T(8,128)(2,1)S(1)}, u32[]{:S(2)}, u32[]{:S(2)}) collective-permute-start(bf16[144,1024]{1,0:T(8,128)(2,1)S(1)} %get-tuple-element.48), channel_id=1, source_target_pairs={{0,2},{1,3},{2,4},{3,5},{4,6},{5,7},{6,0},{7,1},{8,10},{9,11},{10,... | collective-permute-start | bytes 884744 | tf_op jit(solution)/shard_map/ppermute | solution.py:48
  42.4 11.7 %collective-permute-start.14 = (bf16[144,1024]{1,0:T(8,128)(2,1)S(1)}, bf16[144,1024]{1,0:T(8,128)(2,1)S(1)}, u32[]{:S(2)}, u32[]{:S(2)}) collective-permute-start(bf16[144,1024]{1,0:T(8,128)(2,1)S(1)} %get-tuple-element.53), channel_id=1, source_target_pairs={{0,4},{1,5},{2,6},{3,7},{4,0},{5,1},{6,2},{7,3},{8,12},{9,13},{10,... | collective-permute-start | bytes 884744 | tf_op jit(solution)/shard_map/ppermute | solution.py:48
  54.8 10.7 %collective-permute-start.15 = (bf16[160,1024]{1,0:T(8,128)(2,1)S(1)}, bf16[160,1024]{1,0:T(8,128)(2,1)S(1)}, u32[]{:S(2)}, u32[]{:S(2)}) collective-permute-start(bf16[160,1024]{1,0:T(8,128)(2,1)S(1)} %get-tuple-element.59), channel_id=1, source_target_pairs={{0,8},{1,9},{2,10},{3,11},{4,12},{5,13},{6,14},{7,15},{8,0},{9,1},... | collective-permute-start | bytes 983048 | tf_op jit(solution)/shard_map/ppermute | solution.py:57
  59.7 10.6 %collective-permute-start.17 = (bf16[144,1024]{1,0:T(8,128)(2,1)S(1)}, bf16[144,1024]{1,0:T(8,128)(2,1)S(1)}, u32[]{:S(2)}, u32[]{:S(2)}) collective-permute-start(bf16[144,1024]{1,0:T(8,128)(2,1)S(1)} %get-tuple-element.62), channel_id=1, source_target_pairs={{0,4},{1,5},{2,6},{3,7},{4,0},{5,1},{6,2},{7,3},{8,12},{9,13},{10,... | collective-permute-start | bytes 884744 | tf_op jit(solution)/shard_map/ppermute | solution.py:48
  62.3 8.0 %collective-permute-start.18 = (bf16[144,1024]{1,0:T(8,128)(2,1)S(1)}, bf16[144,1024]{1,0:T(8,128)(2,1)S(1)}, u32[]{:S(2)}, u32[]{:S(2)}) collective-permute-start(bf16[144,1024]{1,0:T(8,128)(2,1)S(1)} %get-tuple-element.63), channel_id=1, source_target_pairs={{0,6},{1,7},{2,0},{3,1},{4,2},{5,3},{6,4},{7,5},{8,14},{9,15},{10,... | collective-permute-start | bytes 884744 | tf_op jit(solution)/shard_map/ppermute | solution.py:48
  66.9 11.5 %collective-permute-start.22 = (bf16[128,1024]{1,0:T(8,128)(2,1)S(1)}, bf16[128,1024]{1,0:T(8,128)(2,1)S(1)}, u32[]{:S(2)}, u32[]{:S(2)}) collective-permute-start(bf16[128,1024]{1,0:T(8,128)(2,1)S(1)} %get-tuple-element.64.refs_6_.refs_4_), channel_id=1, source_target_pairs={{0,6},{1,7},{2,0},{3,1},{4,2},{5,3},{6,4},{7,5},{8,14},{9,15},{10,... | collective-permute-start | bytes 786440 | tf_op jit(solution)/shard_map/ppermute | solution.py:48
  68.1 10.3 %collective-permute-start.21 = (bf16[128,1024]{1,0:T(8,128)(2,1)S(1)}, bf16[128,1024]{1,0:T(8,128)(2,1)S(1)}, u32[]{:S(2)}, u32[]{:S(2)}) collective-permute-start(bf16[128,1024]{1,0:T(8,128)(2,1)S(1)} %get-tuple-element.64.refs_6_.refs_4_), channel_id=1, source_target_pairs={{0,2},{1,3},{2,4},{3,5},{4,6},{5,7},{6,0},{7,1},{8,10},{9,11},{10,... | collective-permute-start | bytes 786440 | tf_op jit(solution)/shard_map/ppermute | solution.py:48
  71.0 7.5 %collective-permute-start.19 = (bf16[80,1024]{1,0:T(8,128)(2,1)S(1)}, bf16[80,1024]{1,0:T(8,128)(2,1)S(1)}, u32[]{:S(2)}, u32[]{:S(2)}) collective-permute-start(bf16[80,1024]{1,0:T(8,128)(2,1)S(1)} %get-tuple-element.68), channel_id=1, source_target_pairs={{0,8},{1,9},{2,10},{3,11},{4,12},{5,13},{6,14},{7,15},{8,0},{9,1},... | collective-permute-start | bytes 491528 | tf_op jit(solution)/shard_map/ppermute | solution.py:57
  74.0 17.0 %collective-permute-start.26 = (bf16[128,1024]{1,0:T(8,128)(2,1)S(1)}, bf16[128,1024]{1,0:T(8,128)(2,1)S(1)}, u32[]{:S(2)}, u32[]{:S(2)}) collective-permute-start(bf16[128,1024]{1,0:T(8,128)(2,1)S(1)} %get-tuple-element.64.refs_6_.refs_4_), channel_id=1, source_target_pairs={{0,4},{1,5},{2,6},{3,7},{4,0},{5,1},{6,2},{7,3},{8,12},{9,13},{10,... | collective-permute-start | bytes 786440 | tf_op jit(solution)/shard_map/ppermute | solution.py:48
  79.9 14.1 %collective-permute-start.25 = (bf16[128,1024]{1,0:T(8,128)(2,1)S(1)}, bf16[128,1024]{1,0:T(8,128)(2,1)S(1)}, u32[]{:S(2)}, u32[]{:S(2)}) collective-permute-start(bf16[128,1024]{1,0:T(8,128)(2,1)S(1)} %get-tuple-element.71.refs_3_.refs_4_), channel_id=1, source_target_pairs={{0,6},{1,7},{2,0},{3,1},{4,2},{5,3},{6,4},{7,5},{8,14},{9,15},{10,... | collective-permute-start | bytes 786440 | tf_op jit(solution)/shard_map/ppermute | solution.py:48
  82.0 12.0 %collective-permute-start.24 = (bf16[128,1024]{1,0:T(8,128)(2,1)S(1)}, bf16[128,1024]{1,0:T(8,128)(2,1)S(1)}, u32[]{:S(2)}, u32[]{:S(2)}) collective-permute-start(bf16[128,1024]{1,0:T(8,128)(2,1)S(1)} %get-tuple-element.71.refs_3_.refs_4_), channel_id=1, source_target_pairs={{0,4},{1,5},{2,6},{3,7},{4,0},{5,1},{6,2},{7,3},{8,12},{9,13},{10,... | collective-permute-start | bytes 786440 | tf_op jit(solution)/shard_map/ppermute | solution.py:48
  84.4 9.9 %collective-permute-start.23 = (bf16[128,1024]{1,0:T(8,128)(2,1)S(1)}, bf16[128,1024]{1,0:T(8,128)(2,1)S(1)}, u32[]{:S(2)}, u32[]{:S(2)}) collective-permute-start(bf16[128,1024]{1,0:T(8,128)(2,1)S(1)} %get-tuple-element.71.refs_3_.refs_4_), channel_id=1, source_target_pairs={{0,2},{1,3},{2,4},{3,5},{4,6},{5,7},{6,0},{7,1},{8,10},{9,11},{10,... | collective-permute-start | bytes 786440 | tf_op jit(solution)/shard_map/ppermute | solution.py:48
  96.3 18.6 %collective-permute-start.29 = (bf16[768,512]{1,0:T(8,128)(2,1)S(1)}, bf16[768,512]{1,0:T(8,128)(2,1)S(1)}, u32[]{:S(2)}, u32[]{:S(2)}) collective-permute-start(bf16[768,512]{1,0:T(8,128)(2,1)S(1)} %grad_far_sent.1.refs_10_), channel_id=1, source_target_pairs={{0,1},{1,0},{2,3},{3,2},{4,5},{5,4},{6,7},{7,6},{8,9},{9,8},{10,11... | collective-permute-start | bytes 2359304 | tf_op jit(solution)/shard_map/ppermute | solution.py:40
  (17 other events, 92.0 us)

commit v9 on v7

--- a/solution.py
+++ b/solution.py
@@ -490,6 +490,7 @@
     plane, upper, message, local, row_local = combine_y(
         place, parts, near_sums, True, "combine_y_near", [far_sums[0]]
     )
+    *far_sums, plane = lax.optimization_barrier((*far_sums, plane))
     for d in (1, 3, 2):
         far_sums[d] = shift_y(far_sums[d], d)
     near_masked, parts, near_means, row_offsets, row_stats = combine_z(
@@ -503,7 +504,7 @@
     far_masked, parts, far_means = combine_z(
         place, far_plane, far_local, row_offsets, swap_z_hi(far_upper), swap_z_hi(far_message),
         parts, False,
-        "combine_z_far", near_pieces[1:],
+        "combine_z_far", [near_pieces[1], near_pieces[3]],
     )
     far_pieces = sent_round(far_masked)
 

time: 118 us -> 117 us (level)
  waiting for transfers between devices: 33.7 us -> 31.3 us
  starting transfers between devices: 55.9 us -> 57.3 us
    ppermute x4, waiting for transfers between devices: 9.93 us -> 7.23 us  [swap_z_hi(): return lax.ppermute(block, 'col', [(i, i ^ 8) for i in range(16)])]
  transfers between devices with their start and end apart: 37 -> 37, of which waited for: 12 -> 12; matrix products, arithmetic and copies ran while one was open for 1% -> 1% of each run, Pallas kernels for 16% -> 17%
where the time goes in v9:
time: 117 us; the launch traced here: 116 us
  starting transfers between devices  57.3 us (49%)
  waiting for transfers between devices  31.3 us (27%)
  Pallas kernels  23.4 us (20%)
  local copies, waits for them, and re-layouts  3.18 us (3%)
    pallas_call x17, Pallas kernels, call(): pl.pallas_call(kernel, out_shape=tuple(outs), in_specs=[SMEM if a.dtype =...  23.4 us
    ppermute x12, starting transfers between devices, shift_y(): return lax.ppermute(block, 'col', pairs)  18.3 us
    ppermute x11, waiting for transfers between devices, shift_row(): return lax.ppermute(block, 'row', pairs)  14.3 us
    ppermute x11, starting transfers between devices, shift_row(): return lax.ppermute(block, 'row', pairs)  13.8 us
    ppermute x2, starting transfers between devices, swap_cores(): return lax.ppermute(block, 'col', [(i, i ^ 1) for i in range(16)])  9.1 us
    ppermute x4, waiting for transfers between devices, swap_z_hi(): return lax.ppermute(block, 'col', [(i, i ^ 8) for i in range(16)])  7.23 us
    ppermute x4, starting transfers between devices, swap_z_hi(): return lax.ppermute(block, 'col', [(i, i ^ 8) for i in range(16)])  6.5 us
    ppermute x12, waiting for transfers between devices, shift_y(): return lax.ppermute(block, 'col', pairs)  6.46 us
  transfers between devices with their start and end apart: 37, of which 12 were waited for; matrix products, arithmetic and copies ran while one was open for 1% of the time, Pallas kernels for 17%

profile of v9, /device:TPU:1, one launch (start us, length us, event | category | flops | bytes accessed | tf_op | source)
XLA Modules:
  0.0 116.3 jit_solution(16060782448677712789)
XLA Ops:
  9.2 5.8 %collective-permute-done.1.refs_3_.refs_5_ = bf16[768,256]{1,0:T(8,128)(2,1)S(1)} collective-permute-done((bf16[768,256]{1,0:T(8,128)(2,1)S(1)}, bf16[768,256]{1,0:T(8,128)(2,1)S(1)}, u32[]{:S(2)}, u32[]{:S(2)}) %collective-permute-start.1) | collective-permute-done | bytes 393248 | tf_op jit(solution)/shard_map/ppermute | solution.py:28
  18.6 1.8 %center_own.1 = (bf16[512,1536]{1,0:T(8,128)(2,1)S(1)}, f32[8,512]{1,0:T(8,128)S(1)}, f32[8,128]{1,0:T(8,128)S(1)}) custom-call(bf16[768,512]{1,0:T(8,128)(2,1)S(1)} %copy-done.1, bf16[768,512]{1,0:T(8,128)(2,1)S(1)} %collective-permute-done.refs_1_, bf16[768,512]{1,0:T(8,128)(2,1)S(1)} %copy-done.2, bf16[768,256]{1,0:T(8,128)(2,1)S(1)} %copy-done.4), custom_call_target="tpu_custom_call" | custom-call | tf_op jit(solution)/shard_map/center_own/pallas_call | solution.py:66
  20.5 2.8 %collective-permute-done.3.refs_8_ = bf16[768,256]{1,0:T(8,128)(2,1)} collective-permute-done((bf16[768,256]{1,0:T(8,128)(2,1)S(1)}, bf16[768,256]{1,0:T(8,128)(2,1)}, u32[]{:S(2)}, u32[]{:S(2)}) %collective-permute-start.3) | collective-permute-done | bytes 393248 | tf_op jit(solution)/shard_map/ppermute | solution.py:28
  23.3 2.6 %collective-permute-start.4 = (bf16[768,256]{1,0:T(8,128)(2,1)}, bf16[768,256]{1,0:T(8,128)(2,1)S(1)}, u32[]{:S(2)}, u32[]{:S(2)}) collective-permute-start(bf16[768,256]{1,0:T(8,128)(2,1)} %collective-permute-done.3.refs_8_), channel_id=1, source_target_pairs={{0,96},{16,112},{32,0},{48,16},{64,32},{80,48},{96,64},{112,80},{1... | collective-permute-start | bytes 1179656 | tf_op jit(solution)/shard_map/ppermute | solution.py:28
  25.9 4.5 %partial_near.1 = (f32[144,1024]{1,0:T(8,128)S(1)}, bf16[144,1024]{1,0:T(8,128)(2,1)S(1)}, bf16[144,1024]{1,0:T(8,128)(2,1)S(1)}, bf16[144,1024]{1,0:T(8,128)(2,...) custom-call(s32[5]{0:T(128)S(1)} %stack.23.refs_0_, bf16[512,1536]{1,0:T(8,128)(2,1)S(1)} %get-tuple-element.45.refs_1_, ...), custom_call_target="tpu_custom_call" | custom-call | flops 32212254720 | tf_op jit(solution)/shard_map/partial_near/pallas_call | solution.py:66
  33.4 1.8 %collective-permute-start.11 = (bf16[1536,256]{1,0:T(8,128)(2,1)S(1)}, bf16[1536,256]{1,0:T(8,128)(2,1)S(1)}, u32[]{:S(2)}, u32[]{:S(2)}) collective-permute-start(bf16[1536,256]{1,0:T(8,128)(2,1)S(1)} %join.3.refs_3_), channel_id=1, source_target_pairs={{0,16},{16,0},{32,48},{48,32},{64,80},{80,64},{96,112},{112,96},{1... | collective-permute-start | bytes 2359304 | tf_op jit(solution)/shard_map/ppermute | solution.py:28
  38.0 4.4 %collective-permute-done.12.refs_3_ = bf16[144,1024]{1,0:T(8,128)(2,1)S(1)} collective-permute-done((bf16[144,1024]{1,0:T(8,128)(2,1)S(1)}, bf16[144,1024]{1,0:T(8,128)(2,1)S(1)}, u32[]{:S(2)}, u32[]{:S(2)}) %collective-permute-start.12) | collective-permute-done | bytes 294944 | tf_op jit(solution)/shard_map/ppermute | solution.py:48
  42.4 2.6 %collective-permute-start.14 = (bf16[144,1024]{1,0:T(8,128)(2,1)S(1)}, bf16[144,1024]{1,0:T(8,128)(2,1)S(1)}, u32[]{:S(2)}, u32[]{:S(2)}) collective-permute-start(bf16[144,1024]{1,0:T(8,128)(2,1)S(1)} %get-tuple-element.63), channel_id=1, source_target_pairs={{0,4},{1,5},{2,6},{3,7},{4,0},{5,1},{6,2},{7,3},{8,12},{9,13},{10,... | collective-permute-start | bytes 884744 | tf_op jit(solution)/shard_map/ppermute | solution.py:48
  45.0 5.1 %collective-permute-done.10.refs_5_ = bf16[1536,256]{1,0:T(8,128)(2,1)S(1)} collective-permute-done((bf16[1536,256]{1,0:T(8,128)(2,1)S(1)}, bf16[1536,256]{1,0:T(8,128)(2,1)S(1)}, u32[]{:S(2)}, u32[]{:S(2)}) %collective-permute-start.10) | collective-permute-done | bytes 786464 | tf_op jit(solution)/shard_map/ppermute | solution.py:28
  50.4 3.7 %partial_far.1 = (f32[144,1024]{1,0:T(8,128)S(1)}, bf16[144,1024]{1,0:T(8,128)(2,1)S(1)}, bf16[144,1024]{1,0:T(8,128)(2,1)S(1)}, bf16[144,1024]{1,0:T(8,128)(2,1...) custom-call(s32[5]{0:T(128)S(1)} %stack.23.refs_0_, bf16[512,1536]{1,0:T(8,128)(2,1)S(1)} %get-tuple-element.45.refs_1_, ...), custom_call_target="tpu_custom_call" | custom-call | flops 32212254720 | tf_op jit(solution)/shard_map/partial_far/pallas_call | solution.py:66
  56.2 3.4 %collective-permute-start.16 = (bf16[96,1024]{1,0:T(8,128)(2,1)S(1)}, bf16[96,1024]{1,0:T(8,128)(2,1)S(1)}, u32[]{:S(2)}, u32[]{:S(2)}) collective-permute-start(bf16[96,1024]{1,0:T(8,128)(2,1)S(1)} %get-tuple-element.70), channel_id=1, source_target_pairs={{0,8},{1,9},{2,10},{3,11},{4,12},{5,13},{6,14},{7,15},{8,0},{9,1},... | collective-permute-start | bytes 589832 | tf_op jit(solution)/shard_map/ppermute | solution.py:57
  59.6 2.6 %collective-permute-start.18 = (bf16[144,1024]{1,0:T(8,128)(2,1)S(1)}, bf16[144,1024]{1,0:T(8,128)(2,1)S(1)}, u32[]{:S(2)}, u32[]{:S(2)}) collective-permute-start(bf16[144,1024]{1,0:T(8,128)(2,1)S(1)} %get-tuple-element.74), channel_id=1, source_target_pairs={{0,4},{1,5},{2,6},{3,7},{4,0},{5,1},{6,2},{7,3},{8,12},{9,13},{10,... | collective-permute-start | bytes 884744 | tf_op jit(solution)/shard_map/ppermute | solution.py:48
  63.3 5.3 %collective-permute-done.15.refs_4_ = bf16[64,1024]{1,0:T(8,128)(2,1)S(1)} collective-permute-done((bf16[64,1024]{1,0:T(8,128)(2,1)S(1)}, bf16[64,1024]{1,0:T(8,128)(2,1)S(1)}, u32[]{:S(2)}, u32[]{:S(2)}) %collective-permute-start.15) | collective-permute-done | bytes 131104 | tf_op jit(solution)/shard_map/ppermute | solution.py:57
  70.1 1.8 %collective-permute-start.23 = (bf16[128,1024]{1,0:T(8,128)(2,1)S(1)}, bf16[128,1024]{1,0:T(8,128)(2,1)S(1)}, u32[]{:S(2)}, u32[]{:S(2)}) collective-permute-start(bf16[128,1024]{1,0:T(8,128)(2,1)S(1)} %get-tuple-element.76.refs_6_.refs_4_), channel_id=1, source_target_pairs={{0,6},{1,7},{2,0},{3,1},{4,2},{5,3},{6,4},{7,5},{8,14},{9,15},{10,... | collective-permute-start | bytes 786440 | tf_op jit(solution)/shard_map/ppermute | solution.py:48
  73.6 2.1 %collective-permute-start.20 = (bf16[64,1024]{1,0:T(8,128)(2,1)S(1)}, bf16[64,1024]{1,0:T(8,128)(2,1)S(1)}, u32[]{:S(2)}, u32[]{:S(2)}) collective-permute-start(bf16[64,1024]{1,0:T(8,128)(2,1)S(1)} %get-tuple-element.80), channel_id=1, source_target_pairs={{0,8},{1,9},{2,10},{3,11},{4,12},{5,13},{6,14},{7,15},{8,0},{9,1},... | collective-permute-start | bytes 393224 | tf_op jit(solution)/shard_map/ppermute | solution.py:57
  75.6 2.2 %collective-permute-start.27 = (bf16[128,1024]{1,0:T(8,128)(2,1)S(1)}, bf16[128,1024]{1,0:T(8,128)(2,1)S(1)}, u32[]{:S(2)}, u32[]{:S(2)}) collective-permute-start(bf16[128,1024]{1,0:T(8,128)(2,1)S(1)} %get-tuple-element.76.refs_6_.refs_4_), channel_id=1, source_target_pairs={{0,4},{1,5},{2,6},{3,7},{4,0},{5,1},{6,2},{7,3},{8,12},{9,13},{10,... | collective-permute-start | bytes 786440 | tf_op jit(solution)/shard_map/ppermute | solution.py:48
  77.8 1.9 %collective-permute-done.20.refs_4_ = bf16[64,1024]{1,0:T(8,128)(2,1)S(1)} collective-permute-done((bf16[64,1024]{1,0:T(8,128)(2,1)S(1)}, bf16[64,1024]{1,0:T(8,128)(2,1)S(1)}, u32[]{:S(2)}, u32[]{:S(2)}) %collective-permute-start.20) | collective-permute-done | bytes 131104 | tf_op jit(solution)/shard_map/ppermute | solution.py:57
  81.2 3.2 %collective-permute-start.26 = (bf16[128,1024]{1,0:T(8,128)(2,1)S(1)}, bf16[128,1024]{1,0:T(8,128)(2,1)S(1)}, u32[]{:S(2)}, u32[]{:S(2)}) collective-permute-start(bf16[128,1024]{1,0:T(8,128)(2,1)S(1)} %get-tuple-element.83.refs_3_.refs_4_), channel_id=1, source_target_pairs={{0,6},{1,7},{2,0},{3,1},{4,2},{5,3},{6,4},{7,5},{8,14},{9,15},{10,... | collective-permute-start | bytes 786440 | tf_op jit(solution)/shard_map/ppermute | solution.py:48
  87.5 3.6 %collective-permute-start.29 = (f32[8,128]{1,0:T(8,128)S(1)}, f32[8,128]{1,0:T(8,128)S(1)}, u32[]{:S(2)}, u32[]{:S(2)}) collective-permute-start(f32[8,128]{1,0:T(8,128)S(1)} %pair_sum.2.refs_0_), channel_id=1, source_target_pairs={{0,64},{16,80},{32,96},{48,112},{64,0},{80,16},{96,32},{112,48},{1... | collective-permute-start | bytes 12296 | tf_op jit(solution)/shard_map/ppermute | solution.py:387
  91.5 2.8 %grad_near.1.refs_8_ = f32[1536,512]{1,0:T(8,128)S(1)} custom-call(s32[5]{0:T(128)S(1)} %stack.23.refs_0_, bf16[1536,1024]{1,0:T(8,128)(2,1)S(1)} %get-tuple-element.84.refs_1_, f32[8,1024]{1,0:T(8,128)S(1)} %get-tuple-element.49.refs_2_, f32[8,1024]{1,0:T(8,128)S(1)} %get-tuple-element.85.refs_3_, bf16[128,1024]{1,0:T(8,128)(2,1)S(1)} %get-tuple-element.76.refs_6_.refs_4_, ...), custom_call_target="tpu_custom_call" | custom-call | tf_op jit(solution)/shard_map/grad_near/pallas_call | solution.py:66
  94.4 2.0 %collective-permute-done.24.refs_5_ = bf16[128,1024]{1,0:T(8,128)(2,1)S(1)} collective-permute-done((bf16[128,1024]{1,0:T(8,128)(2,1)S(1)}, bf16[128,1024]{1,0:T(8,128)(2,1)S(1)}, u32[]{:S(2)}, u32[]{:S(2)}) %collective-permute-start.24) | collective-permute-done | bytes 262176 | tf_op jit(solution)/shard_map/ppermute | solution.py:48
  96.4 2.0 %grad_far_sent.1.refs_10_ = bf16[768,512]{1,0:T(8,128)(2,1)S(1)} custom-call(s32[5]{0:T(128)S(1)} %stack.23.refs_0_, bf16[1536,1024]{1,0:T(8,128)(2,1)S(1)} %get-tuple-element.50.refs_1_, f32[8,1024]{1,0:T(8,128)S(1)} %get-tuple-element.51.refs_2_, f32[8,1024]{1,0:T(8,128)S(1)} %get-tuple-element.82.refs_3_, ...), custom_call_target="tpu_custom_call" | custom-call | tf_op jit(solution)/shard_map/grad_far_sent/pallas_call | solution.py:66
  98.3 7.6 %collective-permute-start.30 = (bf16[768,512]{1,0:T(8,128)(2,1)S(1)}, bf16[768,512]{1,0:T(8,128)(2,1)S(1)}, u32[]{:S(2)}, u32[]{:S(2)}) collective-permute-start(bf16[768,512]{1,0:T(8,128)(2,1)S(1)} %grad_far_sent.1.refs_10_), channel_id=1, source_target_pairs={{0,1},{1,0},{2,3},{3,2},{4,5},{5,4},{6,7},{7,6},{8,9},{9,8},{10,11... | collective-permute-start | bytes 2359304 | tf_op jit(solution)/shard_map/ppermute | solution.py:40
  112.8 2.0 %grad_far_kept.1 = f32[768,512]{1,0:T(8,128)S(1)} custom-call(s32[5]{0:T(128)S(1)} %stack.23.refs_0_, bf16[1536,1024]{1,0:T(8,128)(2,1)S(1)} %get-tuple-element.50.refs_1_, f32[8,1024]{1,0:T(8,128)S(1)} %get-tuple-element.51.refs_2_, f32[8,1024]{1,0:T(8,128)S(1)} %get-tuple-element.82.refs_3_, bf16[128,1024]{1,0:T(8,128)(2,1)S(1)} %get-tuple-element.83.refs_3_.refs_4_, ...), custom_call_target="tpu_custom_call" | custom-call | tf_op jit(solution)/shard_map/grad_far_kept/pallas_call | solution.py:66
  (81 shorter events, 37.8 us)
Async XLA Ops:
  3.2 11.9 %collective-permute-start.1 = (bf16[768,256]{1,0:T(8,128)(2,1)S(1)}, bf16[768,256]{1,0:T(8,128)(2,1)S(1)}, u32[]{:S(2)}, u32[]{:S(2)}) collective-permute-start(bf16[768,256]{1,0:T(8,128)(2,1)S(1)} %constant_dynamic-slice_fusion.1.refs_3_), channel_id=1, source_target_pairs={{0,32},{16,48},{32,64},{48,80},{64,96},{80,112},{96,0},{112,16},{1... | collective-permute-start | bytes 1179656 | tf_op jit(solution)/shard_map/ppermute | solution.py:28
  4.5 15.8 %collective-permute-start.8 = (bf16[768,256]{1,0:T(8,128)(2,1)S(1)}, bf16[768,256]{1,0:T(8,128)(2,1)}, u32[]{:S(2)}, u32[]{:S(2)}) collective-permute-start(bf16[768,256]{1,0:T(8,128)(2,1)S(1)} %constant_dynamic-slice_fusion.1.refs_3_), channel_id=1, source_target_pairs={{0,96},{16,112},{32,0},{48,16},{64,32},{80,48},{96,64},{112,80},{1... | collective-permute-start | bytes 1179656 | tf_op jit(solution)/shard_map/ppermute | solution.py:28
  6.0 17.4 %collective-permute-start.3 = (bf16[768,256]{1,0:T(8,128)(2,1)S(1)}, bf16[768,256]{1,0:T(8,128)(2,1)}, u32[]{:S(2)}, u32[]{:S(2)}) collective-permute-start(bf16[768,256]{1,0:T(8,128)(2,1)S(1)} %constant_dynamic-slice_fusion.refs_4_), channel_id=1, source_target_pairs={{0,96},{16,112},{32,0},{48,16},{64,32},{80,48},{96,64},{112,80},{1... | collective-permute-start | bytes 1179656 | tf_op jit(solution)/shard_map/ppermute | solution.py:28
  7.4 18.6 %collective-permute-start.5 = (bf16[768,256]{1,0:T(8,128)(2,1)S(1)}, bf16[768,256]{1,0:T(8,128)(2,1)S(1)}, u32[]{:S(2)}, u32[]{:S(2)}) collective-permute-start(bf16[768,256]{1,0:T(8,128)(2,1)S(1)} %constant_dynamic-slice_fusion.1.refs_3_), channel_id=1, source_target_pairs={{0,16},{16,0},{32,48},{48,32},{64,80},{80,64},{96,112},{112,96},{1... | collective-permute-start | bytes 1179656 | tf_op jit(solution)/shard_map/ppermute | solution.py:28
  9.0 16.9 %collective-permute-start.7 = (bf16[768,256]{1,0:T(8,128)(2,1)S(1)}, bf16[768,256]{1,0:T(8,128)(2,1)}, u32[]{:S(2)}, u32[]{:S(2)}) collective-permute-start(bf16[768,256]{1,0:T(8,128)(2,1)S(1)} %constant_dynamic-slice_fusion.refs_4_), channel_id=1, source_target_pairs={{0,32},{16,48},{32,64},{48,80},{64,96},{80,112},{96,0},{112,16},{1... | collective-permute-start | bytes 1179656 | tf_op jit(solution)/shard_map/ppermute | solution.py:28
  15.8 10.2 %collective-permute-start.6 = (bf16[768,256]{1,0:T(8,128)(2,1)S(1)}, bf16[768,256]{1,0:T(8,128)(2,1)}, u32[]{:S(2)}, u32[]{:S(2)}) collective-permute-start(bf16[768,256]{1,0:T(8,128)(2,1)S(1)} %constant_dynamic-slice_fusion.refs_4_), channel_id=1, source_target_pairs={{0,16},{16,0},{32,48},{48,32},{64,80},{80,64},{96,112},{112,96},{1... | collective-permute-start | bytes 1179656 | tf_op jit(solution)/shard_map/ppermute | solution.py:28
  20.4 12.7 %collective-permute-start.2 = (bf16[768,256]{1,0:T(8,128)(2,1)S(1)}, bf16[768,256]{1,0:T(8,128)(2,1)S(1)}, u32[]{:S(2)}, u32[]{:S(2)}) collective-permute-start(bf16[768,256]{1,0:T(8,128)(2,1)S(1)} %copy-done.4), channel_id=1, source_target_pairs={{0,32},{16,48},{32,64},{48,80},{64,96},{80,112},{96,0},{112,16},{1... | collective-permute-start | bytes 1179656 | tf_op jit(solution)/shard_map/ppermute | solution.py:28
  23.3 10.0 %collective-permute-start.4 = (bf16[768,256]{1,0:T(8,128)(2,1)}, bf16[768,256]{1,0:T(8,128)(2,1)S(1)}, u32[]{:S(2)}, u32[]{:S(2)}) collective-permute-start(bf16[768,256]{1,0:T(8,128)(2,1)} %collective-permute-done.3.refs_8_), channel_id=1, source_target_pairs={{0,96},{16,112},{32,0},{48,16},{64,32},{80,48},{96,64},{112,80},{1... | collective-permute-start | bytes 1179656 | tf_op jit(solution)/shard_map/ppermute | solution.py:28
  31.5 18.6 %collective-permute-start.10 = (bf16[1536,256]{1,0:T(8,128)(2,1)S(1)}, bf16[1536,256]{1,0:T(8,128)(2,1)S(1)}, u32[]{:S(2)}, u32[]{:S(2)}) collective-permute-start(bf16[1536,256]{1,0:T(8,128)(2,1)S(1)} %join.2.refs_2_), channel_id=1, source_target_pairs={{0,96},{16,112},{32,0},{48,16},{64,32},{80,48},{96,64},{112,80},{1... | collective-permute-start | bytes 2359304 | tf_op jit(solution)/shard_map/ppermute | solution.py:28
  32.5 17.8 %collective-permute-start.9 = (bf16[1536,256]{1,0:T(8,128)(2,1)S(1)}, bf16[1536,256]{1,0:T(8,128)(2,1)S(1)}, u32[]{:S(2)}, u32[]{:S(2)}) collective-permute-start(bf16[1536,256]{1,0:T(8,128)(2,1)S(1)} %join.2.refs_2_), channel_id=1, source_target_pairs={{0,32},{16,48},{32,64},{48,80},{64,96},{80,112},{96,0},{112,16},{1... | collective-permute-start | bytes 2359304 | tf_op jit(solution)/shard_map/ppermute | solution.py:28
  33.4 16.9 %collective-permute-start.11 = (bf16[1536,256]{1,0:T(8,128)(2,1)S(1)}, bf16[1536,256]{1,0:T(8,128)(2,1)S(1)}, u32[]{:S(2)}, u32[]{:S(2)}) collective-permute-start(bf16[1536,256]{1,0:T(8,128)(2,1)S(1)} %join.3.refs_3_), channel_id=1, source_target_pairs={{0,16},{16,0},{32,48},{48,32},{64,80},{80,64},{96,112},{112,96},{1... | collective-permute-start | bytes 2359304 | tf_op jit(solution)/shard_map/ppermute | solution.py:28
  42.4 11.7 %collective-permute-start.14 = (bf16[144,1024]{1,0:T(8,128)(2,1)S(1)}, bf16[144,1024]{1,0:T(8,128)(2,1)S(1)}, u32[]{:S(2)}, u32[]{:S(2)}) collective-permute-start(bf16[144,1024]{1,0:T(8,128)(2,1)S(1)} %get-tuple-element.63), channel_id=1, source_target_pairs={{0,4},{1,5},{2,6},{3,7},{4,0},{5,1},{6,2},{7,3},{8,12},{9,13},{10,... | collective-permute-start | bytes 884744 | tf_op jit(solution)/shard_map/ppermute | solution.py:48
  54.8 13.8 %collective-permute-start.17 = (bf16[144,1024]{1,0:T(8,128)(2,1)S(1)}, bf16[144,1024]{1,0:T(8,128)(2,1)S(1)}, u32[]{:S(2)}, u32[]{:S(2)}) collective-permute-start(bf16[144,1024]{1,0:T(8,128)(2,1)S(1)} %get-tuple-element.71), channel_id=1, source_target_pairs={{0,2},{1,3},{2,4},{3,5},{4,6},{5,7},{6,0},{7,1},{8,10},{9,11},{10,... | collective-permute-start | bytes 884744 | tf_op jit(solution)/shard_map/ppermute | solution.py:48
  56.2 12.5 %collective-permute-start.16 = (bf16[96,1024]{1,0:T(8,128)(2,1)S(1)}, bf16[96,1024]{1,0:T(8,128)(2,1)S(1)}, u32[]{:S(2)}, u32[]{:S(2)}) collective-permute-start(bf16[96,1024]{1,0:T(8,128)(2,1)S(1)} %get-tuple-element.70), channel_id=1, source_target_pairs={{0,8},{1,9},{2,10},{3,11},{4,12},{5,13},{6,14},{7,15},{8,0},{9,1},... | collective-permute-start | bytes 589832 | tf_op jit(solution)/shard_map/ppermute | solution.py:57
  59.6 12.2 %collective-permute-start.18 = (bf16[144,1024]{1,0:T(8,128)(2,1)S(1)}, bf16[144,1024]{1,0:T(8,128)(2,1)S(1)}, u32[]{:S(2)}, u32[]{:S(2)}) collective-permute-start(bf16[144,1024]{1,0:T(8,128)(2,1)S(1)} %get-tuple-element.74), channel_id=1, source_target_pairs={{0,4},{1,5},{2,6},{3,7},{4,0},{5,1},{6,2},{7,3},{8,12},{9,13},{10,... | collective-permute-start | bytes 884744 | tf_op jit(solution)/shard_map/ppermute | solution.py:48
  62.3 9.6 %collective-permute-start.19 = (bf16[144,1024]{1,0:T(8,128)(2,1)S(1)}, bf16[144,1024]{1,0:T(8,128)(2,1)S(1)}, u32[]{:S(2)}, u32[]{:S(2)}) collective-permute-start(bf16[144,1024]{1,0:T(8,128)(2,1)S(1)} %get-tuple-element.75), channel_id=1, source_target_pairs={{0,6},{1,7},{2,0},{3,1},{4,2},{5,3},{6,4},{7,5},{8,14},{9,15},{10,... | collective-permute-start | bytes 884744 | tf_op jit(solution)/shard_map/ppermute | solution.py:48
  70.1 9.7 %collective-permute-start.23 = (bf16[128,1024]{1,0:T(8,128)(2,1)S(1)}, bf16[128,1024]{1,0:T(8,128)(2,1)S(1)}, u32[]{:S(2)}, u32[]{:S(2)}) collective-permute-start(bf16[128,1024]{1,0:T(8,128)(2,1)S(1)} %get-tuple-element.76.refs_6_.refs_4_), channel_id=1, source_target_pairs={{0,6},{1,7},{2,0},{3,1},{4,2},{5,3},{6,4},{7,5},{8,14},{9,15},{10,... | collective-permute-start | bytes 786440 | tf_op jit(solution)/shard_map/ppermute | solution.py:48
  71.9 7.9 %collective-permute-start.22 = (bf16[128,1024]{1,0:T(8,128)(2,1)S(1)}, bf16[128,1024]{1,0:T(8,128)(2,1)S(1)}, u32[]{:S(2)}, u32[]{:S(2)}) collective-permute-start(bf16[128,1024]{1,0:T(8,128)(2,1)S(1)} %get-tuple-element.76.refs_6_.refs_4_), channel_id=1, source_target_pairs={{0,2},{1,3},{2,4},{3,5},{4,6},{5,7},{6,0},{7,1},{8,10},{9,11},{10,... | collective-permute-start | bytes 786440 | tf_op jit(solution)/shard_map/ppermute | solution.py:48
  72.6 7.2 %collective-permute-start.21 = (bf16[80,1024]{1,0:T(8,128)(2,1)S(1)}, bf16[80,1024]{1,0:T(8,128)(2,1)S(1)}, u32[]{:S(2)}, u32[]{:S(2)}) collective-permute-start(bf16[80,1024]{1,0:T(8,128)(2,1)S(1)} %get-tuple-element.81), channel_id=1, source_target_pairs={{0,8},{1,9},{2,10},{3,11},{4,12},{5,13},{6,14},{7,15},{8,0},{9,1},... | collective-permute-start | bytes 491528 | tf_op jit(solution)/shard_map/ppermute | solution.py:57
  75.6 15.9 %collective-permute-start.27 = (bf16[128,1024]{1,0:T(8,128)(2,1)S(1)}, bf16[128,1024]{1,0:T(8,128)(2,1)S(1)}, u32[]{:S(2)}, u32[]{:S(2)}) collective-permute-start(bf16[128,1024]{1,0:T(8,128)(2,1)S(1)} %get-tuple-element.76.refs_6_.refs_4_), channel_id=1, source_target_pairs={{0,4},{1,5},{2,6},{3,7},{4,0},{5,1},{6,2},{7,3},{8,12},{9,13},{10,... | collective-permute-start | bytes 786440 | tf_op jit(solution)/shard_map/ppermute | solution.py:48
  81.2 13.2 %collective-permute-start.26 = (bf16[128,1024]{1,0:T(8,128)(2,1)S(1)}, bf16[128,1024]{1,0:T(8,128)(2,1)S(1)}, u32[]{:S(2)}, u32[]{:S(2)}) collective-permute-start(bf16[128,1024]{1,0:T(8,128)(2,1)S(1)} %get-tuple-element.83.refs_3_.refs_4_), channel_id=1, source_target_pairs={{0,6},{1,7},{2,0},{3,1},{4,2},{5,3},{6,4},{7,5},{8,14},{9,15},{10,... | collective-permute-start | bytes 786440 | tf_op jit(solution)/shard_map/ppermute | solution.py:48
  84.4 10.0 %collective-permute-start.25 = (bf16[128,1024]{1,0:T(8,128)(2,1)S(1)}, bf16[128,1024]{1,0:T(8,128)(2,1)S(1)}, u32[]{:S(2)}, u32[]{:S(2)}) collective-permute-start(bf16[128,1024]{1,0:T(8,128)(2,1)S(1)} %get-tuple-element.83.refs_3_.refs_4_), channel_id=1, source_target_pairs={{0,4},{1,5},{2,6},{3,7},{4,0},{5,1},{6,2},{7,3},{8,12},{9,13},{10,... | collective-permute-start | bytes 786440 | tf_op jit(solution)/shard_map/ppermute | solution.py:48
  84.7 11.7 %collective-permute-start.24 = (bf16[128,1024]{1,0:T(8,128)(2,1)S(1)}, bf16[128,1024]{1,0:T(8,128)(2,1)S(1)}, u32[]{:S(2)}, u32[]{:S(2)}) collective-permute-start(bf16[128,1024]{1,0:T(8,128)(2,1)S(1)} %get-tuple-element.83.refs_3_.refs_4_), channel_id=1, source_target_pairs={{0,2},{1,3},{2,4},{3,5},{4,6},{5,7},{6,0},{7,1},{8,10},{9,11},{10,... | collective-permute-start | bytes 786440 | tf_op jit(solution)/shard_map/ppermute | solution.py:48
  98.3 16.5 %collective-permute-start.30 = (bf16[768,512]{1,0:T(8,128)(2,1)S(1)}, bf16[768,512]{1,0:T(8,128)(2,1)S(1)}, u32[]{:S(2)}, u32[]{:S(2)}) collective-permute-start(bf16[768,512]{1,0:T(8,128)(2,1)S(1)} %grad_far_sent.1.refs_10_), channel_id=1, source_target_pairs={{0,1},{1,0},{2,3},{3,2},{4,5},{5,4},{6,7},{7,6},{8,9},{9,8},{10,11... | collective-permute-start | bytes 2359304 | tf_op jit(solution)/shard_map/ppermute | solution.py:40
  (18 other events, 96.3 us)
